TPU v7x, 128 devices: a whole 4x4x4 slice. The times are simulated.
128 devices in a mesh: dp: 16 (over x, z_hi, core), ctx: 8 (over y, z_lo).
Axes of the slice: x: 4, y: 4, z: 4 (z_hi: 2, z_lo: 2; z = z_hi * 2 + z_lo), core: 2. Of those that a mesh axis runs over, the one named last changes fastest.
Arguments:
- inputs: bfloat16 [16, 2, 8, 128, 2048], P('dp', None, 'ctx'), may hold values from -6 to 6
- norm_gain_vector: float32 [2048], replicated, may hold values from 0.1 to 1.9
- w_qkv: bfloat16 [2048, 3072], replicated, may hold values from -2.6958446 to 2.6958446
- doc_lengths: int32 [16, 16], P('dp'), may hold values from 1 to 1024, 2048 in all within a row
- out_grad: bfloat16 [16, 2, 8, 128, 2048], P('dp', None, 'ctx'), may hold values from -6 to 6
Outputs:
- attended: bfloat16 [16, 2, 8, 128, 2048], P('dp', None, 'ctx')
- inputs_grad: bfloat16 [16, 2, 8, 128, 2048], P('dp', None, 'ctx')
- qkv_grad: float32 [2048, 3072], P(('dp', 'ctx'))
- gain_grad: float32 [2048], P(('dp', 'ctx'))
Inputs may be any that keep to these rules, and one draw needn't show every extreme that they name: `doc_lengths`: each row holds the lengths of the documents of one episode, which sum to 2048.
All inputs are finite; a program needn't handle non-finite values.
Results may differ from a plain program's by a relative error of at most 0.012.
Values may be sent and summed in bfloat16 or wider, within the bound.
No kernel may reach another device: no remote copies, remote signals or barrier semaphores. Data moves between devices by JAX's collectives and lax.ppermute only.
A program may use at most 128 MiB of HBM per device.

v0:
```python
import jax
import jax.numpy as jnp
import numpy as np
from jax import lax
from jax.experimental import pallas as pl
from jax.experimental.pallas import tpu as pltpu
from jax.sharding import Mesh
from jax.sharding import PartitionSpec as P

HEAD = 128
GROUP = 4
D = 2048
BLK = 128
TOK = 256
CHIP = 512
NBLK = 16
WCOLS = 384
CHIPS = 4
PAIR_TOK = 2 * BLK
COLS = 4 * PAIR_TOK
WINDOW = 5
EPS = 1e-05
ROPE_BASE = 500000.0
SCALE = HEAD ** (-0.5)
EXP2_SCALE = SCALE * 1.4426950408889634
F32, BF16 = jnp.float32, jnp.bfloat16
VMEM_LIMIT = 56 * 1024 * 1024

ANGLES = np.arange(2048)[:, None] * ROPE_BASE ** (-2.0 * np.arange(64) / HEAD)
TABLE = np.concatenate([np.cos(ANGLES)] * 2 + [-np.sin(ANGLES), np.sin(ANGLES)], axis=1).astype(np.float32)

SPREAD1 = [(0, 2), (3, 1), (1, 0), (2, 3)]
SPREAD2 = [(1, 2), (2, 1)]
RETURN1 = [(2, 0), (1, 3), (0, 1), (3, 2)]
HOME_TO_VISITOR = [(0, 2), (3, 1)]
VISITOR_ACROSS = [(1, 0), (2, 3)]
PAIR = ("c", "zl")


def cost(us):
    return pl.CostEstimate(flops=int(us * 10**6), bytes_accessed=int(us * (1 << 20)), transcendentals=0)


def params():
    return pltpu.CompilerParams(vmem_limit_bytes=VMEM_LIMIT)


def dot_nt(a, b):
    return lax.dot_general(a, b, (((1,), (1,)), ((), ())), preferred_element_type=F32)


def dot_tn(a, b):
    return lax.dot_general(a, b, (((0,), (0,)), ((), ())), preferred_element_type=F32)


def dot_nn(a, b):
    return lax.dot_general(a, b, (((1,), (0,)), ((), ())), preferred_element_type=F32)


def rotate(v, cos, sin):
    return v * cos + pltpu.roll(v, 64, 1) * sin


def kv_kernel(sel_ref, x_ref, gain_ref, wk_ref, wv_ref, ta_ref, tb_ref, normed_ref, mine_ref, other_ref):
    step = pl.program_id(0)

    @pl.when(step == 0)
    def _():
        x = x_ref[...].astype(F32)
        inv = lax.rsqrt(jnp.mean(x * x, axis=1, keepdims=True) + EPS)
        normed_ref[...] = ((x * inv) * gain_ref[...]).astype(BF16)

    keys = dot_nn(normed_ref[...], wk_ref[...])
    values = dot_nn(normed_ref[...], wv_ref[...]).astype(BF16)
    table = jnp.concatenate([ta_ref[...], tb_ref[...]], axis=0)
    cos, sin = table[:, :HEAD], table[:, HEAD:]
    keys = jnp.concatenate(
        [rotate(keys[:, i * HEAD : (i + 1) * HEAD], cos, sin).astype(BF16) for i in range(2)], axis=1
    )

    @pl.when(step == 0)
    def _():
        mine_ref[:, :256] = keys
        mine_ref[:, 256:] = values

    @pl.when(step == 1)
    def _():
        other_ref[:, :256] = keys
        other_ref[:, 256:] = values


def kv_call(sel, x, gain, w, table):
    half = jax.ShapeDtypeStruct((TOK, 512), BF16)
    return pl.pallas_call(
        kv_kernel,
        grid_spec=pltpu.PrefetchScalarGridSpec(
            num_scalar_prefetch=1,
            grid=(2,),
            in_specs=[
                pl.BlockSpec((TOK, D), lambda t, sel: (0, 0)),
                pl.BlockSpec((1, D), lambda t, sel: (0, 0)),
                pl.BlockSpec((D, 256), lambda t, sel: (0, 8 + (sel[0] + t) % 2)),
                pl.BlockSpec((D, 256), lambda t, sel: (0, 10 + (sel[0] + t) % 2)),
                pl.BlockSpec((BLK, 256), lambda t, sel: (sel[1], 0)),
                pl.BlockSpec((BLK, 256), lambda t, sel: (sel[2], 0)),
            ],
            out_specs=[
                pl.BlockSpec((TOK, D), lambda t, sel: (0, 0)),
                pl.BlockSpec((TOK, 512), lambda t, sel: (0, 0)),
                pl.BlockSpec((TOK, 512), lambda t, sel: (0, 0)),
            ],
        ),
        out_shape=[jax.ShapeDtypeStruct((TOK, D), BF16), half, half],
        compiler_params=params(),
        cost_estimate=cost(0.01),
        name="kv_home",
    )(sel, x, gain, w, w, table, table)


def q_kernel(sel_ref, n_ref, w_ref, ta_ref, tb_ref, q_ref):
    out = dot_nn(n_ref[...], w_ref[...])
    table = jnp.concatenate([ta_ref[...], tb_ref[...]], axis=0)
    for i in range(4):
        cols = slice(i * HEAD, (i + 1) * HEAD)
        q_ref[:, cols] = rotate(out[:, cols], table[:, :HEAD], table[:, HEAD:]).astype(BF16)


def q_call(sel, normed, w, table):
    return pl.pallas_call(
        q_kernel,
        grid_spec=pltpu.PrefetchScalarGridSpec(
            num_scalar_prefetch=1,
            grid=(2,),
            in_specs=[
                pl.BlockSpec((TOK, D), lambda t, sel: (0, 0)),
                pl.BlockSpec((D, 512), lambda t, sel: (0, sel[0] * 2 + t)),
                pl.BlockSpec((BLK, 256), lambda t, sel: (sel[1], 0)),
                pl.BlockSpec((BLK, 256), lambda t, sel: (sel[2], 0)),
            ],
            out_specs=pl.BlockSpec((TOK, 512), lambda t, sel: (0, t)),
        ),
        out_shape=jax.ShapeDtypeStruct((TOK, 1024), BF16),
        compiler_params=params(),
        cost_estimate=cost(4),
        name="q_proj",
    )(sel, normed, w, table, table)


def attention_kernel(
    where_ref, qs_ref, qm_ref, dos_ref, dom_ref, table_ref, start_ref, kv0, kv1, kv2, kv3,
    keep_ref, give_ref, dq_ref, x0, x1, x2, x3, t0, t1, t2, t3, kvbuf, acc, score, quarters,
):
    pieces = (kv0, kv1, kv2, kv3)
    home = where_ref[7] == 0
    for r in range(CHIPS):
        for part in range(2):
            for half in range(2):
                block = where_ref[8 + r * 4 + part * 2 + half]
                kvbuf[block] = pieces[r][part, half * BLK : (half + 1) * BLK, :]
    acc[...] = jnp.zeros_like(acc)
    row = lax.broadcasted_iota(jnp.int32, (PAIR_TOK, COLS), 0)
    for p in range(2):
        rows = slice(p * BLK, (p + 1) * BLK)
        heads = [[slice((h * GROUP + g) * HEAD, (h * GROUP + g + 1) * HEAD) for g in range(GROUP)] for h in range(2)]
        kc = [slice(h * HEAD, (h + 1) * HEAD) for h in range(2)]
        vc = [slice(256 + h * HEAD, 256 + (h + 1) * HEAD) for h in range(2)]
        queries = [jnp.concatenate([ref[rows, g] for ref in (qs_ref, qm_ref) for g in heads[h]], axis=0) for h in range(2)]
        grads = [jnp.concatenate([ref[rows, g] for ref in (dos_ref, dom_ref) for g in heads[h]], axis=0) for h in range(2)]
        first = where_ref[4 + p]
        count = where_ref[p] // 2 - first + 1
        start = jnp.concatenate([start_ref[p]] * GROUP + [start_ref[2 + p]] * GROUP, axis=1)
        token = lax.broadcasted_iota(jnp.int32, (1, GROUP * BLK), 1) % BLK
        pos = jnp.concatenate([where_ref[p] * BLK + token, where_ref[2 + p] * BLK + token], axis=1)

        def pair(i, cols):
            return jnp.concatenate([kvbuf[2 * i, :, cols], kvbuf[2 * i + 1, :, cols]], axis=0)

        def score_step(i, tops, first=first, kc=kc, queries=queries, start=start, pos=pos):
            at = (first + i) * PAIR_TOK + row
            allowed = (at >= start) & (at <= pos)
            out = []
            for h in range(2):
                s = dot_nt(pair(first + i, kc[h]), queries[h])
                s = jnp.where(allowed, s, -jnp.inf)
                score[h, i] = s
                out.append(jnp.maximum(tops[h], jnp.max(s.reshape(PAIR_TOK // 8, 8, COLS), axis=0)))
            return tuple(out)

        tops = lax.fori_loop(0, count, score_step, (jnp.full((8, COLS), -jnp.inf, F32),) * 2)
        tops = [jnp.max(t, axis=0, keepdims=True) * EXP2_SCALE for t in tops]

        def value_step(i, carry, first=first, vc=vc, tops=tops):
            res = []
            for h in range(2):
                total, out = carry[h]
                e = jnp.exp2(score[h, i] * EXP2_SCALE - tops[h])
                score[h, i] = e
                total = total + jnp.sum(e.reshape(PAIR_TOK // 8, 8, COLS), axis=0)
                out = out + dot_tn(pair(first + i, vc[h]), e.astype(BF16))
                res.append((total, out))
            return tuple(res)

        carry = lax.fori_loop(
            0, count, value_step, ((jnp.zeros((8, COLS), F32), jnp.zeros((HEAD, COLS), F32)),) * 2
        )
        invs, deltas = [], []
        for h in range(2):
            total, out = carry[h]
            inv = 1.0 / jnp.sum(total, axis=0, keepdims=True)
            out = (out * inv).astype(BF16).astype(F32)
            deltas.append(jnp.sum(out * grads[h].astype(F32).T, axis=0, keepdims=True))
            invs.append(inv)
            for g in range(GROUP):
                of_s = out[:, g * BLK : (g + 1) * BLK].T.astype(BF16)
                of_m = out[:, (GROUP + g) * BLK : (GROUP + g + 1) * BLK].T.astype(BF16)
                keep_ref[rows, heads[h][g]] = jnp.where(home, of_s, of_m)
                give_ref[rows, heads[h][g]] = jnp.where(home, of_m, of_s)

        def grad_step(i, dqs, first=first, kc=kc, vc=vc, invs=invs, deltas=deltas, queries=queries, grads=grads):
            res = []
            j = first + i
            for h in range(2):
                keys, values = pair(j, kc[h]), pair(j, vc[h])
                prob = score[h, i] * invs[h]
                dp = dot_nt(values, grads[h])
                ds = (prob * (dp - deltas[h])).astype(BF16)
                dv = dot_nn(prob.astype(BF16), grads[h])
                dk = dot_nn(ds, queries[h])
                for k in range(2):
                    acc[2 * j + k, :, vc[h]] += dv[k * BLK : (k + 1) * BLK]
                    acc[2 * j + k, :, kc[h]] += dk[k * BLK : (k + 1) * BLK]
                res.append(dqs[h] + dot_tn(keys, ds))
            return tuple(res)

        dqs = lax.fori_loop(0, count, grad_step, (jnp.zeros((HEAD, COLS), F32),) * 2)
        for k in range(2):
            at = (2 * k + p) * BLK
            rows = slice(at, at + BLK)
            cos, sin = table_ref[rows, :HEAD] * SCALE, table_ref[rows, HEAD:] * SCALE
            for h in range(2):
                for g in range(GROUP):
                    at = (k * GROUP + g) * BLK
                    part = rotate(dqs[h][:, at : at + BLK].T, cos, -sin).astype(BF16)
                    dq_ref[rows, heads[h][g]] = part
                    j = h * GROUP + g
                    quarters[j // 2, rows, (j % 2) * HEAD : (j % 2 + 1) * HEAD] = part
    for r, out in enumerate((x0, x1, x2, x3)):
        out[...] = quarters[(where_ref[6] + r) % 4]
    for r, out in enumerate((t0, t1, t2, t3)):
        for j in range(4):
            at, rows = where_ref[8 + r * 4 + j], slice(j * BLK, (j + 1) * BLK)
            out[rows, :256] = (acc[at, :, :256] * SCALE).astype(BF16)
            out[rows, 256:] = acc[at, :, 256:].astype(BF16)


def attention_call(where, q, do, table, start, pieces):
    vmem = pl.BlockSpec(memory_space=pltpu.VMEM)
    half = jax.ShapeDtypeStruct((TOK, 1024), BF16)
    out = pl.pallas_call(
        attention_kernel,
        in_specs=[pl.BlockSpec(memory_space=pltpu.SMEM)] + [vmem] * 10,
        out_specs=[vmem] * 11,
        out_shape=[half, half, jax.ShapeDtypeStruct((CHIP, 1024), BF16)]
        + [jax.ShapeDtypeStruct((CHIP, 256), BF16)] * 4
        + [jax.ShapeDtypeStruct((CHIP, 512), BF16)] * 4,
        scratch_shapes=[
            pltpu.VMEM((NBLK, BLK, 512), BF16),
            pltpu.VMEM((NBLK, BLK, 512), F32),
            pltpu.VMEM((2, WINDOW, PAIR_TOK, COLS), F32),
            pltpu.VMEM((4, CHIP, 256), BF16),
        ],
        compiler_params=params(),
        cost_estimate=cost(0.1),
        name="attention",
    )(where, *q, *do, table, start, *pieces)
    return out[0], out[1], out[2], out[3:7], out[7:]


def joined_kernel(x_ref, a, b, c, d, table_ref, out_ref, j0, j1, j2, j3):
    total = a[...].astype(F32) + b[...].astype(F32) + c[...].astype(F32) + d[...].astype(F32)
    for i in range(2):
        cols = slice(i * HEAD, (i + 1) * HEAD)
        out_ref[:, cols] = rotate(total[:, cols], table_ref[:, :HEAD], -table_ref[:, HEAD:]).astype(BF16)
    out_ref[:, 256:] = total[:, 256:].astype(BF16)
    for r, out in enumerate((j0, j1, j2, j3)):
        out[...] = out_ref[:, pl.ds(pl.multiple_of((x_ref[0] + r) % 4 * HEAD, HEAD), HEAD)]


def joined_call(x_at, own, others, table):
    vmem = pl.BlockSpec(memory_space=pltpu.VMEM)
    out = pl.pallas_call(
        joined_kernel,
        in_specs=[pl.BlockSpec(memory_space=pltpu.SMEM)] + [vmem] * 5,
        out_specs=[vmem] * 5,
        out_shape=[jax.ShapeDtypeStruct((CHIP, 512), BF16)] + [jax.ShapeDtypeStruct((CHIP, HEAD), BF16)] * 4,
        compiler_params=params(),
        cost_estimate=cost(0.1),
        name="joined_kv",
    )(x_at, own, *others, table)
    return out[0], out[1:]


def dnorm_q_kernel(sel_ref, j_ref, w_ref, out_ref):
    out_ref[...] = dot_nt(j_ref[...], w_ref[...]).astype(BF16)


def dnorm_q_call(sel, jq, w):
    tile = 512
    return pl.pallas_call(
        dnorm_q_kernel,
        grid_spec=pltpu.PrefetchScalarGridSpec(
            num_scalar_prefetch=1,
            grid=(D // tile,),
            in_specs=[
                pl.BlockSpec((CHIP, 1024), lambda t, sel: (0, 0)),
                pl.BlockSpec((tile, 1024), lambda t, sel: (t, sel[0])),
            ],
            out_specs=pl.BlockSpec((CHIP, tile), lambda t, sel: (0, t)),
        ),
        out_shape=jax.ShapeDtypeStruct((CHIP, D), BF16),
        compiler_params=params(),
        cost_estimate=cost(6),
        name="d_normed_q",
    )(sel, jq, w)


def dnorm_kernel(sel_ref, part_ref, jkv_ref, wk_ref, wv_ref, keep_ref, give_ref):
    out = part_ref[...].astype(F32)
    out += dot_nt(jkv_ref[:, :256], wk_ref[...])
    out += dot_nt(jkv_ref[:, 256:], wv_ref[...])
    home = sel_ref[1] == 0
    of_s, of_m = out[:TOK].astype(BF16), out[TOK:].astype(BF16)
    keep_ref[...] = jnp.where(home, of_s, of_m)
    give_ref[...] = jnp.where(home, of_m, of_s)


def dnorm_call(sel, part, jkv, w):
    tile = 1024
    return pl.pallas_call(
        dnorm_kernel,
        grid_spec=pltpu.PrefetchScalarGridSpec(
            num_scalar_prefetch=1,
            grid=(D // tile,),
            in_specs=[
                pl.BlockSpec((CHIP, tile), lambda t, sel: (0, t)),
                pl.BlockSpec((CHIP, 512), lambda t, sel: (0, 0)),
                pl.BlockSpec((tile, 256), lambda t, sel: (t, 8 + sel[0])),
                pl.BlockSpec((tile, 256), lambda t, sel: (t, 10 + sel[0])),
            ],
            out_specs=[pl.BlockSpec((TOK, tile), lambda t, sel: (0, t))] * 2,
        ),
        out_shape=[jax.ShapeDtypeStruct((TOK, D), BF16)] * 2,
        compiler_params=params(),
        cost_estimate=cost(3),
        name="d_normed",
    )(sel, part, jkv, w, w)


def weight_kernel(sel_ref, ns, nm, d1, d2, d3, v1, v2, v3, q0, q1, q2, q3, k0, k1, k2, k3, out_ref, jt):
    role = sel_ref[1]
    pieces = ((ns, q0, k0, 0), (nm, q0, k0, TOK))
    for direct, via, q, k in ((d1, v1, q1, k1), (d2, v2, q2, k2), (d3, v3, q3, k3)):
        pieces += ((direct, q, k, role * TOK), (via, q, k, (1 - role) * TOK))

    @pl.when(pl.program_id(0) == 0)
    def _():
        for i, (_, q, k, at) in enumerate(pieces):
            jt[:256, i * TOK : (i + 1) * TOK] = q[pl.ds(at, TOK), :].T
            jt[256:, i * TOK : (i + 1) * TOK] = k[pl.ds(at, TOK), :].T

    out = jnp.zeros((WCOLS, out_ref.shape[0] * TOK), F32)
    for i, (n, _, _, _) in enumerate(pieces):
        out += dot_nn(jt[:, i * TOK : (i + 1) * TOK], n[...])
    for t in range(out_ref.shape[0]):
        part = out[:, t * TOK : (t + 1) * TOK].T.astype(BF16)
        for i in range(2):
            for k in range(8):
                at = i * 128 + k * 16
                out_ref[t, k, i] = part[at : at + 16]


def weight_call(sel, tokens, direct, via, jq, jkv):
    tile = 512
    part = pl.BlockSpec((TOK, tile), lambda t, sel: (0, t))
    return pl.pallas_call(
        weight_kernel,
        grid_spec=pltpu.PrefetchScalarGridSpec(
            num_scalar_prefetch=1,
            grid=(D // tile,),
            in_specs=[part] * 8
            + [pl.BlockSpec((CHIP, 256), lambda t, sel: (0, 0))] * 4
            + [pl.BlockSpec((CHIP, HEAD), lambda t, sel: (0, 0))] * 4,
            out_specs=pl.BlockSpec((tile // TOK, 8, 2, 16, WCOLS), lambda t, sel: (t, 0, 0, 0, 0)),
            scratch_shapes=[pltpu.VMEM((WCOLS, 8 * TOK), BF16)],
        ),
        out_shape=jax.ShapeDtypeStruct((8, 8, 2, 16, WCOLS), BF16),
        compiler_params=params(),
        cost_estimate=cost(0.1),
        name="weight_grad",
    )(sel, *tokens, *direct, *via, *jq, *jkv)


def sum_kernel(sel_ref, parts_ref, keep_ref, give_ref):
    core = sel_ref[0]
    for x in range(4):
        keep_ref[x] = jnp.sum(parts_ref[x * 16 : (x + 1) * 16, core].astype(F32), axis=0)
        give_ref[x] = jnp.sum(parts_ref[x * 16 : (x + 1) * 16, 1 - core].astype(F32), axis=0)


def sum_call(sel, parts):
    vmem = pl.BlockSpec(memory_space=pltpu.VMEM)
    out = jax.ShapeDtypeStruct((4, 16, WCOLS), F32)
    return pl.pallas_call(
        sum_kernel,
        in_specs=[pl.BlockSpec(memory_space=pltpu.SMEM), vmem],
        out_specs=[vmem] * 2,
        out_shape=[out, out],
        compiler_params=params(),
        cost_estimate=cost(0.1),
        name="weight_sum",
    )(sel, parts)


def finish_kernel(sel_ref, own, got, w_ref, gain_ref, grad_ref, gain_grad_ref):
    first = sel_ref[0] == 0
    for core in range(2):
        for x in range(4):
            value = jnp.where(first == (core == 0), own[x], got[x])
            at = core * 1024 + x * 256
            grad_ref[:, at : at + 256] = value[:, :256]
            at = 2048 + (x // 2) * 512 + core * 256 + (x % 2) * HEAD
            grad_ref[:, at : at + HEAD] = value[:, 256:]
    total = jnp.sum(w_ref[...].astype(F32) * grad_ref[...], axis=1, keepdims=True)
    gain_grad_ref[...] = jnp.broadcast_to(total, (16, HEAD)).T[:1] / gain_ref[...]


def finish_call(sel, own, got, w_rows, gain_rows):
    vmem = pl.BlockSpec(memory_space=pltpu.VMEM)
    return pl.pallas_call(
        finish_kernel,
        in_specs=[pl.BlockSpec(memory_space=pltpu.SMEM)] + [vmem] * 4,
        out_specs=[vmem] * 2,
        out_shape=[jax.ShapeDtypeStruct((16, 3072), F32), jax.ShapeDtypeStruct((1, 16), F32)],
        compiler_params=params(),
        cost_estimate=cost(0.1),
        name="finish",
    )(sel, own, got, w_rows, gain_rows)


def inputs_kernel(sel_ref, x_ref, gain_ref, keep_ref, near_ref, far_ref, out_ref):
    x = x_ref[...].astype(F32)
    inv = lax.rsqrt(jnp.mean(x * x, axis=1, keepdims=True) + EPS)
    unit = x * inv
    here = keep_ref[...].astype(F32) + near_ref[...].astype(F32)
    d_normed = jnp.where(sel_ref[1] == 0, here, far_ref[...].astype(F32))
    scaled = d_normed * gain_ref[...]
    mean = jnp.mean(scaled * unit, axis=1, keepdims=True)
    out_ref[...] = (inv * (scaled - unit * mean)).astype(BF16)


def inputs_call(sel, x, gain, keep, near, far):
    tile = 128
    rows = pl.BlockSpec((tile, D), lambda t, sel: (t, 0))
    return pl.pallas_call(
        inputs_kernel,
        grid_spec=pltpu.PrefetchScalarGridSpec(
            num_scalar_prefetch=1,
            grid=(TOK // tile,),
            in_specs=[rows, pl.BlockSpec((1, D), lambda t, sel: (0, 0)), rows, rows, rows],
            out_specs=rows,
        ),
        out_shape=jax.ShapeDtypeStruct((TOK, D), BF16),
        compiler_params=params(),
        cost_estimate=cost(0.1),
        name="inputs_grad",
    )(sel, x, gain, keep, near, far)


def shift(value, axis, by):
    return lax.ppermute(value, axis, [(i, (i + by) % 4) for i in range(4)])


def swap_cores(value):
    return lax.ppermute(value, "c", [(0, 1), (1, 0)])


def after(value, *others):
    return lax.optimization_barrier((value,) + others)[0]


def body(inputs, gain, w, doc_lengths, out_grad):
    c, zl, y, x_at, zh = (lax.axis_index(a).astype(jnp.int32) for a in ("c", "zl", "y", "x", "zh"))
    resident = c == zl
    role = jnp.where(resident, 0, 1).astype(jnp.int32)
    sel = jnp.stack([c, role])
    x = inputs.reshape(TOK, D)
    grads = out_grad.reshape(TOK, 2048)
    gain2 = gain.reshape(1, D)
    near, far = 2 * y + zl, 2 * y + 1 - zl
    table = jnp.asarray(TABLE)

    g_mine = lax.dynamic_slice_in_dim(grads, zl * 1024, 1024, 1)
    g_other = lax.dynamic_slice_in_dim(grads, (1 - zl) * 1024, 1024, 1)
    g1 = lax.ppermute(g_other, PAIR, SPREAD1)
    g2 = lax.ppermute(g_mine, PAIR, SPREAD2)
    lengths = doc_lengths.reshape(16)

    normed, kv_mine, kv_other = kv_call(jnp.stack([zl, near, 15 - near]), x, gain2, w, table)

    r1 = lax.ppermute(kv_other, PAIR, SPREAD1)
    r2 = lax.ppermute(kv_mine, PAIR, SPREAD2)
    kv = jnp.stack([jnp.where(resident, kv_mine, r1), jnp.where(resident, r1, r2)])
    kv, g1, g2 = lax.optimization_barrier((kv, g1, g2))
    kv_from = {(4 - by) % 4: shift(kv, "y", by) for by in (2, 1, 3)}

    n1 = lax.ppermute(after(normed, r1, r2), PAIR, HOME_TO_VISITOR)
    sent = after(normed, r1, r2)
    n2 = lax.ppermute(sent, PAIR, SPREAD2)
    n3 = lax.ppermute(sent, PAIR, VISITOR_ACROSS)
    n_s, n_m = jnp.where(resident, normed, n1), jnp.where(resident, n3, n2)

    q = (
        q_call(jnp.stack([c, near, 15 - near]), n_s, w, table),
        q_call(jnp.stack([c, far, 15 - far]), n_m, w, table),
    )

    mine = after(jnp.where(resident, normed, n2), kv_from[1], kv_from[2], kv_from[3], *q)
    direct = {(4 - by) % 4: shift(mine, "x", by) for by in (2, 1, 3)}
    direct = [direct[r] for r in (1, 2, 3)]

    do = (jnp.where(resident, g_mine, g1), jnp.where(resident, g1, g2))

    lengths_near = lax.ppermute(after(lengths, n2), PAIR, HOME_TO_VISITOR)
    lengths = jnp.where(resident, lengths, lengths_near)
    upto = jnp.arange(16)
    ends = jnp.sum(jnp.where(upto[None, :] <= upto[:, None], lengths[None, :], 0), axis=1)
    blocks = []
    for r in range(CHIPS):
        a, b = 2 * ((y + r) % 4) + zl, 2 * ((y + r) % 4) + 1 - zl
        blocks += [a, 15 - a, b, 15 - b]
    own = jnp.stack(blocks[:4])
    positions = (own[:, None] * BLK + jnp.arange(BLK, dtype=jnp.int32)[None, :]).reshape(CHIP)
    start = jnp.max(jnp.where(positions[:, None] >= ends[None, :], ends[None, :], 0), axis=1).astype(jnp.int32)
    start = start.reshape(4, 1, BLK)
    lowest = start[:, 0, 0] // PAIR_TOK
    where = jnp.stack(
        blocks[:4]
        + [jnp.minimum(lowest[0], lowest[2]), jnp.minimum(lowest[1], lowest[3]), x_at, role]
        + blocks
    ).astype(jnp.int32)
    own_table = jnp.concatenate([lax.dynamic_slice_in_dim(table, b * BLK, BLK, 0) for b in blocks[:4]], axis=0)

    o_keep, o_give, dq, dq_to, dkv_to = attention_call(
        where, q, do, own_table, start, [kv, kv_from[1], kv_from[2], kv_from[3]]
    )

    others = [shift(dkv_to[by], "y", by) for by in (2, 1, 3)]
    jq = {(4 - by) % 4: shift(after(dq_to[by], *direct), "x", by) for by in (2, 1, 3)}
    jq = [dq_to[0], jq[1], jq[2], jq[3]]
    dn_q = dnorm_q_call(sel, dq, w)
    via = [swap_cores(after(piece, dn_q, *others, *jq[1:])) for piece in direct]
    joined_kv, jkv_to = joined_call(x_at.reshape(1), after(dkv_to[0], dn_q), others, own_table)
    jkv = {(4 - by) % 4: shift(after(jkv_to[by], *via), "x", by) for by in (2, 1, 3)}
    jkv = [jkv_to[0], jkv[1], jkv[2], jkv[3]]

    parts = weight_call(sel, (n_s, n_m), direct, via, jq, jkv)
    dn_keep, dn_give = dnorm_call(sel, after(dn_q, parts), joined_kv, w)
    parts = lax.all_to_all(parts.reshape(64, 2, 16, WCOLS), ("x", "zh", "y", "zl"), 0, 0, tiled=True)

    d1 = swap_cores(dn_give)
    summed = (dn_keep.astype(F32) + d1.astype(F32)).astype(BF16)
    d2 = lax.ppermute(summed, PAIR, SPREAD2)
    inputs_grad = inputs_call(sel, x, gain2, dn_keep, d1, d2)

    h1 = lax.ppermute(o_give, PAIR, RETURN1)
    h2 = lax.ppermute(o_keep, PAIR, SPREAD2)
    half_mine = jnp.where(resident, o_keep, h2)
    attended = jnp.concatenate(
        [jnp.where(zl == 0, half_mine, h1), jnp.where(zl == 0, h1, half_mine)], axis=1
    )

    keep, give = sum_call(sel, parts)
    got = swap_cores(give)
    at = ((((x_at * 2 + zh) * 2 + c) * 4 + y) * 2 + zl) * 16
    w_rows = lax.dynamic_slice_in_dim(w, at, 16, 0)
    gain_rows = lax.dynamic_slice_in_dim(gain2, at, 16, 1)
    qkv_grad, gain_grad = finish_call(sel, keep, got, w_rows, gain_rows)
    return (
        attended.reshape(1, 2, 1, BLK, 2048),
        inputs_grad.reshape(1, 2, 1, BLK, D),
        qkv_grad,
        gain_grad.reshape(16),
    )


def solution(mesh):
    fine = Mesh(mesh.devices.reshape(4, 2, 2, 4, 2), ("x", "zh", "c", "y", "zl"))
    dp, ctx = ("x", "zh", "c"), ("y", "zl")
    rows = P(dp, None, ctx, None, None)
    return jax.shard_map(
        body,
        mesh=fine,
        in_specs=(rows, P(), P(), P(dp, None), rows),
        out_specs=(rows, rows, P(dp + ctx, None), P(dp + ctx)),
        check_vma=False,
    )
```

profile of v0, /device:TPU:1, one launch (start us, length us, event | category | flops | bytes accessed | tf_op | source)
XLA Modules:
  0.0 223.1 jit_solution(6220784374131472996)
XLA Ops:
  1.2 6.0 %kv_home.1 = (bf16[256,2048]{1,0:T(8,128)(2,1)}, bf16[256,512]{1,0:T(8,128)(2,1)}, bf16[256,512]{1,0:T(8,128)(2,1)}) custom-call(s32[3]{0:T(128)} %add_add_fusion.sel_ref, bf16[256,2048]{1,0:T(8,128)(2,1)} %bitcast.46, f32[1,2048]{1,0:T(1,128)} %bitcast.51, bf16[2048,3072]{1,0:T(8,128)(2,1)} %wv_ref.3, bf16[2048,3072]{1,0:T(8,128)(2,1)} %wv_ref.3, ...), custom_call_target="tpu_custom_call" | custom-call | flops 10000 | bytes 10485 | tf_op jit(solution)/shard_map/kv_home/pallas_call | solution.py:94
  7.2 5.1 %collective-permute-start.1 = (bf16[256,512]{1,0:T(8,128)(2,1)}, bf16[256,512]{1,0:T(8,128)(2,1)S(1)}, u32[]{:S(2)}, u32[]{:S(2)}) collective-permute-start(bf16[256,512]{1,0:T(8,128)(2,1)} %get-tuple-element.48), channel_id=1, source_target_pairs={{1,8},{8,1},{3,10},{10,3},{5,12},{12,5},{7,14},{14,7},{17,24},{24,... | collective-permute-start | bytes 786440 | tf_op jit(solution)/shard_map/ppermute | solution.py:511
  22.5 5.8 %collective-permute-start.5 = (bf16[256,2048]{1,0:T(8,128)(2,1)S(1)}, bf16[256,2048]{1,0:T(8,128)(2,1)}, u32[]{:S(2)}, u32[]{:S(2)}) collective-permute-start(bf16[256,2048]{1,0:T(8,128)(2,1)S(1)} %copy-done.10), channel_id=1, source_target_pairs={{1,0},{8,9},{3,2},{10,11},{5,4},{12,13},{7,6},{14,15},{17,16},{24,... | collective-permute-start | bytes 3145736 | tf_op jit(solution)/shard_map/ppermute | solution.py:519
  37.3 4.8 %collective-permute-done.2 = bf16[256,2048]{1,0:T(8,128)(2,1)S(1)} collective-permute-done((bf16[256,2048]{1,0:T(8,128)(2,1)S(1)}, bf16[256,2048]{1,0:T(8,128)(2,1)S(1)}, u32[]{:S(2)}, u32[]{:S(2)}) %collective-permute-start.2) | collective-permute-done | bytes 1048608 | tf_op jit(solution)/shard_map/ppermute | solution.py:518
  42.1 2.9 %collective-permute-start.9 = (bf16[2,256,512]{2,1,0:T(8,128)(2,1)S(1)}, bf16[2,256,512]{2,1,0:T(8,128)(2,1)S(1)}, u32[]{:S(2)}, u32[]{:S(2)}) collective-permute-start(bf16[2,256,512]{2,1,0:T(8,128)(2,1)S(1)} %pad_maximum_fusion.1.kv0), channel_id=1, source_target_pairs={{0,4},{2,6},{4,0},{6,2},{1,5},{3,7},{5,1},{7,3},{8,12},{10,14},{12... | collective-permute-start | bytes 1572872 | tf_op jit(solution)/shard_map/ppermute | solution.py:480
  45.0 7.3 %collective-permute-done.5 = bf16[256,2048]{1,0:T(8,128)(2,1)} collective-permute-done((bf16[256,2048]{1,0:T(8,128)(2,1)S(1)}, bf16[256,2048]{1,0:T(8,128)(2,1)}, u32[]{:S(2)}, u32[]{:S(2)}) %collective-permute-start.5) | collective-permute-done | bytes 1048608 | tf_op jit(solution)/shard_map/ppermute | solution.py:519
  52.3 3.0 %broadcast_select_fusion = (bf16[256,2048]{1,0:T(8,128)(2,1)}, bf16[256,2048]{1,0:T(8,128)(2,1)}, bf16[256,2048]{1,0:T(8,128)(2,1)}) fusion(bf16[256,2048]{1,0:T(8,128)(2,1)S(1)} %copy-done.10, bf16[256,2048]{1,0:T(8,128)(2,1)S(1)} %collective-permute-done.2, pred[]{:T(512)S(6)} %eq.17, bf16[256,2048]{1,0:T(8,128)(2,1)} %collective-permute-done.5, ...), kind=kLoop, calls=%fused_computation.2 | loop fusion | flops 1572864 | bytes 7340033 | tf_op jit(solution)/shard_map/jit(_where)/select_n | solution.py:527
  55.3 5.1 %q_proj.3.qm_ref = bf16[256,1024]{1,0:T(8,128)(2,1)} custom-call(s32[3]{0:T(128)} %get-tuple-element.120.sel_ref, bf16[256,2048]{1,0:T(8,128)(2,1)} %get-tuple-element.107.n_ref.nm, bf16[2048,3072]{1,0:T(8,128)(2,1)} %wv_ref.3, f32[2048,256]{1,0:T(8,128)} %constant.87.clone.ta_ref.tb_ref, f32[2048,256]{1,0:T(8,128)} %constant.87.clone.ta_ref.tb_ref), custom_call_target="tpu_custom_call" | custom-call | flops 4000000 | bytes 4194304 | tf_op jit(solution)/shard_map/q_proj/pallas_call | solution.py:129
  60.4 5.2 %q_proj.2.qs_ref = bf16[256,1024]{1,0:T(8,128)(2,1)} custom-call(s32[3]{0:T(128)} %get-tuple-element.119.sel_ref, bf16[256,2048]{1,0:T(8,128)(2,1)} %get-tuple-element.108.n_ref.ns, bf16[2048,3072]{1,0:T(8,128)(2,1)} %wv_ref.3, f32[2048,256]{1,0:T(8,128)} %constant.87.clone.ta_ref.tb_ref, f32[2048,256]{1,0:T(8,128)} %constant.87.clone.ta_ref.tb_ref), custom_call_target="tpu_custom_call" | custom-call | flops 4000000 | bytes 4194304 | tf_op jit(solution)/shard_map/q_proj/pallas_call | solution.py:129
  77.7 16.4 %attention.1 = (bf16[256,1024]{1,0:T(8,128)(2,1)}, bf16[256,1024]{1,0:T(8,128)(2,1)}, bf16[512,1024]{1,0:T(8,128)(2,1)}, bf16[512,256]{1,0:T(8,128)(2,1)}, bf16[...) custom-call(s32[24]{0:T(128)} %stack.137.where_ref, ...), custom_call_target="tpu_custom_call" | custom-call | flops 100000 | bytes 104857 | tf_op jit(solution)/shard_map/attention/pallas_call | solution.py:259
  94.2 10.7 %collective-permute-start.16 = (bf16[512,512]{1,0:T(8,128)(2,1)}, bf16[512,512]{1,0:T(8,128)(2,1)S(1)}, u32[]{:S(2)}, u32[]{:S(2)}) collective-permute-start(bf16[512,512]{1,0:T(8,128)(2,1)} %get-tuple-element.58), channel_id=1, source_target_pairs={{0,4},{2,6},{4,0},{6,2},{1,5},{3,7},{5,1},{7,3},{8,12},{10,14},{12... | collective-permute-start | bytes 1572872 | tf_op jit(solution)/shard_map/ppermute | solution.py:480
  108.3 9.9 %collective-permute-done.15.d3 = bf16[256,2048]{1,0:T(8,128)(2,1)S(1)} collective-permute-done((bf16[256,2048]{1,0:T(8,128)(2,1)}, bf16[256,2048]{1,0:T(8,128)(2,1)S(1)}, u32[]{:S(2)}, u32[]{:S(2)}) %collective-permute-start.15) | collective-permute-done | bytes 1048608 | tf_op jit(solution)/shard_map/ppermute | solution.py:480
  121.5 6.8 %d_normed_q.1.part_ref = bf16[512,2048]{1,0:T(8,128)(2,1)} custom-call(s32[2]{0:T(128)} %pad_add_fusion.1.sel_ref, bf16[512,1024]{1,0:T(8,128)(2,1)} %get-tuple-element.56.j_ref, bf16[2048,3072]{1,0:T(8,128)(2,1)} %wv_ref.3), custom_call_target="tpu_custom_call" | custom-call | flops 6000000 | bytes 6291456 | tf_op jit(solution)/shard_map/d_normed_q/pallas_call | solution.py:309
  129.3 3.5 %collective-permute-done.21.q3 = bf16[512,256]{1,0:T(8,128)(2,1)S(1)} collective-permute-done((bf16[512,256]{1,0:T(8,128)(2,1)}, bf16[512,256]{1,0:T(8,128)(2,1)S(1)}, u32[]{:S(2)}, u32[]{:S(2)}) %collective-permute-start.21) | collective-permute-done | bytes 262176 | tf_op jit(solution)/shard_map/ppermute | solution.py:480
  135.1 3.1 %joined_kv.1 = (bf16[512,512]{1,0:T(8,128)(2,1)}, bf16[512,128]{1,0:T(8,128)(2,1)}, bf16[512,128]{1,0:T(8,128)(2,1)}, bf16[512,128]{1,0:T(8,128)(2,1)}, bf16[512,128]{1,0:T(8,128)(2,1)}) custom-call(s32[1]{0:T(128)} %bitcast.12.x_ref, bf16[512,512]{1,0:T(8,128)(2,1)} %get-tuple-element.72.a, bf16[512,512]{1,0:T(8,128)(2,1)} %copy-done.15, ...), custom_call_target="tpu_custom_call" | custom-call | flops 100000 | bytes 104857 | tf_op jit(solution)/shard_map/joined_kv/pallas_call | solution.py:291
  139.9 3.3 %collective-permute-start.26 = (bf16[512,128]{1,0:T(8,128)(2,1)}, bf16[512,128]{1,0:T(8,128)(2,1)S(1)}, u32[]{:S(2)}, u32[]{:S(2)}) collective-permute-start(bf16[512,128]{1,0:T(8,128)(2,1)} %get-tuple-element.77), channel_id=1, source_target_pairs={{0,64},{32,96},{64,0},{96,32},{1,65},{33,97},{65,1},{97,33},{2,66}... | collective-permute-start | bytes 393224 | tf_op jit(solution)/shard_map/ppermute | solution.py:480
  143.2 2.8 %collective-permute-done.27.k3 = bf16[512,128]{1,0:T(8,128)(2,1)S(1)} collective-permute-done((bf16[512,128]{1,0:T(8,128)(2,1)}, bf16[512,128]{1,0:T(8,128)(2,1)S(1)}, u32[]{:S(2)}, u32[]{:S(2)}) %collective-permute-start.27) | collective-permute-done | bytes 131104 | tf_op jit(solution)/shard_map/ppermute | solution.py:480
  146.0 3.4 %collective-permute-done.26.k2 = bf16[512,128]{1,0:T(8,128)(2,1)S(1)} collective-permute-done((bf16[512,128]{1,0:T(8,128)(2,1)}, bf16[512,128]{1,0:T(8,128)(2,1)S(1)}, u32[]{:S(2)}, u32[]{:S(2)}) %collective-permute-start.26) | collective-permute-done | bytes 131104 | tf_op jit(solution)/shard_map/ppermute | solution.py:480
  150.2 9.3 %weight_grad.1 = bf16[8,8,2,16,384]{4,3,2,1,0:T(8,128)(2,1)} custom-call(s32[2]{0:T(128)} %pad_add_fusion.1.sel_ref, bf16[256,2048]{1,0:T(8,128)(2,1)} %get-tuple-element.108.n_ref.ns, bf16[256,2048]{1,0:T(8,128)(2,1)} %get-tuple-element.107.n_ref.nm, bf16[256,2048]{1,0:T(8,128)(2,1)} %copy-done.3, bf16[256,2048]{1,0:T(8,128)(2,1)} %copy-done.4, ...), custom_call_target="tpu_custom_call" | custom-call | flops 100000 | bytes 104857 | tf_op jit(solution)/shard_map/weight_grad/pallas_call | solution.py:385
  159.4 5.1 %d_normed.1 = (bf16[256,2048]{1,0:T(8,128)(2,1)}, bf16[256,2048]{1,0:T(8,128)(2,1)}) custom-call(s32[2]{0:T(128)} %pad_add_fusion.1.sel_ref, bf16[512,2048]{1,0:T(8,128)(2,1)} %d_normed_q.1.part_ref, bf16[512,512]{1,0:T(8,128)(2,1)} %get-tuple-element.81.jkv_ref, bf16[2048,3072]{1,0:T(8,128)(2,1)} %wv_ref.3, bf16[2048,3072]{1,0:T(8,128)(2,1)} %wv_ref.3), custom_call_target="tpu_custom_call" | custom-call | flops 3000000 | bytes 3145728 | tf_op jit(solution)/shard_map/d_normed/pallas_call | solution.py:339
  165.8 10.8 %all-to-all-start = ((bf16[64,2,16,384]{3,2,1,0:T(8,128)(2,1)}), bf16[64,2,16,384]{3,2,1,0:T(8,128)(2,1)S(1)}, u32[]{:S(2)}, u32[]{:S(2)}) async-start(bf16[64,2,16,384]{3,2,1,0:T(8,128)(2,1)} %bitcast.36), calls=%async_computation | async-start | bytes 3145728 | tf_op jit(solution)/shard_map/all_to_all | solution.py:568
  176.6 3.5 %collective-permute-start.11 = (bf16[256,1024]{1,0:T(8,128)(2,1)S(1)}, bf16[256,1024]{1,0:T(8,128)(2,1)}, u32[]{:S(2)}, u32[]{:S(2)}) collective-permute-start(bf16[256,1024]{1,0:T(8,128)(2,1)S(1)} %copy-done.11), channel_id=1, source_target_pairs={{1,8},{8,1},{3,10},{10,3},{5,12},{12,5},{7,14},{14,7},{17,24},{24,... | collective-permute-start | bytes 1572872 | tf_op jit(solution)/shard_map/ppermute | solution.py:576
  187.7 19.5 %collective-permute-done.11 = bf16[256,1024]{1,0:T(8,128)(2,1)} collective-permute-done((bf16[256,1024]{1,0:T(8,128)(2,1)S(1)}, bf16[256,1024]{1,0:T(8,128)(2,1)}, u32[]{:S(2)}, u32[]{:S(2)}) %collective-permute-start.11) | collective-permute-done | bytes 524320 | tf_op jit(solution)/shard_map/ppermute | solution.py:576
  218.6 4.5 %inputs_grad.1 = bf16[256,2048]{1,0:T(8,128)(2,1)} custom-call(s32[2]{0:T(128)} %pad_add_fusion.1.sel_ref, bf16[256,2048]{1,0:T(8,128)(2,1)} %bitcast.47, f32[1,2048]{1,0:T(1,128)} %bitcast.52, bf16[256,2048]{1,0:T(8,128)(2,1)} %get-tuple-element.82.keep_ref, bf16[256,2048]{1,0:T(8,128)(2,1)} %collective-permute-done.28.near_ref, ...), custom_call_target="tpu_custom_call" | custom-call | flops 100000 | bytes 104857 | tf_op jit(solution)/shard_map/inputs_grad/pallas_call | solution.py:464
  (135 shorter events, 61.7 us)
Async XLA Ops:
  7.2 9.3 %collective-permute-start.1 = (bf16[256,512]{1,0:T(8,128)(2,1)}, bf16[256,512]{1,0:T(8,128)(2,1)S(1)}, u32[]{:S(2)}, u32[]{:S(2)}) collective-permute-start(bf16[256,512]{1,0:T(8,128)(2,1)} %get-tuple-element.48), channel_id=1, source_target_pairs={{1,8},{8,1},{3,10},{10,3},{5,12},{12,5},{7,14},{14,7},{17,24},{24,... | collective-permute-start | bytes 786440 | tf_op jit(solution)/shard_map/ppermute | solution.py:511
  13.3 18.8 %collective-permute-start.7 = (bf16[256,1024]{1,0:T(8,128)(2,1)S(1)}, bf16[256,1024]{1,0:T(8,128)(2,1)}, u32[]{:S(2)}, u32[]{:S(2)}) collective-permute-start(bf16[256,1024]{1,0:T(8,128)(2,1)S(1)} %get-tuple-element.110), channel_id=1, source_target_pairs={{1,8},{8,1},{3,10},{10,3},{5,12},{12,5},{7,14},{14,7},{17,24},{24,... | collective-permute-start | bytes 1572872 | tf_op jit(solution)/shard_map/ppermute | solution.py:505
  15.2 16.9 %collective-permute-start.6 = (bf16[256,1024]{1,0:T(8,128)(2,1)}, bf16[256,1024]{1,0:T(8,128)(2,1)}, u32[]{:S(2)}, u32[]{:S(2)}) collective-permute-start(bf16[256,1024]{1,0:T(8,128)(2,1)} %get-tuple-element.109), channel_id=1, source_target_pairs={{0,8},{9,1},{1,0},{8,9},{2,10},{11,3},{3,2},{10,11},{4,12},{13,5},... | collective-permute-start | bytes 1572872 | tf_op jit(solution)/shard_map/ppermute | solution.py:504
  18.7 23.4 %collective-permute-start.2 = (bf16[256,2048]{1,0:T(8,128)(2,1)S(1)}, bf16[256,2048]{1,0:T(8,128)(2,1)S(1)}, u32[]{:S(2)}, u32[]{:S(2)}) collective-permute-start(bf16[256,2048]{1,0:T(8,128)(2,1)S(1)} %copy-done.10), channel_id=1, source_target_pairs={{1,8},{8,1},{3,10},{10,3},{5,12},{12,5},{7,14},{14,7},{17,24},{24,... | collective-permute-start | bytes 3145736 | tf_op jit(solution)/shard_map/ppermute | solution.py:518
  21.2 23.8 %collective-permute-start.4 = (bf16[256,2048]{1,0:T(8,128)(2,1)S(1)}, bf16[256,2048]{1,0:T(8,128)(2,1)}, u32[]{:S(2)}, u32[]{:S(2)}) collective-permute-start(bf16[256,2048]{1,0:T(8,128)(2,1)S(1)} %copy-done.10), channel_id=1, source_target_pairs={{0,8},{9,1},{2,10},{11,3},{4,12},{13,5},{6,14},{15,7},{16,24},{25,... | collective-permute-start | bytes 3145736 | tf_op jit(solution)/shard_map/ppermute | solution.py:516
  22.5 29.8 %collective-permute-start.5 = (bf16[256,2048]{1,0:T(8,128)(2,1)S(1)}, bf16[256,2048]{1,0:T(8,128)(2,1)}, u32[]{:S(2)}, u32[]{:S(2)}) collective-permute-start(bf16[256,2048]{1,0:T(8,128)(2,1)S(1)} %copy-done.10), channel_id=1, source_target_pairs={{1,0},{8,9},{3,2},{10,11},{5,4},{12,13},{7,6},{14,15},{17,16},{24,... | collective-permute-start | bytes 3145736 | tf_op jit(solution)/shard_map/ppermute | solution.py:519
  32.1 33.5 %collective-permute-start.10 = (bf16[2,256,512]{2,1,0:T(8,128)(2,1)S(1)}, bf16[2,256,512]{2,1,0:T(8,128)(2,1)S(1)}, u32[]{:S(2)}, u32[]{:S(2)}) collective-permute-start(bf16[2,256,512]{2,1,0:T(8,128)(2,1)S(1)} %pad_maximum_fusion.1.kv0), channel_id=1, source_target_pairs={{0,2},{2,4},{4,6},{6,0},{1,3},{3,5},{5,7},{7,1},{8,10},{10,12},{12... | collective-permute-start | bytes 1572872 | tf_op jit(solution)/shard_map/ppermute | solution.py:480
  33.5 32.1 %collective-permute-start.8 = (bf16[2,256,512]{2,1,0:T(8,128)(2,1)S(1)}, bf16[2,256,512]{2,1,0:T(8,128)(2,1)S(1)}, u32[]{:S(2)}, u32[]{:S(2)}) collective-permute-start(bf16[2,256,512]{2,1,0:T(8,128)(2,1)S(1)} %pad_maximum_fusion.1.kv0), channel_id=1, source_target_pairs={{0,6},{2,0},{4,2},{6,4},{1,7},{3,1},{5,3},{7,5},{8,14},{10,8},{12,... | collective-permute-start | bytes 1572872 | tf_op jit(solution)/shard_map/ppermute | solution.py:480
  42.1 23.5 %collective-permute-start.9 = (bf16[2,256,512]{2,1,0:T(8,128)(2,1)S(1)}, bf16[2,256,512]{2,1,0:T(8,128)(2,1)S(1)}, u32[]{:S(2)}, u32[]{:S(2)}) collective-permute-start(bf16[2,256,512]{2,1,0:T(8,128)(2,1)S(1)} %pad_maximum_fusion.1.kv0), channel_id=1, source_target_pairs={{0,4},{2,6},{4,0},{6,2},{1,5},{3,7},{5,1},{7,3},{8,12},{10,14},{12... | collective-permute-start | bytes 1572872 | tf_op jit(solution)/shard_map/ppermute | solution.py:480
  66.5 39.4 %collective-permute-start.13 = (bf16[256,2048]{1,0:T(8,128)(2,1)}, bf16[256,2048]{1,0:T(8,128)(2,1)S(1)}, u32[]{:S(2)}, u32[]{:S(2)}) collective-permute-start(bf16[256,2048]{1,0:T(8,128)(2,1)} %get-tuple-element.57), channel_id=1, source_target_pairs={{0,96},{32,0},{64,32},{96,64},{1,97},{33,1},{65,33},{97,65},{2,98}... | collective-permute-start | bytes 3145736 | tf_op jit(solution)/shard_map/ppermute | solution.py:480
  68.9 39.4 %collective-permute-start.14 = (bf16[256,2048]{1,0:T(8,128)(2,1)}, bf16[256,2048]{1,0:T(8,128)(2,1)S(1)}, u32[]{:S(2)}, u32[]{:S(2)}) collective-permute-start(bf16[256,2048]{1,0:T(8,128)(2,1)} %get-tuple-element.57), channel_id=1, source_target_pairs={{0,64},{32,96},{64,0},{96,32},{1,65},{33,97},{65,1},{97,33},{2,66}... | collective-permute-start | bytes 3145736 | tf_op jit(solution)/shard_map/ppermute | solution.py:480
  70.8 47.4 %collective-permute-start.15 = (bf16[256,2048]{1,0:T(8,128)(2,1)}, bf16[256,2048]{1,0:T(8,128)(2,1)S(1)}, u32[]{:S(2)}, u32[]{:S(2)}) collective-permute-start(bf16[256,2048]{1,0:T(8,128)(2,1)} %get-tuple-element.57), channel_id=1, source_target_pairs={{0,32},{32,64},{64,96},{96,0},{1,33},{33,65},{65,97},{97,1},{2,34}... | collective-permute-start | bytes 3145736 | tf_op jit(solution)/shard_map/ppermute | solution.py:480
  94.2 24.6 %collective-permute-start.16 = (bf16[512,512]{1,0:T(8,128)(2,1)}, bf16[512,512]{1,0:T(8,128)(2,1)S(1)}, u32[]{:S(2)}, u32[]{:S(2)}) collective-permute-start(bf16[512,512]{1,0:T(8,128)(2,1)} %get-tuple-element.58), channel_id=1, source_target_pairs={{0,4},{2,6},{4,0},{6,2},{1,5},{3,7},{5,1},{7,3},{8,12},{10,14},{12... | collective-permute-start | bytes 1572872 | tf_op jit(solution)/shard_map/ppermute | solution.py:480
  104.9 23.8 %collective-permute-start.17 = (bf16[512,512]{1,0:T(8,128)(2,1)}, bf16[512,512]{1,0:T(8,128)(2,1)S(1)}, u32[]{:S(2)}, u32[]{:S(2)}) collective-permute-start(bf16[512,512]{1,0:T(8,128)(2,1)} %get-tuple-element.59), channel_id=1, source_target_pairs={{0,2},{2,4},{4,6},{6,0},{1,3},{3,5},{5,7},{7,1},{8,10},{10,12},{12... | collective-permute-start | bytes 1572872 | tf_op jit(solution)/shard_map/ppermute | solution.py:480
  105.9 23.4 %collective-permute-start.18 = (bf16[512,512]{1,0:T(8,128)(2,1)}, bf16[512,512]{1,0:T(8,128)(2,1)S(1)}, u32[]{:S(2)}, u32[]{:S(2)}) collective-permute-start(bf16[512,512]{1,0:T(8,128)(2,1)} %get-tuple-element.60), channel_id=1, source_target_pairs={{0,6},{2,0},{4,2},{6,4},{1,7},{3,1},{5,3},{7,5},{8,14},{10,8},{12,... | collective-permute-start | bytes 1572872 | tf_op jit(solution)/shard_map/ppermute | solution.py:480
  118.2 14.6 %collective-permute-start.21 = (bf16[512,256]{1,0:T(8,128)(2,1)}, bf16[512,256]{1,0:T(8,128)(2,1)S(1)}, u32[]{:S(2)}, u32[]{:S(2)}) collective-permute-start(bf16[512,256]{1,0:T(8,128)(2,1)} %get-tuple-element.66), channel_id=1, source_target_pairs={{0,32},{32,64},{64,96},{96,0},{1,33},{33,65},{65,97},{97,1},{2,34}... | collective-permute-start | bytes 786440 | tf_op jit(solution)/shard_map/ppermute | solution.py:480
  118.2 14.6 %collective-permute-start.20 = (bf16[512,256]{1,0:T(8,128)(2,1)}, bf16[512,256]{1,0:T(8,128)(2,1)S(1)}, u32[]{:S(2)}, u32[]{:S(2)}) collective-permute-start(bf16[512,256]{1,0:T(8,128)(2,1)} %get-tuple-element.64), channel_id=1, source_target_pairs={{0,64},{32,96},{64,0},{96,32},{1,65},{33,97},{65,1},{97,33},{2,66}... | collective-permute-start | bytes 786440 | tf_op jit(solution)/shard_map/ppermute | solution.py:480
  118.8 14.2 %collective-permute-start.19 = (bf16[512,256]{1,0:T(8,128)(2,1)}, bf16[512,256]{1,0:T(8,128)(2,1)S(1)}, u32[]{:S(2)}, u32[]{:S(2)}) collective-permute-start(bf16[512,256]{1,0:T(8,128)(2,1)} %get-tuple-element.62), channel_id=1, source_target_pairs={{0,96},{32,0},{64,32},{96,64},{1,97},{33,1},{65,33},{97,65},{2,98}... | collective-permute-start | bytes 786440 | tf_op jit(solution)/shard_map/ppermute | solution.py:480
  139.9 9.6 %collective-permute-start.26 = (bf16[512,128]{1,0:T(8,128)(2,1)}, bf16[512,128]{1,0:T(8,128)(2,1)S(1)}, u32[]{:S(2)}, u32[]{:S(2)}) collective-permute-start(bf16[512,128]{1,0:T(8,128)(2,1)} %get-tuple-element.77), channel_id=1, source_target_pairs={{0,64},{32,96},{64,0},{96,32},{1,65},{33,97},{65,1},{97,33},{2,66}... | collective-permute-start | bytes 393224 | tf_op jit(solution)/shard_map/ppermute | solution.py:480
  164.5 15.7 %collective-permute-start.28 = (bf16[256,2048]{1,0:T(8,128)(2,1)}, bf16[256,2048]{1,0:T(8,128)(2,1)}, u32[]{:S(2)}, u32[]{:S(2)}) collective-permute-start(bf16[256,2048]{1,0:T(8,128)(2,1)} %get-tuple-element.83), channel_id=1, source_target_pairs={{0,8},{8,0},{1,9},{9,1},{2,10},{10,2},{3,11},{11,3},{4,12},{12,4},... | collective-permute-start | bytes 3145736 | tf_op jit(solution)/shard_map/ppermute | solution.py:484
  165.8 43.0 %all-to-all-start = ((bf16[64,2,16,384]{3,2,1,0:T(8,128)(2,1)}), bf16[64,2,16,384]{3,2,1,0:T(8,128)(2,1)S(1)}, u32[]{:S(2)}, u32[]{:S(2)}) async-start(bf16[64,2,16,384]{3,2,1,0:T(8,128)(2,1)} %bitcast.36), calls=%async_computation | async-start | bytes 3145728 | tf_op jit(solution)/shard_map/all_to_all | solution.py:568
  176.6 30.6 %collective-permute-start.11 = (bf16[256,1024]{1,0:T(8,128)(2,1)S(1)}, bf16[256,1024]{1,0:T(8,128)(2,1)}, u32[]{:S(2)}, u32[]{:S(2)}) collective-permute-start(bf16[256,1024]{1,0:T(8,128)(2,1)S(1)} %copy-done.11), channel_id=1, source_target_pairs={{1,8},{8,1},{3,10},{10,3},{5,12},{12,5},{7,14},{14,7},{17,24},{24,... | collective-permute-start | bytes 1572872 | tf_op jit(solution)/shard_map/ppermute | solution.py:576
  180.2 27.4 %collective-permute-start.12 = (bf16[256,1024]{1,0:T(8,128)(2,1)}, bf16[256,1024]{1,0:T(8,128)(2,1)}, u32[]{:S(2)}, u32[]{:S(2)}) collective-permute-start(bf16[256,1024]{1,0:T(8,128)(2,1)} %get-tuple-element.55), channel_id=1, source_target_pairs={{8,0},{1,9},{0,1},{9,8},{10,2},{3,11},{2,3},{11,10},{12,4},{5,13},... | collective-permute-start | bytes 1572872 | tf_op jit(solution)/shard_map/ppermute | solution.py:575
  182.9 35.7 %collective-permute-start.29 = (bf16[256,2048]{1,0:T(8,128)(2,1)}, bf16[256,2048]{1,0:T(8,128)(2,1)}, u32[]{:S(2)}, u32[]{:S(2)}) collective-permute-start(bf16[256,2048]{1,0:T(8,128)(2,1)} %add_convert_fusion), channel_id=1, source_target_pairs={{1,8},{8,1},{3,10},{10,3},{5,12},{12,5},{7,14},{14,7},{17,24},{24,... | collective-permute-start | bytes 3145736 | tf_op jit(solution)/shard_map/ppermute | solution.py:572
  (38 other events, 355.6 us)
where the time goes:
time: 225 us; the launch traced here: 223 us
  starting transfers between devices  67.5 us (30%)
  Pallas kernels  65.5 us (29%)
  waiting for transfers between devices  62.7 us (28%)
  other arithmetic  14.3 us (6%)
  local copies, waits for them, and re-layouts  9.59 us (4%)
  between operations  3.5 us (2%)
    ppermute x15, starting transfers between devices, shift(): return lax.ppermute(value, axis, [(i, (i + by) % 4) for i in range(4)])  29.7 us
    ppermute x15, waiting for transfers between devices, shift(): return lax.ppermute(value, axis, [(i, (i + by) % 4) for i in range(4)])  20.8 us
    ppermute x1, waiting for transfers between devices, body(): h2 = lax.ppermute(o_keep, PAIR, SPREAD2)  19.5 us
    pallas_call x1, Pallas kernels, attention_call(): pl.pallas_call(attention_kernel, in_specs=[pl.BlockSpec(memory_space=pltp...  16.4 us
    all_to_all x1, starting transfers between devices, body(): lax.all_to_all(parts.reshape(64, 2, 16, WCOLS), ('x', 'zh', 'y', 'zl'), 0...  10.8 us
    pallas_call x2, Pallas kernels, q_call(): pl.pallas_call(q_kernel, grid_spec=pltpu.PrefetchScalarGridSpec(num_scala...  10.3 us
    pallas_call x1, Pallas kernels, weight_call(): pl.pallas_call(weight_kernel, grid_spec=pltpu.PrefetchScalarGridSpec(num_...  9.29 us
    ppermute x1, waiting for transfers between devices, body(): n3 = lax.ppermute(sent, PAIR, VISITOR_ACROSS)  7.28 us
  transfers between devices with their start and end apart: 32, of which 18 were waited for; matrix products, arithmetic and copies ran while one was open for 9% of the time, Pallas kernels for 18%

commit v1 on v0

--- a/solution.py
+++ b/solution.py
@@ -141,22 +141,21 @@
         ),
         out_shape=jax.ShapeDtypeStruct((TOK, 1024), BF16),
         compiler_params=params(),
-        cost_estimate=cost(4),
+        cost_estimate=cost(0.1),
         name="q_proj",
     )(sel, normed, w, table, table)
 
 
 def attention_kernel(
-    where_ref, qs_ref, qm_ref, dos_ref, dom_ref, table_ref, start_ref, kv0, kv1, kv2, kv3,
-    keep_ref, give_ref, dq_ref, x0, x1, x2, x3, t0, t1, t2, t3, kvbuf, acc, score, quarters,
+    where_ref, qs_ref, qm_ref, dos_ref, dom_ref, table_ref, start_ref, kv_ref,
+    keep_ref, give_ref, dq_ref, x0, x1, x2, x3, dkv_ref, kvbuf, acc, score, quarters,
 ):
-    pieces = (kv0, kv1, kv2, kv3)
     home = where_ref[7] == 0
     for r in range(CHIPS):
         for part in range(2):
             for half in range(2):
                 block = where_ref[8 + r * 4 + part * 2 + half]
-                kvbuf[block] = pieces[r][part, half * BLK : (half + 1) * BLK, :]
+                kvbuf[block] = kv_ref[r, part, half * BLK : (half + 1) * BLK, :]
     acc[...] = jnp.zeros_like(acc)
     row = lax.broadcasted_iota(jnp.int32, (PAIR_TOK, COLS), 0)
     for p in range(2):
@@ -246,23 +245,23 @@
                     quarters[j // 2, rows, (j % 2) * HEAD : (j % 2 + 1) * HEAD] = part
     for r, out in enumerate((x0, x1, x2, x3)):
         out[...] = quarters[(where_ref[6] + r) % 4]
-    for r, out in enumerate((t0, t1, t2, t3)):
+    for r in range(CHIPS):
         for j in range(4):
             at, rows = where_ref[8 + r * 4 + j], slice(j * BLK, (j + 1) * BLK)
-            out[rows, :256] = (acc[at, :, :256] * SCALE).astype(BF16)
-            out[rows, 256:] = acc[at, :, 256:].astype(BF16)
-
-
-def attention_call(where, q, do, table, start, pieces):
+            dkv_ref[r, rows, :256] = (acc[at, :, :256] * SCALE).astype(BF16)
+            dkv_ref[r, rows, 256:] = acc[at, :, 256:].astype(BF16)
+
+
+def attention_call(where, q, do, table, start, kv):
     vmem = pl.BlockSpec(memory_space=pltpu.VMEM)
     half = jax.ShapeDtypeStruct((TOK, 1024), BF16)
     out = pl.pallas_call(
         attention_kernel,
-        in_specs=[pl.BlockSpec(memory_space=pltpu.SMEM)] + [vmem] * 10,
-        out_specs=[vmem] * 11,
+        in_specs=[pl.BlockSpec(memory_space=pltpu.SMEM)] + [vmem] * 7,
+        out_specs=[vmem] * 8,
         out_shape=[half, half, jax.ShapeDtypeStruct((CHIP, 1024), BF16)]
         + [jax.ShapeDtypeStruct((CHIP, 256), BF16)] * 4
-        + [jax.ShapeDtypeStruct((CHIP, 512), BF16)] * 4,
+        + [jax.ShapeDtypeStruct((CHIPS, CHIP, 512), BF16)],
         scratch_shapes=[
             pltpu.VMEM((NBLK, BLK, 512), BF16),
             pltpu.VMEM((NBLK, BLK, 512), F32),
@@ -272,12 +271,12 @@
         compiler_params=params(),
         cost_estimate=cost(0.1),
         name="attention",
-    )(where, *q, *do, table, start, *pieces)
-    return out[0], out[1], out[2], out[3:7], out[7:]
-
-
-def joined_kernel(x_ref, a, b, c, d, table_ref, out_ref, j0, j1, j2, j3):
-    total = a[...].astype(F32) + b[...].astype(F32) + c[...].astype(F32) + d[...].astype(F32)
+    )(where, *q, *do, table, start, kv)
+    return out[0], out[1], out[2], out[3:7], out[7]
+
+
+def joined_kernel(x_ref, parts_ref, table_ref, out_ref, j0, j1, j2, j3):
+    total = jnp.sum(parts_ref[...].astype(F32), axis=0)
     for i in range(2):
         cols = slice(i * HEAD, (i + 1) * HEAD)
         out_ref[:, cols] = rotate(total[:, cols], table_ref[:, :HEAD], -table_ref[:, HEAD:]).astype(BF16)
@@ -286,17 +285,17 @@
         out[...] = out_ref[:, pl.ds(pl.multiple_of((x_ref[0] + r) % 4 * HEAD, HEAD), HEAD)]
 
 
-def joined_call(x_at, own, others, table):
+def joined_call(x_at, parts, table):
     vmem = pl.BlockSpec(memory_space=pltpu.VMEM)
     out = pl.pallas_call(
         joined_kernel,
-        in_specs=[pl.BlockSpec(memory_space=pltpu.SMEM)] + [vmem] * 5,
+        in_specs=[pl.BlockSpec(memory_space=pltpu.SMEM)] + [vmem] * 2,
         out_specs=[vmem] * 5,
         out_shape=[jax.ShapeDtypeStruct((CHIP, 512), BF16)] + [jax.ShapeDtypeStruct((CHIP, HEAD), BF16)] * 4,
         compiler_params=params(),
         cost_estimate=cost(0.1),
         name="joined_kv",
-    )(x_at, own, *others, table)
+    )(x_at, parts, table)
     return out[0], out[1:]
 
 
@@ -319,7 +318,7 @@
         ),
         out_shape=jax.ShapeDtypeStruct((CHIP, D), BF16),
         compiler_params=params(),
-        cost_estimate=cost(6),
+        cost_estimate=cost(0.01),
         name="d_normed_q",
     )(sel, jq, w)
 
@@ -351,7 +350,7 @@
         ),
         out_shape=[jax.ShapeDtypeStruct((TOK, D), BF16)] * 2,
         compiler_params=params(),
-        cost_estimate=cost(3),
+        cost_estimate=cost(0.01),
         name="d_normed",
     )(sel, part, jkv, w, w)
 
@@ -501,77 +500,65 @@
 
     g_mine = lax.dynamic_slice_in_dim(grads, zl * 1024, 1024, 1)
     g_other = lax.dynamic_slice_in_dim(grads, (1 - zl) * 1024, 1024, 1)
-    g1 = lax.ppermute(g_other, PAIR, SPREAD1)
-    g2 = lax.ppermute(g_mine, PAIR, SPREAD2)
     lengths = doc_lengths.reshape(16)
+    lengths_near = lax.ppermute(lengths, PAIR, HOME_TO_VISITOR)
 
     normed, kv_mine, kv_other = kv_call(jnp.stack([zl, near, 15 - near]), x, gain2, w, table)
 
-    r1 = lax.ppermute(kv_other, PAIR, SPREAD1)
+    r1 = lax.ppermute(after(kv_other, lengths_near), PAIR, SPREAD1)
     r2 = lax.ppermute(kv_mine, PAIR, SPREAD2)
     kv = jnp.stack([jnp.where(resident, kv_mine, r1), jnp.where(resident, r1, r2)])
-    kv, g1, g2 = lax.optimization_barrier((kv, g1, g2))
-    kv_from = {(4 - by) % 4: shift(kv, "y", by) for by in (2, 1, 3)}
-
-    n1 = lax.ppermute(after(normed, r1, r2), PAIR, HOME_TO_VISITOR)
-    sent = after(normed, r1, r2)
+    kv = jnp.broadcast_to(kv, (CHIPS,) + kv.shape)
+
+    n1 = lax.ppermute(normed, PAIR, HOME_TO_VISITOR)
+    sent = after(normed, kv, n1)
+    kv_all = lax.all_to_all(after(kv, n1), "y", 0, 0, tiled=True)
     n2 = lax.ppermute(sent, PAIR, SPREAD2)
     n3 = lax.ppermute(sent, PAIR, VISITOR_ACROSS)
-    n_s, n_m = jnp.where(resident, normed, n1), jnp.where(resident, n3, n2)
-
-    q = (
-        q_call(jnp.stack([c, near, 15 - near]), n_s, w, table),
-        q_call(jnp.stack([c, far, 15 - far]), n_m, w, table),
-    )
-
-    mine = after(jnp.where(resident, normed, n2), kv_from[1], kv_from[2], kv_from[3], *q)
-    direct = {(4 - by) % 4: shift(mine, "x", by) for by in (2, 1, 3)}
-    direct = [direct[r] for r in (1, 2, 3)]
-
+    n_s = jnp.where(resident, normed, n1)
+
+    q_s = q_call(jnp.stack([c, near, 15 - near]), n_s, w, table)
+
+    g1 = lax.ppermute(after(g_other, q_s), PAIR, SPREAD1)
+    g2 = lax.ppermute(after(g_mine, q_s), PAIR, SPREAD2)
+    g1, g2 = lax.optimization_barrier((g1, g2))
     do = (jnp.where(resident, g_mine, g1), jnp.where(resident, g1, g2))
 
-    lengths_near = lax.ppermute(after(lengths, n2), PAIR, HOME_TO_VISITOR)
     lengths = jnp.where(resident, lengths, lengths_near)
     upto = jnp.arange(16)
     ends = jnp.sum(jnp.where(upto[None, :] <= upto[:, None], lengths[None, :], 0), axis=1)
+    own = [near, 15 - near, far, 15 - far]
     blocks = []
     for r in range(CHIPS):
-        a, b = 2 * ((y + r) % 4) + zl, 2 * ((y + r) % 4) + 1 - zl
+        a, b = 2 * r + zl, 2 * r + 1 - zl
         blocks += [a, 15 - a, b, 15 - b]
-    own = jnp.stack(blocks[:4])
-    positions = (own[:, None] * BLK + jnp.arange(BLK, dtype=jnp.int32)[None, :]).reshape(CHIP)
+    positions = (jnp.stack(own)[:, None] * BLK + jnp.arange(BLK, dtype=jnp.int32)[None, :]).reshape(CHIP)
     start = jnp.max(jnp.where(positions[:, None] >= ends[None, :], ends[None, :], 0), axis=1).astype(jnp.int32)
     start = start.reshape(4, 1, BLK)
     lowest = start[:, 0, 0] // PAIR_TOK
     where = jnp.stack(
-        blocks[:4]
+        own
         + [jnp.minimum(lowest[0], lowest[2]), jnp.minimum(lowest[1], lowest[3]), x_at, role]
         + blocks
     ).astype(jnp.int32)
-    own_table = jnp.concatenate([lax.dynamic_slice_in_dim(table, b * BLK, BLK, 0) for b in blocks[:4]], axis=0)
-
-    o_keep, o_give, dq, dq_to, dkv_to = attention_call(
-        where, q, do, own_table, start, [kv, kv_from[1], kv_from[2], kv_from[3]]
+    own_table = jnp.concatenate([lax.dynamic_slice_in_dim(table, b * BLK, BLK, 0) for b in own], axis=0)
+
+    n3 = after(n3, q_s, where, start, own_table)
+    n_m = jnp.where(resident, n3, n2)
+    q = (q_s, q_call(jnp.stack([c, far, 15 - far]), n_m, w, table))
+
+    mine = after(jnp.where(resident, normed, n2), g1, g2)
+    direct = {(4 - by) % 4: shift(mine, "x", by) for by in (2, 1, 3)}
+    direct = [direct[r] for r in (1, 2, 3)]
+
+    o_keep, o_give, dq, dq_to, dkv = attention_call(
+        where, q, do, own_table, start, kv_all
     )
 
-    others = [shift(dkv_to[by], "y", by) for by in (2, 1, 3)]
+    dkv = lax.all_to_all(dkv, "y", 0, 0, tiled=True)
+    dn_q = dnorm_q_call(sel, dq, w)
     jq = {(4 - by) % 4: shift(after(dq_to[by], *direct), "x", by) for by in (2, 1, 3)}
     jq = [dq_to[0], jq[1], jq[2], jq[3]]
-    dn_q = dnorm_q_call(sel, dq, w)
-    via = [swap_cores(after(piece, dn_q, *others, *jq[1:])) for piece in direct]
-    joined_kv, jkv_to = joined_call(x_at.reshape(1), after(dkv_to[0], dn_q), others, own_table)
-    jkv = {(4 - by) % 4: shift(after(jkv_to[by], *via), "x", by) for by in (2, 1, 3)}
-    jkv = [jkv_to[0], jkv[1], jkv[2], jkv[3]]
-
-    parts = weight_call(sel, (n_s, n_m), direct, via, jq, jkv)
-    dn_keep, dn_give = dnorm_call(sel, after(dn_q, parts), joined_kv, w)
-    parts = lax.all_to_all(parts.reshape(64, 2, 16, WCOLS), ("x", "zh", "y", "zl"), 0, 0, tiled=True)
-
-    d1 = swap_cores(dn_give)
-    summed = (dn_keep.astype(F32) + d1.astype(F32)).astype(BF16)
-    d2 = lax.ppermute(summed, PAIR, SPREAD2)
-    inputs_grad = inputs_call(sel, x, gain2, dn_keep, d1, d2)
-
     h1 = lax.ppermute(o_give, PAIR, RETURN1)
     h2 = lax.ppermute(o_keep, PAIR, SPREAD2)
     half_mine = jnp.where(resident, o_keep, h2)
@@ -579,11 +566,25 @@
         [jnp.where(zl == 0, half_mine, h1), jnp.where(zl == 0, h1, half_mine)], axis=1
     )
 
-    keep, give = sum_call(sel, parts)
-    got = swap_cores(give)
+    via = [swap_cores(after(piece, dn_q, h2, *jq[1:])) for piece in direct]
+    joined_kv, jkv_to = joined_call(x_at.reshape(1), after(dkv, dn_q, attended, *via), own_table)
+    jkv = {(4 - by) % 4: shift(jkv_to[by], "x", by) for by in (2, 1, 3)}
+    jkv = [jkv_to[0], jkv[1], jkv[2], jkv[3]]
+
+    dn_keep, dn_give = dnorm_call(sel, dn_q, joined_kv, w)
+    d1 = swap_cores(dn_give)
+    summed = (dn_keep.astype(F32) + after(d1, *jkv).astype(F32)).astype(BF16)
+    d2 = lax.ppermute(summed, PAIR, SPREAD2)
+    parts = weight_call(after(sel, summed), (n_s, n_m), direct, via, jq, jkv)
+    parts = lax.all_to_all(after(parts, d2).reshape(64, 2, 16, WCOLS), ("x", "zh", "y", "zl"), 0, 0, tiled=True)
+
+    inputs_grad = inputs_call(sel, x, gain2, dn_keep, d1, d2)
+
     at = ((((x_at * 2 + zh) * 2 + c) * 4 + y) * 2 + zl) * 16
     w_rows = lax.dynamic_slice_in_dim(w, at, 16, 0)
     gain_rows = lax.dynamic_slice_in_dim(gain2, at, 16, 1)
+    keep, give = sum_call(sel, after(parts, inputs_grad, w_rows, gain_rows))
+    got = swap_cores(give)
     qkv_grad, gain_grad = finish_call(sel, keep, got, w_rows, gain_rows)
     return (
         attended.reshape(1, 2, 1, BLK, 2048),

time: 225 us -> 216 us (0.960)
  waiting for transfers between devices: 62.7 us -> 49.9 us
  local copies, waits for them, and re-layouts: 9.59 us -> 13.2 us
    ppermute x1, waiting for transfers between devices: 19.5 us -> 0.01 us  [body(): h2 = lax.ppermute(o_keep, PAIR, SPREAD2)]
    all_to_all x1 -> x3, waiting for transfers between devices: 0.01 us -> 16.4 us  [the longest x1 16.4 us: body(): lax.all_to_all(after(parts, d2).reshape(64, 2, 16, WCOLS), ('x', 'zh', 'y...]
    all_to_all x1 -> x3, starting transfers between devices: 10.8 us -> 26.7 us  [the longest x1 14.7 us: body(): dkv = lax.all_to_all(dkv, 'y', 0, 0, tiled=True)]
    ppermute x15 -> x9, starting transfers between devices: 29.7 us -> 15.7 us  [shift(): return lax.ppermute(value, axis, [(i, (i + by) % 4) for i in range(4)])]
    ppermute x15 -> x9, waiting for transfers between devices: 20.8 us -> 8.09 us  [shift(): return lax.ppermute(value, axis, [(i, (i + by) % 4) for i in range(4)])]
    ppermute x5, waiting for transfers between devices: 4.32 us -> 16.6 us  [the longest x1 7.7 us: body(): g2 = lax.ppermute(after(g_mine, q_s), PAIR, SPREAD2)]
    ppermute x1, waiting for transfers between devices: 7.28 us -> 0.01 us  [body(): n3 = lax.ppermute(sent, PAIR, VISITOR_ACROSS)]
    ppermute x1, waiting for transfers between devices: 4.79 us -> 0.01 us  [body(): n2 = lax.ppermute(sent, PAIR, SPREAD2)]
  transfers between devices with their start and end apart: 32 -> 28, of which waited for: 18 -> 15; matrix products, arithmetic and copies ran while one was open for 9% -> 9% of each run, Pallas kernels for 18% -> 25%
where the time goes in v1:
time: 216 us; the launch traced here: 215 us
  starting transfers between devices  69.5 us (32%)
  Pallas kernels  65.2 us (30%)
  waiting for transfers between devices  49.9 us (23%)
  other arithmetic  14.2 us (7%)
  local copies, waits for them, and re-layouts  13.2 us (6%)
  between operations  3.52 us (2%)
    all_to_all x1, waiting for transfers between devices, body(): lax.all_to_all(after(parts, d2).reshape(64, 2, 16, WCOLS), ('x', 'zh', 'y...  16.4 us
    pallas_call x1, Pallas kernels, attention_call(): pl.pallas_call(attention_kernel, in_specs=[pl.BlockSpec(memory_space=pltp...  16.2 us
    ppermute x9, starting transfers between devices, shift(): return lax.ppermute(value, axis, [(i, (i + by) % 4) for i in range(4)])  15.7 us
    all_to_all x1, starting transfers between devices, body(): dkv = lax.all_to_all(dkv, 'y', 0, 0, tiled=True)  14.7 us
    pallas_call x2, Pallas kernels, q_call(): pl.pallas_call(q_kernel, grid_spec=pltpu.PrefetchScalarGridSpec(num_scala...  10.1 us
    pallas_call x1, Pallas kernels, weight_call(): pl.pallas_call(weight_kernel, grid_spec=pltpu.PrefetchScalarGridSpec(num_...  9.28 us
    ppermute x9, waiting for transfers between devices, shift(): return lax.ppermute(value, axis, [(i, (i + by) % 4) for i in range(4)])  8.09 us
    all_to_all x1, starting transfers between devices, body(): lax.all_to_all(after(parts, d2).reshape(64, 2, 16, WCOLS), ('x', 'zh', 'y...  7.8 us
  transfers between devices with their start and end apart: 28, of which 15 were waited for; matrix products, arithmetic and copies ran while one was open for 9% of the time, Pallas kernels for 25%

profile of v1, /device:TPU:1, one launch (start us, length us, event | category | flops | bytes accessed | tf_op | source)
XLA Modules:
  0.0 215.4 jit_solution(2288952285048044059)
XLA Ops:
  2.5 6.0 %kv_home.1 = (bf16[256,2048]{1,0:T(8,128)(2,1)}, bf16[256,512]{1,0:T(8,128)(2,1)}, bf16[256,512]{1,0:T(8,128)(2,1)}) custom-call(s32[3]{0:T(128)} %add_add_fusion.1.sel_ref, bf16[256,2048]{1,0:T(8,128)(2,1)} %bitcast.46, f32[1,2048]{1,0:T(1,128)} %bitcast.51, bf16[2048,3072]{1,0:T(8,128)(2,1)} %wv_ref.3, bf16[2048,3072]{1,0:T(8,128)(2,1)} %wv_ref.3, ...), custom_call_target="tpu_custom_call" | custom-call | flops 10000 | bytes 10485 | tf_op jit(solution)/shard_map/kv_home/pallas_call | solution.py:94
  9.8 4.9 %collective-permute-start.3 = (bf16[256,512]{1,0:T(8,128)(2,1)}, bf16[256,512]{1,0:T(8,128)(2,1)S(1)}, u32[]{:S(2)}, u32[]{:S(2)}) collective-permute-start(bf16[256,512]{1,0:T(8,128)(2,1)} %get-tuple-element.47), channel_id=1, source_target_pairs={{1,8},{8,1},{3,10},{10,3},{5,12},{12,5},{7,14},{14,7},{17,24},{24,... | collective-permute-start | bytes 786440 | tf_op jit(solution)/shard_map/ppermute | solution.py:509
  25.5 3.9 %collective-permute-start.4 = (bf16[256,2048]{1,0:T(8,128)(2,1)S(1)}, bf16[256,2048]{1,0:T(8,128)(2,1)}, u32[]{:S(2)}, u32[]{:S(2)}) collective-permute-start(bf16[256,2048]{1,0:T(8,128)(2,1)S(1)} %copy-done.4), channel_id=1, source_target_pairs={{1,0},{8,9},{3,2},{10,11},{5,4},{12,13},{7,6},{14,15},{17,16},{24,... | collective-permute-start | bytes 3145736 | tf_op jit(solution)/shard_map/ppermute | solution.py:517
  30.6 5.1 %q_proj.2.qs_ref = bf16[256,1024]{1,0:T(8,128)(2,1)} custom-call(s32[3]{0:T(128)} %add_add_fusion.sel_ref, bf16[256,2048]{1,0:T(8,128)(2,1)} %broadcast_select_fusion.2.n_ref.ns, bf16[2048,3072]{1,0:T(8,128)(2,1)} %wv_ref.3, f32[2048,256]{1,0:T(8,128)} %constant.64.clone.ta_ref.tb_ref, f32[2048,256]{1,0:T(8,128)} %constant.64.clone.ta_ref.tb_ref), custom_call_target="tpu_custom_call" | custom-call | flops 100000 | bytes 104857 | tf_op jit(solution)/shard_map/q_proj/pallas_call | solution.py:129
  35.7 3.1 %collective-permute-start.7 = (bf16[256,1024]{1,0:T(8,128)(2,1)}, bf16[256,1024]{1,0:T(8,128)(2,1)}, u32[]{:S(2)}, u32[]{:S(2)}) collective-permute-start(bf16[256,1024]{1,0:T(8,128)(2,1)} %get-tuple-element.53), channel_id=1, source_target_pairs={{1,8},{8,1},{3,10},{10,3},{5,12},{12,5},{7,14},{14,7},{17,24},{24,... | collective-permute-start | bytes 1572872 | tf_op jit(solution)/shard_map/ppermute | solution.py:523
  39.4 4.2 %all-to-all-start = ((bf16[4,2,256,512]{3,2,1,0:T(8,128)(2,1)}), bf16[4,2,256,512]{3,2,1,0:T(8,128)(2,1)S(1)}, u32[]{:S(2)}, u32[]{:S(2)}) async-start(bf16[4,2,256,512]{3,2,1,0:T(8,128)(2,1)} %broadcast_in_dim.35), calls=%async_computation | async-start | bytes 4194304 | tf_op jit(solution)/shard_map/all_to_all | solution.py:515
  47.6 6.5 %collective-permute-done.6 = bf16[256,1024]{1,0:T(8,128)(2,1)} collective-permute-done((bf16[256,1024]{1,0:T(8,128)(2,1)}, bf16[256,1024]{1,0:T(8,128)(2,1)}, u32[]{:S(2)}, u32[]{:S(2)}) %collective-permute-start.6) | collective-permute-done | bytes 524320 | tf_op jit(solution)/shard_map/ppermute | solution.py:522
  54.2 7.7 %collective-permute-done.7 = bf16[256,1024]{1,0:T(8,128)(2,1)} collective-permute-done((bf16[256,1024]{1,0:T(8,128)(2,1)}, bf16[256,1024]{1,0:T(8,128)(2,1)}, u32[]{:S(2)}, u32[]{:S(2)}) %collective-permute-start.7) | collective-permute-done | bytes 524320 | tf_op jit(solution)/shard_map/ppermute | solution.py:523
  61.9 2.7 %broadcast_select_fusion = (bf16[256,2048]{1,0:T(8,128)(2,1)}, bf16[256,2048]{1,0:T(8,128)(2,1)}) fusion(bf16[256,2048]{1,0:T(8,128)(2,1)S(1)} %copy-done.4, bf16[256,2048]{1,0:T(8,128)(2,1)} %collective-permute-done.5, pred[]{:T(512)S(6)} %eq.8, bf16[256,2048]{1,0:T(8,128)(2,1)} %collective-permute-done.4), kind=kLoop, calls=%fused_computation.2 | loop fusion | flops 1048576 | bytes 5242881 | tf_op jit(solution)/shard_map/jit(_where)/select_n | solution.py:550
  71.1 5.0 %q_proj.3.qm_ref = bf16[256,1024]{1,0:T(8,128)(2,1)} custom-call(s32[3]{0:T(128)} %pad_add_fusion.sel_ref, bf16[256,2048]{1,0:T(8,128)(2,1)} %get-tuple-element.107.n_ref.nm, bf16[2048,3072]{1,0:T(8,128)(2,1)} %wv_ref.3, f32[2048,256]{1,0:T(8,128)} %constant.64.clone.ta_ref.tb_ref, f32[2048,256]{1,0:T(8,128)} %constant.64.clone.ta_ref.tb_ref), custom_call_target="tpu_custom_call" | custom-call | flops 100000 | bytes 104857 | tf_op jit(solution)/shard_map/q_proj/pallas_call | solution.py:129
  77.6 16.2 %attention.1 = (bf16[256,1024]{1,0:T(8,128)(2,1)}, bf16[256,1024]{1,0:T(8,128)(2,1)}, bf16[512,1024]{1,0:T(8,128)(2,1)}, bf16[512,256]{1,0:T(8,128)(2,1)}, bf16[...) custom-call(s32[24]{0:T(128)} %stack.135.where_ref, ...), custom_call_target="tpu_custom_call" | custom-call | flops 100000 | bytes 104857 | tf_op jit(solution)/shard_map/attention/pallas_call | solution.py:258
  93.8 3.3 %collective-permute-start.8 = (bf16[256,1024]{1,0:T(8,128)(2,1)}, bf16[256,1024]{1,0:T(8,128)(2,1)S(1)}, u32[]{:S(2)}, u32[]{:S(2)}) collective-permute-start(bf16[256,1024]{1,0:T(8,128)(2,1)} %get-tuple-element.57), channel_id=1, source_target_pairs={{1,8},{8,1},{3,10},{10,3},{5,12},{12,5},{7,14},{14,7},{17,24},{24,... | collective-permute-start | bytes 1572872 | tf_op jit(solution)/shard_map/ppermute | solution.py:563
  97.0 14.7 %all-to-all-start.1 = ((bf16[4,512,512]{2,1,0:T(8,128)(2,1)}), bf16[4,512,512]{2,1,0:T(8,128)(2,1)S(1)}, u32[]{:S(2)}, u32[]{:S(2)}) async-start(bf16[4,512,512]{2,1,0:T(8,128)(2,1)} %get-tuple-element.60), calls=%async_computation.1 | async-start | bytes 4194304 | tf_op jit(solution)/shard_map/all_to_all | solution.py:558
  112.7 6.1 %collective-permute-start.14 = (bf16[512,256]{1,0:T(8,128)(2,1)}, bf16[512,256]{1,0:T(8,128)(2,1)S(1)}, u32[]{:S(2)}, u32[]{:S(2)}) collective-permute-start(bf16[512,256]{1,0:T(8,128)(2,1)} %get-tuple-element.65), channel_id=1, source_target_pairs={{0,64},{32,96},{64,0},{96,32},{1,65},{33,97},{65,1},{97,33},{2,66}... | collective-permute-start | bytes 786440 | tf_op jit(solution)/shard_map/ppermute | solution.py:479
  119.4 6.8 %d_normed_q.1.part_ref = bf16[512,2048]{1,0:T(8,128)(2,1)} custom-call(s32[2]{0:T(128)} %pad_add_fusion.1.sel_ref, bf16[512,1024]{1,0:T(8,128)(2,1)} %get-tuple-element.59.j_ref, bf16[2048,3072]{1,0:T(8,128)(2,1)} %wv_ref.3), custom_call_target="tpu_custom_call" | custom-call | flops 10000 | bytes 10485 | tf_op jit(solution)/shard_map/d_normed_q/pallas_call | solution.py:308
  136.4 3.0 %joined_kv.1 = (bf16[512,512]{1,0:T(8,128)(2,1)}, bf16[512,128]{1,0:T(8,128)(2,1)}, bf16[512,128]{1,0:T(8,128)(2,1)}, bf16[512,128]{1,0:T(8,128)(2,1)}, bf16[512,128]{1,0:T(8,128)(2,1)}) custom-call(s32[1]{0:T(128)} %bitcast.7.x_ref, bf16[4,512,512]{2,1,0:T(8,128)(2,1)} %copy-done.1, f32[512,256]{1,0:T(8,128)} %pad_maximum_fusion.2.table_ref), custom_call_target="tpu_custom_call" | custom-call | flops 100000 | bytes 104857 | tf_op jit(solution)/shard_map/joined_kv/pallas_call | solution.py:290
  139.4 5.3 %d_normed.1 = (bf16[256,2048]{1,0:T(8,128)(2,1)}, bf16[256,2048]{1,0:T(8,128)(2,1)}) custom-call(s32[2]{0:T(128)} %pad_add_fusion.1.sel_ref, bf16[512,2048]{1,0:T(8,128)(2,1)} %d_normed_q.1.part_ref, bf16[512,512]{1,0:T(8,128)(2,1)} %get-tuple-element.72.jkv_ref, bf16[2048,3072]{1,0:T(8,128)(2,1)} %wv_ref.3, bf16[2048,3072]{1,0:T(8,128)(2,1)} %wv_ref.3), custom_call_target="tpu_custom_call" | custom-call | flops 10000 | bytes 10485 | tf_op jit(solution)/shard_map/d_normed/pallas_call | solution.py:338
  145.1 3.0 %collective-permute-start.20 = (bf16[512,128]{1,0:T(8,128)(2,1)S(1)}, bf16[512,128]{1,0:T(8,128)(2,1)S(1)}, u32[]{:S(2)}, u32[]{:S(2)}) collective-permute-start(bf16[512,128]{1,0:T(8,128)(2,1)S(1)} %copy-done.22), channel_id=1, source_target_pairs={{0,96},{32,0},{64,32},{96,64},{1,97},{33,1},{65,33},{97,65},{2,98}... | collective-permute-start | bytes 393224 | tf_op jit(solution)/shard_map/ppermute | solution.py:479
  154.2 3.0 %collective-permute-done.22.k3 = bf16[512,128]{1,0:T(8,128)(2,1)S(1)} collective-permute-done((bf16[512,128]{1,0:T(8,128)(2,1)S(1)}, bf16[512,128]{1,0:T(8,128)(2,1)S(1)}, u32[]{:S(2)}, u32[]{:S(2)}) %collective-permute-start.22) | collective-permute-done | bytes 131104 | tf_op jit(solution)/shard_map/ppermute | solution.py:479
  161.6 9.3 %weight_grad.1 = bf16[8,8,2,16,384]{4,3,2,1,0:T(8,128)(2,1)} custom-call(s32[2]{0:T(128)} %pad_add_fusion.1.sel_ref, bf16[256,2048]{1,0:T(8,128)(2,1)} %broadcast_select_fusion.2.n_ref.ns, bf16[256,2048]{1,0:T(8,128)(2,1)} %get-tuple-element.107.n_ref.nm, bf16[256,2048]{1,0:T(8,128)(2,1)} %collective-permute-done.10.d1, ...), custom_call_target="tpu_custom_call" | custom-call | flops 100000 | bytes 104857 | tf_op jit(solution)/shard_map/weight_grad/pallas_call | solution.py:384
  170.9 4.5 %collective-permute-done.23.far_ref = bf16[256,2048]{1,0:T(8,128)(2,1)S(1)} collective-permute-done((bf16[256,2048]{1,0:T(8,128)(2,1)S(1)}, bf16[256,2048]{1,0:T(8,128)(2,1)S(1)}, u32[]{:S(2)}, u32[]{:S(2)}) %collective-permute-start.23) | collective-permute-done | bytes 1048608 | tf_op jit(solution)/shard_map/ppermute | solution.py:577
  175.4 7.8 %all-to-all-start.2 = ((bf16[64,2,16,384]{3,2,1,0:T(8,128)(2,1)}), bf16[64,2,16,384]{3,2,1,0:T(8,128)(2,1)S(1)}, u32[]{:S(2)}, u32[]{:S(2)}) async-start(bf16[64,2,16,384]{3,2,1,0:T(8,128)(2,1)} %bitcast.45), calls=%async_computation.2 | async-start | bytes 3145728 | tf_op jit(solution)/shard_map/all_to_all | solution.py:579
  186.0 4.5 %inputs_grad.1 = bf16[256,2048]{1,0:T(8,128)(2,1)} custom-call(s32[2]{0:T(128)} %pad_add_fusion.1.sel_ref, bf16[256,2048]{1,0:T(8,128)(2,1)} %bitcast.47, f32[1,2048]{1,0:T(1,128)} %bitcast.52, bf16[256,2048]{1,0:T(8,128)(2,1)} %get-tuple-element.73.keep_ref, bf16[256,2048]{1,0:T(8,128)(2,1)} %copy-done.3, bf16[256,2048]{1,0:T(8,128)(2,1)} %copy-done.7), custom_call_target="tpu_custom_call" | custom-call | flops 100000 | bytes 104857 | tf_op jit(solution)/shard_map/inputs_grad/pallas_call | solution.py:463
  190.5 16.4 %all-to-all-done.2.parts_ref = bf16[64,2,16,384]{3,2,1,0:T(8,128)(2,1)S(1)} async-done(((bf16[64,2,16,384]{3,2,1,0:T(8,128)(2,1)}), bf16[64,2,16,384]{3,2,1,0:T(8,128)(2,1)S(1)}, u32[]{:S(2)}, u32[]{:S(2)}) %all-to-all-start.2) | async-done | bytes 1572896 | tf_op jit(solution)/shard_map/all_to_all | solution.py:579
  (116 shorter events, 58.8 us)
Async XLA Ops:
  0.6 17.3 %collective-permute-start = (s32[16]{0:T(128)}, s32[16]{0:T(128)S(1)}, u32[]{:S(2)}, u32[]{:S(2)}) collective-permute-start(s32[16]{0:T(128)} %bitcast.55), channel_id=1, source_target_pairs={{0,8},{9,1},{2,10},{11,3},{4,12},{13,5},{6,14},{15,7},{16,24},{25,... | collective-permute-start | bytes 200 | tf_op jit(solution)/shard_map/ppermute | solution.py:504
  8.5 12.9 %collective-permute-start.1 = (bf16[256,2048]{1,0:T(8,128)(2,1)}, bf16[256,2048]{1,0:T(8,128)(2,1)S(1)}, u32[]{:S(2)}, u32[]{:S(2)}) collective-permute-start(bf16[256,2048]{1,0:T(8,128)(2,1)} %get-tuple-element.50), channel_id=1, source_target_pairs={{0,8},{9,1},{2,10},{11,3},{4,12},{13,5},{6,14},{15,7},{16,24},{25,... | collective-permute-start | bytes 3145736 | tf_op jit(solution)/shard_map/ppermute | solution.py:513
  9.8 9.2 %collective-permute-start.3 = (bf16[256,512]{1,0:T(8,128)(2,1)}, bf16[256,512]{1,0:T(8,128)(2,1)S(1)}, u32[]{:S(2)}, u32[]{:S(2)}) collective-permute-start(bf16[256,512]{1,0:T(8,128)(2,1)} %get-tuple-element.47), channel_id=1, source_target_pairs={{1,8},{8,1},{3,10},{10,3},{5,12},{12,5},{7,14},{14,7},{17,24},{24,... | collective-permute-start | bytes 786440 | tf_op jit(solution)/shard_map/ppermute | solution.py:509
  23.0 38.9 %collective-permute-start.5 = (bf16[256,2048]{1,0:T(8,128)(2,1)S(1)}, bf16[256,2048]{1,0:T(8,128)(2,1)}, u32[]{:S(2)}, u32[]{:S(2)}) collective-permute-start(bf16[256,2048]{1,0:T(8,128)(2,1)S(1)} %copy-done.4), channel_id=1, source_target_pairs={{1,8},{8,1},{3,10},{10,3},{5,12},{12,5},{7,14},{14,7},{17,24},{24,... | collective-permute-start | bytes 3145736 | tf_op jit(solution)/shard_map/ppermute | solution.py:516
  25.5 36.4 %collective-permute-start.4 = (bf16[256,2048]{1,0:T(8,128)(2,1)S(1)}, bf16[256,2048]{1,0:T(8,128)(2,1)}, u32[]{:S(2)}, u32[]{:S(2)}) collective-permute-start(bf16[256,2048]{1,0:T(8,128)(2,1)S(1)} %copy-done.4), channel_id=1, source_target_pairs={{1,0},{8,9},{3,2},{10,11},{5,4},{12,13},{7,6},{14,15},{17,16},{24,... | collective-permute-start | bytes 3145736 | tf_op jit(solution)/shard_map/ppermute | solution.py:517
  35.7 18.5 %collective-permute-start.6 = (bf16[256,1024]{1,0:T(8,128)(2,1)}, bf16[256,1024]{1,0:T(8,128)(2,1)}, u32[]{:S(2)}, u32[]{:S(2)}) collective-permute-start(bf16[256,1024]{1,0:T(8,128)(2,1)} %get-tuple-element.52), channel_id=1, source_target_pairs={{0,8},{9,1},{1,0},{8,9},{2,10},{11,3},{3,2},{10,11},{4,12},{13,5},... | collective-permute-start | bytes 1572872 | tf_op jit(solution)/shard_map/ppermute | solution.py:522
  35.7 26.2 %collective-permute-start.7 = (bf16[256,1024]{1,0:T(8,128)(2,1)}, bf16[256,1024]{1,0:T(8,128)(2,1)}, u32[]{:S(2)}, u32[]{:S(2)}) collective-permute-start(bf16[256,1024]{1,0:T(8,128)(2,1)} %get-tuple-element.53), channel_id=1, source_target_pairs={{1,8},{8,1},{3,10},{10,3},{5,12},{12,5},{7,14},{14,7},{17,24},{24,... | collective-permute-start | bytes 1572872 | tf_op jit(solution)/shard_map/ppermute | solution.py:523
  39.4 36.7 %all-to-all-start = ((bf16[4,2,256,512]{3,2,1,0:T(8,128)(2,1)}), bf16[4,2,256,512]{3,2,1,0:T(8,128)(2,1)S(1)}, u32[]{:S(2)}, u32[]{:S(2)}) async-start(bf16[4,2,256,512]{3,2,1,0:T(8,128)(2,1)} %broadcast_in_dim.35), calls=%async_computation | async-start | bytes 4194304 | tf_op jit(solution)/shard_map/all_to_all | solution.py:515
  64.6 47.1 %collective-permute-start.10 = (bf16[256,2048]{1,0:T(8,128)(2,1)}, bf16[256,2048]{1,0:T(8,128)(2,1)}, u32[]{:S(2)}, u32[]{:S(2)}) collective-permute-start(bf16[256,2048]{1,0:T(8,128)(2,1)} %get-tuple-element.61), channel_id=1, source_target_pairs={{0,96},{32,0},{64,32},{96,64},{1,97},{33,1},{65,33},{97,65},{2,98}... | collective-permute-start | bytes 3145736 | tf_op jit(solution)/shard_map/ppermute | solution.py:479
  67.1 44.6 %collective-permute-start.11 = (bf16[256,2048]{1,0:T(8,128)(2,1)}, bf16[256,2048]{1,0:T(8,128)(2,1)}, u32[]{:S(2)}, u32[]{:S(2)}) collective-permute-start(bf16[256,2048]{1,0:T(8,128)(2,1)} %get-tuple-element.61), channel_id=1, source_target_pairs={{0,64},{32,96},{64,0},{96,32},{1,65},{33,97},{65,1},{97,33},{2,66}... | collective-permute-start | bytes 3145736 | tf_op jit(solution)/shard_map/ppermute | solution.py:479
  67.6 44.8 %collective-permute-start.12 = (bf16[256,2048]{1,0:T(8,128)(2,1)}, bf16[256,2048]{1,0:T(8,128)(2,1)}, u32[]{:S(2)}, u32[]{:S(2)}) collective-permute-start(bf16[256,2048]{1,0:T(8,128)(2,1)} %get-tuple-element.61), channel_id=1, source_target_pairs={{0,32},{32,64},{64,96},{96,0},{1,33},{33,65},{65,97},{97,1},{2,34}... | collective-permute-start | bytes 3145736 | tf_op jit(solution)/shard_map/ppermute | solution.py:479
  93.8 32.5 %collective-permute-start.8 = (bf16[256,1024]{1,0:T(8,128)(2,1)}, bf16[256,1024]{1,0:T(8,128)(2,1)S(1)}, u32[]{:S(2)}, u32[]{:S(2)}) collective-permute-start(bf16[256,1024]{1,0:T(8,128)(2,1)} %get-tuple-element.57), channel_id=1, source_target_pairs={{1,8},{8,1},{3,10},{10,3},{5,12},{12,5},{7,14},{14,7},{17,24},{24,... | collective-permute-start | bytes 1572872 | tf_op jit(solution)/shard_map/ppermute | solution.py:563
  97.0 36.6 %all-to-all-start.1 = ((bf16[4,512,512]{2,1,0:T(8,128)(2,1)}), bf16[4,512,512]{2,1,0:T(8,128)(2,1)S(1)}, u32[]{:S(2)}, u32[]{:S(2)}) async-start(bf16[4,512,512]{2,1,0:T(8,128)(2,1)} %get-tuple-element.60), calls=%async_computation.1 | async-start | bytes 4194304 | tf_op jit(solution)/shard_map/all_to_all | solution.py:558
  112.4 13.9 %collective-permute-start.13 = (bf16[512,256]{1,0:T(8,128)(2,1)}, bf16[512,256]{1,0:T(8,128)(2,1)S(1)}, u32[]{:S(2)}, u32[]{:S(2)}) collective-permute-start(bf16[512,256]{1,0:T(8,128)(2,1)} %get-tuple-element.63), channel_id=1, source_target_pairs={{0,96},{32,0},{64,32},{96,64},{1,97},{33,1},{65,33},{97,65},{2,98}... | collective-permute-start | bytes 786440 | tf_op jit(solution)/shard_map/ppermute | solution.py:479
  112.7 13.6 %collective-permute-start.14 = (bf16[512,256]{1,0:T(8,128)(2,1)}, bf16[512,256]{1,0:T(8,128)(2,1)S(1)}, u32[]{:S(2)}, u32[]{:S(2)}) collective-permute-start(bf16[512,256]{1,0:T(8,128)(2,1)} %get-tuple-element.65), channel_id=1, source_target_pairs={{0,64},{32,96},{64,0},{96,32},{1,65},{33,97},{65,1},{97,33},{2,66}... | collective-permute-start | bytes 786440 | tf_op jit(solution)/shard_map/ppermute | solution.py:479
  118.8 9.9 %collective-permute-start.15 = (bf16[512,256]{1,0:T(8,128)(2,1)S(1)}, bf16[512,256]{1,0:T(8,128)(2,1)}, u32[]{:S(2)}, u32[]{:S(2)}) collective-permute-start(bf16[512,256]{1,0:T(8,128)(2,1)S(1)} %copy-done.19), channel_id=1, source_target_pairs={{0,32},{32,64},{64,96},{96,0},{1,33},{33,65},{65,97},{97,1},{2,34}... | collective-permute-start | bytes 786440 | tf_op jit(solution)/shard_map/ppermute | solution.py:479
  118.8 12.4 %collective-permute-start.9 = (bf16[256,1024]{1,0:T(8,128)(2,1)}, bf16[256,1024]{1,0:T(8,128)(2,1)}, u32[]{:S(2)}, u32[]{:S(2)}) collective-permute-start(bf16[256,1024]{1,0:T(8,128)(2,1)} %get-tuple-element.58), channel_id=1, source_target_pairs={{8,0},{1,9},{0,1},{9,8},{10,2},{3,11},{2,3},{11,10},{12,4},{5,13},... | collective-permute-start | bytes 1572872 | tf_op jit(solution)/shard_map/ppermute | solution.py:562
  128.7 6.0 %collective-permute-start.16 = (bf16[256,2048]{1,0:T(8,128)(2,1)}, bf16[256,2048]{1,0:T(8,128)(2,1)S(1)}, u32[]{:S(2)}, u32[]{:S(2)}) collective-permute-start(bf16[256,2048]{1,0:T(8,128)(2,1)} %collective-permute-done.10.d1), channel_id=1, source_target_pairs={{0,8},{8,0},{1,9},{9,1},{2,10},{10,2},{3,11},{11,3},{4,12},{12,4},... | collective-permute-start | bytes 3145736 | tf_op jit(solution)/shard_map/ppermute | solution.py:483
  144.7 12.5 %collective-permute-start.19 = (bf16[256,2048]{1,0:T(8,128)(2,1)}, bf16[256,2048]{1,0:T(8,128)(2,1)S(1)}, u32[]{:S(2)}, u32[]{:S(2)}) collective-permute-start(bf16[256,2048]{1,0:T(8,128)(2,1)} %get-tuple-element.74), channel_id=1, source_target_pairs={{0,8},{8,0},{1,9},{9,1},{2,10},{10,2},{3,11},{11,3},{4,12},{12,4},... | collective-permute-start | bytes 3145736 | tf_op jit(solution)/shard_map/ppermute | solution.py:483
  145.1 7.4 %collective-permute-start.20 = (bf16[512,128]{1,0:T(8,128)(2,1)S(1)}, bf16[512,128]{1,0:T(8,128)(2,1)S(1)}, u32[]{:S(2)}, u32[]{:S(2)}) collective-permute-start(bf16[512,128]{1,0:T(8,128)(2,1)S(1)} %copy-done.22), channel_id=1, source_target_pairs={{0,96},{32,0},{64,32},{96,64},{1,97},{33,1},{65,33},{97,65},{2,98}... | collective-permute-start | bytes 393224 | tf_op jit(solution)/shard_map/ppermute | solution.py:479
  148.0 6.1 %collective-permute-start.21 = (bf16[512,128]{1,0:T(8,128)(2,1)S(1)}, bf16[512,128]{1,0:T(8,128)(2,1)S(1)}, u32[]{:S(2)}, u32[]{:S(2)}) collective-permute-start(bf16[512,128]{1,0:T(8,128)(2,1)S(1)} %copy-done.21), channel_id=1, source_target_pairs={{0,64},{32,96},{64,0},{96,32},{1,65},{33,97},{65,1},{97,33},{2,66}... | collective-permute-start | bytes 393224 | tf_op jit(solution)/shard_map/ppermute | solution.py:479
  150.8 6.5 %collective-permute-start.22 = (bf16[512,128]{1,0:T(8,128)(2,1)S(1)}, bf16[512,128]{1,0:T(8,128)(2,1)S(1)}, u32[]{:S(2)}, u32[]{:S(2)}) collective-permute-start(bf16[512,128]{1,0:T(8,128)(2,1)S(1)} %copy-done.20), channel_id=1, source_target_pairs={{0,32},{32,64},{64,96},{96,0},{1,33},{33,65},{65,97},{97,1},{2,34}... | collective-permute-start | bytes 393224 | tf_op jit(solution)/shard_map/ppermute | solution.py:479
  159.3 16.1 %collective-permute-start.23 = (bf16[256,2048]{1,0:T(8,128)(2,1)S(1)}, bf16[256,2048]{1,0:T(8,128)(2,1)S(1)}, u32[]{:S(2)}, u32[]{:S(2)}) collective-permute-start(bf16[256,2048]{1,0:T(8,128)(2,1)S(1)} %add_convert_fusion), channel_id=1, source_target_pairs={{1,8},{8,1},{3,10},{10,3},{5,12},{12,5},{7,14},{14,7},{17,24},{24,... | collective-permute-start | bytes 3145736 | tf_op jit(solution)/shard_map/ppermute | solution.py:577
  175.4 31.5 %all-to-all-start.2 = ((bf16[64,2,16,384]{3,2,1,0:T(8,128)(2,1)}), bf16[64,2,16,384]{3,2,1,0:T(8,128)(2,1)S(1)}, u32[]{:S(2)}, u32[]{:S(2)}) async-start(bf16[64,2,16,384]{3,2,1,0:T(8,128)(2,1)} %bitcast.45), calls=%async_computation.2 | async-start | bytes 3145728 | tf_op jit(solution)/shard_map/all_to_all | solution.py:579
  (27 other events, 161.2 us)

commit v2 on v1

--- a/solution.py
+++ b/solution.py
@@ -521,8 +521,6 @@
 
     g1 = lax.ppermute(after(g_other, q_s), PAIR, SPREAD1)
     g2 = lax.ppermute(after(g_mine, q_s), PAIR, SPREAD2)
-    g1, g2 = lax.optimization_barrier((g1, g2))
-    do = (jnp.where(resident, g_mine, g1), jnp.where(resident, g1, g2))
 
     lengths = jnp.where(resident, lengths, lengths_near)
     upto = jnp.arange(16)
@@ -545,7 +543,10 @@
 
     n3 = after(n3, q_s, where, start, own_table)
     n_m = jnp.where(resident, n3, n2)
-    q = (q_s, q_call(jnp.stack([c, far, 15 - far]), n_m, w, table))
+    q_m = q_call(jnp.stack([c, far, 15 - far]), n_m, w, table)
+    g1, g2, q_m = lax.optimization_barrier((g1, g2, q_m))
+    q = (q_s, q_m)
+    do = (jnp.where(resident, g_mine, g1), jnp.where(resident, g1, g2))
 
     mine = after(jnp.where(resident, normed, n2), g1, g2)
     direct = {(4 - by) % 4: shift(mine, "x", by) for by in (2, 1, 3)}

time: 216 us -> 214 us (level)
  starting transfers between devices: 69.5 us -> 48.4 us
  waiting for transfers between devices: 49.9 us -> 60.5 us
  Pallas kernels: 65.2 us -> 73.1 us
    ppermute x9, waiting for transfers between devices: 8.09 us -> 26.4 us  [shift(): return lax.ppermute(value, axis, [(i, (i + by) % 4) for i in range(4)])]
    all_to_all x1, starting transfers between devices: 14.7 us -> 3.75 us  [body(): dkv = lax.all_to_all(dkv, 'y', 0, 0, tiled=True)]
    ppermute x9, starting transfers between devices: 15.7 us -> 6.91 us  [shift(): return lax.ppermute(value, axis, [(i, (i + by) % 4) for i in range(4)])]
    pallas_call x1, Pallas kernels: 16.2 us -> 24 us  [attention_call(): pl.pallas_call(attention_kernel, in_specs=[pl.BlockSpec(memory_space=pltp...]
    ppermute x1, waiting for transfers between devices: 6.55 us -> 0.01 us  [body(): g1 = lax.ppermute(after(g_other, q_s), PAIR, SPREAD1)]
    ppermute x5, starting transfers between devices: 4.45 us -> 1.49 us  [swap_cores(): return lax.ppermute(value, 'c', [(0, 1), (1, 0)])]
    ppermute x1, waiting for transfers between devices: 7.7 us -> 5.09 us  [body(): g2 = lax.ppermute(after(g_mine, q_s), PAIR, SPREAD2)]
    unnamed x46 -> x52, local copies, waits for them, and re-layouts: 5.15 us -> 4.87 us
  transfers between devices with their start and end apart: 28 -> 28, of which waited for: 15 -> 14; matrix products, arithmetic and copies ran while one was open for 9% -> 9% of each run, Pallas kernels for 25% -> 29%
where the time goes in v2:
time: 214 us; the launch traced here: 213 us
  Pallas kernels  73.1 us (34%)
  waiting for transfers between devices  60.5 us (28%)
  starting transfers between devices  48.4 us (23%)
  other arithmetic  14.3 us (7%)
  local copies, waits for them, and re-layouts  13 us (6%)
  between operations  3.6 us (2%)
    ppermute x9, waiting for transfers between devices, shift(): return lax.ppermute(value, axis, [(i, (i + by) % 4) for i in range(4)])  26.4 us
    pallas_call x1, Pallas kernels, attention_call(): pl.pallas_call(attention_kernel, in_specs=[pl.BlockSpec(memory_space=pltp...  24 us
    all_to_all x1, waiting for transfers between devices, body(): lax.all_to_all(after(parts, d2).reshape(64, 2, 16, WCOLS), ('x', 'zh', 'y...  16.8 us
    pallas_call x2, Pallas kernels, q_call(): pl.pallas_call(q_kernel, grid_spec=pltpu.PrefetchScalarGridSpec(num_scala...  10.2 us
    pallas_call x1, Pallas kernels, weight_call(): pl.pallas_call(weight_kernel, grid_spec=pltpu.PrefetchScalarGridSpec(num_...  9.26 us
    all_to_all x1, starting transfers between devices, body(): lax.all_to_all(after(parts, d2).reshape(64, 2, 16, WCOLS), ('x', 'zh', 'y...  8.32 us
    ppermute x9, starting transfers between devices, shift(): return lax.ppermute(value, axis, [(i, (i + by) % 4) for i in range(4)])  6.91 us
    pallas_call x1, Pallas kernels, dnorm_q_call(): pl.pallas_call(dnorm_q_kernel, grid_spec=pltpu.PrefetchScalarGridSpec(num...  6.82 us
  transfers between devices with their start and end apart: 28, of which 14 were waited for; matrix products, arithmetic and copies ran while one was open for 9% of the time, Pallas kernels for 29%

profile of v2, /device:TPU:1, one launch (start us, length us, event | category | flops | bytes accessed | tf_op | source)
XLA Modules:
  0.0 212.9 jit_solution(12829034577348005576)
XLA Ops:
  2.5 6.0 %kv_home.1 = (bf16[256,2048]{1,0:T(8,128)(2,1)}, bf16[256,512]{1,0:T(8,128)(2,1)}, bf16[256,512]{1,0:T(8,128)(2,1)}) custom-call(s32[3]{0:T(128)} %add_add_fusion.1.sel_ref, bf16[256,2048]{1,0:T(8,128)(2,1)} %bitcast.46, f32[1,2048]{1,0:T(1,128)} %bitcast.51, bf16[2048,3072]{1,0:T(8,128)(2,1)} %wv_ref.3, bf16[2048,3072]{1,0:T(8,128)(2,1)} %wv_ref.3, ...), custom_call_target="tpu_custom_call" | custom-call | flops 10000 | bytes 10485 | tf_op jit(solution)/shard_map/kv_home/pallas_call | solution.py:94
  9.8 4.9 %collective-permute-start.5 = (bf16[256,512]{1,0:T(8,128)(2,1)}, bf16[256,512]{1,0:T(8,128)(2,1)S(1)}, u32[]{:S(2)}, u32[]{:S(2)}) collective-permute-start(bf16[256,512]{1,0:T(8,128)(2,1)} %get-tuple-element.50), channel_id=1, source_target_pairs={{1,8},{8,1},{3,10},{10,3},{5,12},{12,5},{7,14},{14,7},{17,24},{24,... | collective-permute-start | bytes 786440 | tf_op jit(solution)/shard_map/ppermute | solution.py:509
  19.4 3.2 %collective-permute-done.4 = bf16[256,512]{1,0:T(8,128)(2,1)S(1)} collective-permute-done((bf16[256,512]{1,0:T(8,128)(2,1)S(1)}, bf16[256,512]{1,0:T(8,128)(2,1)S(1)}, u32[]{:S(2)}, u32[]{:S(2)}) %collective-permute-start.4) | collective-permute-done | bytes 262176 | tf_op jit(solution)/shard_map/ppermute | solution.py:508
  26.9 3.9 %collective-permute-start.6 = (bf16[256,2048]{1,0:T(8,128)(2,1)S(1)}, bf16[256,2048]{1,0:T(8,128)(2,1)}, u32[]{:S(2)}, u32[]{:S(2)}) collective-permute-start(bf16[256,2048]{1,0:T(8,128)(2,1)S(1)} %copy-done.4), channel_id=1, source_target_pairs={{1,0},{8,9},{3,2},{10,11},{5,4},{12,13},{7,6},{14,15},{17,16},{24,... | collective-permute-start | bytes 3145736 | tf_op jit(solution)/shard_map/ppermute | solution.py:517
  34.3 4.2 %all-to-all-start = ((bf16[4,2,256,512]{3,2,1,0:T(8,128)(2,1)}), bf16[4,2,256,512]{3,2,1,0:T(8,128)(2,1)S(1)}, u32[]{:S(2)}, u32[]{:S(2)}) async-start(bf16[4,2,256,512]{3,2,1,0:T(8,128)(2,1)} %broadcast_in_dim.35), calls=%async_computation | async-start | bytes 4194304 | tf_op jit(solution)/shard_map/all_to_all | solution.py:515
  41.5 5.2 %q_proj.2.qs_ref = bf16[256,1024]{1,0:T(8,128)(2,1)} custom-call(s32[3]{0:T(128)} %add_add_fusion.sel_ref, bf16[256,2048]{1,0:T(8,128)(2,1)} %broadcast_select_fusion.2.n_ref.ns, bf16[2048,3072]{1,0:T(8,128)(2,1)} %wv_ref.3, f32[2048,256]{1,0:T(8,128)} %constant.64.clone.ta_ref.tb_ref, f32[2048,256]{1,0:T(8,128)} %constant.64.clone.ta_ref.tb_ref), custom_call_target="tpu_custom_call" | custom-call | flops 100000 | bytes 104857 | tf_op jit(solution)/shard_map/q_proj/pallas_call | solution.py:129
  46.7 3.4 %collective-permute-start.3 = (bf16[256,1024]{1,0:T(8,128)(2,1)S(1)}, bf16[256,1024]{1,0:T(8,128)(2,1)S(1)}, u32[]{:S(2)}, u32[]{:S(2)}) collective-permute-start(bf16[256,1024]{1,0:T(8,128)(2,1)S(1)} %copy-done.5), channel_id=1, source_target_pairs={{1,8},{8,1},{3,10},{10,3},{5,12},{12,5},{7,14},{14,7},{17,24},{24,... | collective-permute-start | bytes 1572872 | tf_op jit(solution)/shard_map/ppermute | solution.py:523
  52.9 5.0 %q_proj.3.qm_ref = bf16[256,1024]{1,0:T(8,128)(2,1)} custom-call(s32[3]{0:T(128)} %pad_add_fusion.sel_ref, bf16[256,2048]{1,0:T(8,128)(2,1)} %get-tuple-element.109.n_ref.nm, bf16[2048,3072]{1,0:T(8,128)(2,1)} %wv_ref.3, f32[2048,256]{1,0:T(8,128)} %constant.64.clone.ta_ref.tb_ref, f32[2048,256]{1,0:T(8,128)} %constant.64.clone.ta_ref.tb_ref), custom_call_target="tpu_custom_call" | custom-call | flops 100000 | bytes 104857 | tf_op jit(solution)/shard_map/q_proj/pallas_call | solution.py:129
  57.9 5.1 %collective-permute-done.3 = bf16[256,1024]{1,0:T(8,128)(2,1)S(1)} collective-permute-done((bf16[256,1024]{1,0:T(8,128)(2,1)S(1)}, bf16[256,1024]{1,0:T(8,128)(2,1)S(1)}, u32[]{:S(2)}, u32[]{:S(2)}) %collective-permute-start.3) | collective-permute-done | bytes 524320 | tf_op jit(solution)/shard_map/ppermute | solution.py:523
  69.1 24.0 %attention.1 = (bf16[256,1024]{1,0:T(8,128)(2,1)}, bf16[256,1024]{1,0:T(8,128)(2,1)}, bf16[512,1024]{1,0:T(8,128)(2,1)}, bf16[512,256]{1,0:T(8,128)(2,1)}, bf16[...) custom-call(s32[24]{0:T(128)} %stack.135.where_ref, ...), custom_call_target="tpu_custom_call" | custom-call | flops 100000 | bytes 104857 | tf_op jit(solution)/shard_map/attention/pallas_call | solution.py:258
  93.1 3.3 %collective-permute-start.8 = (bf16[256,1024]{1,0:T(8,128)(2,1)}, bf16[256,1024]{1,0:T(8,128)(2,1)S(1)}, u32[]{:S(2)}, u32[]{:S(2)}) collective-permute-start(bf16[256,1024]{1,0:T(8,128)(2,1)} %get-tuple-element.59), channel_id=1, source_target_pairs={{1,8},{8,1},{3,10},{10,3},{5,12},{12,5},{7,14},{14,7},{17,24},{24,... | collective-permute-start | bytes 1572872 | tf_op jit(solution)/shard_map/ppermute | solution.py:564
  96.4 3.8 %all-to-all-start.1 = ((bf16[4,512,512]{2,1,0:T(8,128)(2,1)}), bf16[4,512,512]{2,1,0:T(8,128)(2,1)S(1)}, u32[]{:S(2)}, u32[]{:S(2)}) async-start(bf16[4,512,512]{2,1,0:T(8,128)(2,1)} %get-tuple-element.62), calls=%async_computation.1 | async-start | bytes 4194304 | tf_op jit(solution)/shard_map/all_to_all | solution.py:559
  100.2 9.4 %collective-permute-done.10.d1 = bf16[256,2048]{1,0:T(8,128)(2,1)} collective-permute-done((bf16[256,2048]{1,0:T(8,128)(2,1)}, bf16[256,2048]{1,0:T(8,128)(2,1)}, u32[]{:S(2)}, u32[]{:S(2)}) %collective-permute-start.10) | collective-permute-done | bytes 1048608 | tf_op jit(solution)/shard_map/ppermute | solution.py:479
  109.6 3.8 %collective-permute-done.12.d3 = bf16[256,2048]{1,0:T(8,128)(2,1)} collective-permute-done((bf16[256,2048]{1,0:T(8,128)(2,1)}, bf16[256,2048]{1,0:T(8,128)(2,1)}, u32[]{:S(2)}, u32[]{:S(2)}) %collective-permute-start.12) | collective-permute-done | bytes 1048608 | tf_op jit(solution)/shard_map/ppermute | solution.py:479
  116.7 6.8 %d_normed_q.1.part_ref = bf16[512,2048]{1,0:T(8,128)(2,1)} custom-call(s32[2]{0:T(128)} %pad_add_fusion.1.sel_ref, bf16[512,1024]{1,0:T(8,128)(2,1)} %get-tuple-element.61.j_ref, bf16[2048,3072]{1,0:T(8,128)(2,1)} %wv_ref.3), custom_call_target="tpu_custom_call" | custom-call | flops 10000 | bytes 10485 | tf_op jit(solution)/shard_map/d_normed_q/pallas_call | solution.py:308
  125.0 4.4 %collective-permute-done.15.q3 = bf16[512,256]{1,0:T(8,128)(2,1)} collective-permute-done((bf16[512,256]{1,0:T(8,128)(2,1)S(1)}, bf16[512,256]{1,0:T(8,128)(2,1)}, u32[]{:S(2)}, u32[]{:S(2)}) %collective-permute-start.15) | collective-permute-done | bytes 262176 | tf_op jit(solution)/shard_map/ppermute | solution.py:479
  138.6 5.3 %d_normed.1 = (bf16[256,2048]{1,0:T(8,128)(2,1)}, bf16[256,2048]{1,0:T(8,128)(2,1)}) custom-call(s32[2]{0:T(128)} %pad_add_fusion.1.sel_ref, bf16[512,2048]{1,0:T(8,128)(2,1)} %d_normed_q.1.part_ref, bf16[512,512]{1,0:T(8,128)(2,1)} %get-tuple-element.74.jkv_ref, bf16[2048,3072]{1,0:T(8,128)(2,1)} %wv_ref.3, bf16[2048,3072]{1,0:T(8,128)(2,1)} %wv_ref.3), custom_call_target="tpu_custom_call" | custom-call | flops 10000 | bytes 10485 | tf_op jit(solution)/shard_map/d_normed/pallas_call | solution.py:338
  146.2 3.1 %collective-permute-done.20.k1 = bf16[512,128]{1,0:T(8,128)(2,1)S(1)} collective-permute-done((bf16[512,128]{1,0:T(8,128)(2,1)S(1)}, bf16[512,128]{1,0:T(8,128)(2,1)S(1)}, u32[]{:S(2)}, u32[]{:S(2)}) %collective-permute-start.20) | collective-permute-done | bytes 131104 | tf_op jit(solution)/shard_map/ppermute | solution.py:479
  151.7 3.1 %collective-permute-done.22.k3 = bf16[512,128]{1,0:T(8,128)(2,1)S(1)} collective-permute-done((bf16[512,128]{1,0:T(8,128)(2,1)S(1)}, bf16[512,128]{1,0:T(8,128)(2,1)S(1)}, u32[]{:S(2)}, u32[]{:S(2)}) %collective-permute-start.22) | collective-permute-done | bytes 131104 | tf_op jit(solution)/shard_map/ppermute | solution.py:479
  158.8 9.3 %weight_grad.1 = bf16[8,8,2,16,384]{4,3,2,1,0:T(8,128)(2,1)} custom-call(s32[2]{0:T(128)} %pad_add_fusion.1.sel_ref, bf16[256,2048]{1,0:T(8,128)(2,1)} %broadcast_select_fusion.2.n_ref.ns, bf16[256,2048]{1,0:T(8,128)(2,1)} %get-tuple-element.109.n_ref.nm, bf16[256,2048]{1,0:T(8,128)(2,1)} %collective-permute-done.10.d1, ...), custom_call_target="tpu_custom_call" | custom-call | flops 100000 | bytes 104857 | tf_op jit(solution)/shard_map/weight_grad/pallas_call | solution.py:384
  168.1 4.9 %collective-permute-done.23.far_ref = bf16[256,2048]{1,0:T(8,128)(2,1)S(1)} collective-permute-done((bf16[256,2048]{1,0:T(8,128)(2,1)S(1)}, bf16[256,2048]{1,0:T(8,128)(2,1)S(1)}, u32[]{:S(2)}, u32[]{:S(2)}) %collective-permute-start.23) | collective-permute-done | bytes 1048608 | tf_op jit(solution)/shard_map/ppermute | solution.py:578
  173.0 8.3 %all-to-all-start.2 = ((bf16[64,2,16,384]{3,2,1,0:T(8,128)(2,1)}), bf16[64,2,16,384]{3,2,1,0:T(8,128)(2,1)S(1)}, u32[]{:S(2)}, u32[]{:S(2)}) async-start(bf16[64,2,16,384]{3,2,1,0:T(8,128)(2,1)} %bitcast.45), calls=%async_computation.2 | async-start | bytes 3145728 | tf_op jit(solution)/shard_map/all_to_all | solution.py:580
  184.2 4.5 %inputs_grad.1 = bf16[256,2048]{1,0:T(8,128)(2,1)} custom-call(s32[2]{0:T(128)} %pad_add_fusion.1.sel_ref, bf16[256,2048]{1,0:T(8,128)(2,1)} %bitcast.47, f32[1,2048]{1,0:T(1,128)} %bitcast.52, bf16[256,2048]{1,0:T(8,128)(2,1)} %get-tuple-element.75.keep_ref, bf16[256,2048]{1,0:T(8,128)(2,1)} %copy-done.3, bf16[256,2048]{1,0:T(8,128)(2,1)} %copy-done.9), custom_call_target="tpu_custom_call" | custom-call | flops 100000 | bytes 104857 | tf_op jit(solution)/shard_map/inputs_grad/pallas_call | solution.py:463
  188.7 16.8 %all-to-all-done.2.parts_ref = bf16[64,2,16,384]{3,2,1,0:T(8,128)(2,1)S(1)} async-done(((bf16[64,2,16,384]{3,2,1,0:T(8,128)(2,1)}), bf16[64,2,16,384]{3,2,1,0:T(8,128)(2,1)S(1)}, u32[]{:S(2)}, u32[]{:S(2)}) %all-to-all-start.2) | async-done | bytes 1572896 | tf_op jit(solution)/shard_map/all_to_all | solution.py:580
  (122 shorter events, 57.4 us)
Async XLA Ops:
  0.6 18.6 %collective-permute-start = (s32[16]{0:T(128)}, s32[16]{0:T(128)S(1)}, u32[]{:S(2)}, u32[]{:S(2)}) collective-permute-start(s32[16]{0:T(128)} %bitcast.55), channel_id=1, source_target_pairs={{0,8},{9,1},{2,10},{11,3},{4,12},{13,5},{6,14},{15,7},{16,24},{25,... | collective-permute-start | bytes 200 | tf_op jit(solution)/shard_map/ppermute | solution.py:504
  8.5 14.2 %collective-permute-start.1 = (bf16[256,2048]{1,0:T(8,128)(2,1)}, bf16[256,2048]{1,0:T(8,128)(2,1)S(1)}, u32[]{:S(2)}, u32[]{:S(2)}) collective-permute-start(bf16[256,2048]{1,0:T(8,128)(2,1)} %get-tuple-element.53), channel_id=1, source_target_pairs={{0,8},{9,1},{2,10},{11,3},{4,12},{13,5},{6,14},{15,7},{16,24},{25,... | collective-permute-start | bytes 3145736 | tf_op jit(solution)/shard_map/ppermute | solution.py:513
  9.8 9.6 %collective-permute-start.5 = (bf16[256,512]{1,0:T(8,128)(2,1)}, bf16[256,512]{1,0:T(8,128)(2,1)S(1)}, u32[]{:S(2)}, u32[]{:S(2)}) collective-permute-start(bf16[256,512]{1,0:T(8,128)(2,1)} %get-tuple-element.50), channel_id=1, source_target_pairs={{1,8},{8,1},{3,10},{10,3},{5,12},{12,5},{7,14},{14,7},{17,24},{24,... | collective-permute-start | bytes 786440 | tf_op jit(solution)/shard_map/ppermute | solution.py:509
  24.4 25.7 %collective-permute-start.7 = (bf16[256,2048]{1,0:T(8,128)(2,1)S(1)}, bf16[256,2048]{1,0:T(8,128)(2,1)}, u32[]{:S(2)}, u32[]{:S(2)}) collective-permute-start(bf16[256,2048]{1,0:T(8,128)(2,1)S(1)} %copy-done.4), channel_id=1, source_target_pairs={{1,8},{8,1},{3,10},{10,3},{5,12},{12,5},{7,14},{14,7},{17,24},{24,... | collective-permute-start | bytes 3145736 | tf_op jit(solution)/shard_map/ppermute | solution.py:516
  26.9 23.2 %collective-permute-start.6 = (bf16[256,2048]{1,0:T(8,128)(2,1)S(1)}, bf16[256,2048]{1,0:T(8,128)(2,1)}, u32[]{:S(2)}, u32[]{:S(2)}) collective-permute-start(bf16[256,2048]{1,0:T(8,128)(2,1)S(1)} %copy-done.4), channel_id=1, source_target_pairs={{1,0},{8,9},{3,2},{10,11},{5,4},{12,13},{7,6},{14,15},{17,16},{24,... | collective-permute-start | bytes 3145736 | tf_op jit(solution)/shard_map/ppermute | solution.py:517
  34.3 33.4 %all-to-all-start = ((bf16[4,2,256,512]{3,2,1,0:T(8,128)(2,1)}), bf16[4,2,256,512]{3,2,1,0:T(8,128)(2,1)S(1)}, u32[]{:S(2)}, u32[]{:S(2)}) async-start(bf16[4,2,256,512]{3,2,1,0:T(8,128)(2,1)} %broadcast_in_dim.35), calls=%async_computation | async-start | bytes 4194304 | tf_op jit(solution)/shard_map/all_to_all | solution.py:515
  46.7 11.2 %collective-permute-start.2 = (bf16[256,1024]{1,0:T(8,128)(2,1)S(1)}, bf16[256,1024]{1,0:T(8,128)(2,1)S(1)}, u32[]{:S(2)}, u32[]{:S(2)}) collective-permute-start(bf16[256,1024]{1,0:T(8,128)(2,1)S(1)} %copy-done.11), channel_id=1, source_target_pairs={{0,8},{9,1},{1,0},{8,9},{2,10},{11,3},{3,2},{10,11},{4,12},{13,5},... | collective-permute-start | bytes 1572872 | tf_op jit(solution)/shard_map/ppermute | solution.py:522
  46.7 16.3 %collective-permute-start.3 = (bf16[256,1024]{1,0:T(8,128)(2,1)S(1)}, bf16[256,1024]{1,0:T(8,128)(2,1)S(1)}, u32[]{:S(2)}, u32[]{:S(2)}) collective-permute-start(bf16[256,1024]{1,0:T(8,128)(2,1)S(1)} %copy-done.5), channel_id=1, source_target_pairs={{1,8},{8,1},{3,10},{10,3},{5,12},{12,5},{7,14},{14,7},{17,24},{24,... | collective-permute-start | bytes 1572872 | tf_op jit(solution)/shard_map/ppermute | solution.py:523
  63.0 46.6 %collective-permute-start.10 = (bf16[256,2048]{1,0:T(8,128)(2,1)}, bf16[256,2048]{1,0:T(8,128)(2,1)}, u32[]{:S(2)}, u32[]{:S(2)}) collective-permute-start(bf16[256,2048]{1,0:T(8,128)(2,1)} %get-tuple-element.63), channel_id=1, source_target_pairs={{0,96},{32,0},{64,32},{96,64},{1,97},{33,1},{65,33},{97,65},{2,98}... | collective-permute-start | bytes 3145736 | tf_op jit(solution)/shard_map/ppermute | solution.py:479
  65.5 44.1 %collective-permute-start.11 = (bf16[256,2048]{1,0:T(8,128)(2,1)}, bf16[256,2048]{1,0:T(8,128)(2,1)}, u32[]{:S(2)}, u32[]{:S(2)}) collective-permute-start(bf16[256,2048]{1,0:T(8,128)(2,1)} %get-tuple-element.63), channel_id=1, source_target_pairs={{0,64},{32,96},{64,0},{96,32},{1,65},{33,97},{65,1},{97,33},{2,66}... | collective-permute-start | bytes 3145736 | tf_op jit(solution)/shard_map/ppermute | solution.py:479
  66.0 47.5 %collective-permute-start.12 = (bf16[256,2048]{1,0:T(8,128)(2,1)}, bf16[256,2048]{1,0:T(8,128)(2,1)}, u32[]{:S(2)}, u32[]{:S(2)}) collective-permute-start(bf16[256,2048]{1,0:T(8,128)(2,1)} %get-tuple-element.63), channel_id=1, source_target_pairs={{0,32},{32,64},{64,96},{96,0},{1,33},{33,65},{65,97},{97,1},{2,34}... | collective-permute-start | bytes 3145736 | tf_op jit(solution)/shard_map/ppermute | solution.py:479
  93.1 30.4 %collective-permute-start.8 = (bf16[256,1024]{1,0:T(8,128)(2,1)}, bf16[256,1024]{1,0:T(8,128)(2,1)S(1)}, u32[]{:S(2)}, u32[]{:S(2)}) collective-permute-start(bf16[256,1024]{1,0:T(8,128)(2,1)} %get-tuple-element.59), channel_id=1, source_target_pairs={{1,8},{8,1},{3,10},{10,3},{5,12},{12,5},{7,14},{14,7},{17,24},{24,... | collective-permute-start | bytes 1572872 | tf_op jit(solution)/shard_map/ppermute | solution.py:564
  96.4 36.4 %all-to-all-start.1 = ((bf16[4,512,512]{2,1,0:T(8,128)(2,1)}), bf16[4,512,512]{2,1,0:T(8,128)(2,1)S(1)}, u32[]{:S(2)}, u32[]{:S(2)}) async-start(bf16[4,512,512]{2,1,0:T(8,128)(2,1)} %get-tuple-element.62), calls=%async_computation.1 | async-start | bytes 4194304 | tf_op jit(solution)/shard_map/all_to_all | solution.py:559
  113.5 10.0 %collective-permute-start.13 = (bf16[512,256]{1,0:T(8,128)(2,1)}, bf16[512,256]{1,0:T(8,128)(2,1)S(1)}, u32[]{:S(2)}, u32[]{:S(2)}) collective-permute-start(bf16[512,256]{1,0:T(8,128)(2,1)} %get-tuple-element.65), channel_id=1, source_target_pairs={{0,96},{32,0},{64,32},{96,64},{1,97},{33,1},{65,33},{97,65},{2,98}... | collective-permute-start | bytes 786440 | tf_op jit(solution)/shard_map/ppermute | solution.py:479
  113.8 9.7 %collective-permute-start.14 = (bf16[512,256]{1,0:T(8,128)(2,1)}, bf16[512,256]{1,0:T(8,128)(2,1)S(1)}, u32[]{:S(2)}, u32[]{:S(2)}) collective-permute-start(bf16[512,256]{1,0:T(8,128)(2,1)} %get-tuple-element.67), channel_id=1, source_target_pairs={{0,64},{32,96},{64,0},{96,32},{1,65},{33,97},{65,1},{97,33},{2,66}... | collective-permute-start | bytes 786440 | tf_op jit(solution)/shard_map/ppermute | solution.py:479
  114.3 15.1 %collective-permute-start.15 = (bf16[512,256]{1,0:T(8,128)(2,1)S(1)}, bf16[512,256]{1,0:T(8,128)(2,1)}, u32[]{:S(2)}, u32[]{:S(2)}) collective-permute-start(bf16[512,256]{1,0:T(8,128)(2,1)S(1)} %copy-done.22), channel_id=1, source_target_pairs={{0,32},{32,64},{64,96},{96,0},{1,33},{33,65},{65,97},{97,1},{2,34}... | collective-permute-start | bytes 786440 | tf_op jit(solution)/shard_map/ppermute | solution.py:479
  114.9 15.5 %collective-permute-start.9 = (bf16[256,1024]{1,0:T(8,128)(2,1)}, bf16[256,1024]{1,0:T(8,128)(2,1)}, u32[]{:S(2)}, u32[]{:S(2)}) collective-permute-start(bf16[256,1024]{1,0:T(8,128)(2,1)} %get-tuple-element.60), channel_id=1, source_target_pairs={{8,0},{1,9},{0,1},{9,8},{10,2},{3,11},{2,3},{11,10},{12,4},{5,13},... | collective-permute-start | bytes 1572872 | tf_op jit(solution)/shard_map/ppermute | solution.py:563
  130.0 5.6 %collective-permute-start.18 = (bf16[256,2048]{1,0:T(8,128)(2,1)}, bf16[256,2048]{1,0:T(8,128)(2,1)}, u32[]{:S(2)}, u32[]{:S(2)}) collective-permute-start(bf16[256,2048]{1,0:T(8,128)(2,1)} %collective-permute-done.12.d3), channel_id=1, source_target_pairs={{0,8},{8,0},{1,9},{9,1},{2,10},{10,2},{3,11},{11,3},{4,12},{12,4},... | collective-permute-start | bytes 3145736 | tf_op jit(solution)/shard_map/ppermute | solution.py:483
  143.9 10.9 %collective-permute-start.19 = (bf16[256,2048]{1,0:T(8,128)(2,1)}, bf16[256,2048]{1,0:T(8,128)(2,1)S(1)}, u32[]{:S(2)}, u32[]{:S(2)}) collective-permute-start(bf16[256,2048]{1,0:T(8,128)(2,1)} %get-tuple-element.76), channel_id=1, source_target_pairs={{0,8},{8,0},{1,9},{9,1},{2,10},{10,2},{3,11},{11,3},{4,12},{12,4},... | collective-permute-start | bytes 3145736 | tf_op jit(solution)/shard_map/ppermute | solution.py:483
  144.3 5.0 %collective-permute-start.20 = (bf16[512,128]{1,0:T(8,128)(2,1)S(1)}, bf16[512,128]{1,0:T(8,128)(2,1)S(1)}, u32[]{:S(2)}, u32[]{:S(2)}) collective-permute-start(bf16[512,128]{1,0:T(8,128)(2,1)S(1)} %copy-done.25), channel_id=1, source_target_pairs={{0,96},{32,0},{64,32},{96,64},{1,97},{33,1},{65,33},{97,65},{2,98}... | collective-permute-start | bytes 393224 | tf_op jit(solution)/shard_map/ppermute | solution.py:479
  145.5 6.2 %collective-permute-start.21 = (bf16[512,128]{1,0:T(8,128)(2,1)S(1)}, bf16[512,128]{1,0:T(8,128)(2,1)S(1)}, u32[]{:S(2)}, u32[]{:S(2)}) collective-permute-start(bf16[512,128]{1,0:T(8,128)(2,1)S(1)} %copy-done.24), channel_id=1, source_target_pairs={{0,64},{32,96},{64,0},{96,32},{1,65},{33,97},{65,1},{97,33},{2,66}... | collective-permute-start | bytes 393224 | tf_op jit(solution)/shard_map/ppermute | solution.py:479
  145.5 9.3 %collective-permute-start.22 = (bf16[512,128]{1,0:T(8,128)(2,1)S(1)}, bf16[512,128]{1,0:T(8,128)(2,1)S(1)}, u32[]{:S(2)}, u32[]{:S(2)}) collective-permute-start(bf16[512,128]{1,0:T(8,128)(2,1)S(1)} %copy-done.23), channel_id=1, source_target_pairs={{0,32},{32,64},{64,96},{96,0},{1,33},{33,65},{65,97},{97,1},{2,34}... | collective-permute-start | bytes 393224 | tf_op jit(solution)/shard_map/ppermute | solution.py:479
  156.8 16.1 %collective-permute-start.23 = (bf16[256,2048]{1,0:T(8,128)(2,1)S(1)}, bf16[256,2048]{1,0:T(8,128)(2,1)S(1)}, u32[]{:S(2)}, u32[]{:S(2)}) collective-permute-start(bf16[256,2048]{1,0:T(8,128)(2,1)S(1)} %add_convert_fusion), channel_id=1, source_target_pairs={{1,8},{8,1},{3,10},{10,3},{5,12},{12,5},{7,14},{14,7},{17,24},{24,... | collective-permute-start | bytes 3145736 | tf_op jit(solution)/shard_map/ppermute | solution.py:578
  173.0 32.6 %all-to-all-start.2 = ((bf16[64,2,16,384]{3,2,1,0:T(8,128)(2,1)}), bf16[64,2,16,384]{3,2,1,0:T(8,128)(2,1)S(1)}, u32[]{:S(2)}, u32[]{:S(2)}) async-start(bf16[64,2,16,384]{3,2,1,0:T(8,128)(2,1)} %bitcast.45), calls=%async_computation.2 | async-start | bytes 3145728 | tf_op jit(solution)/shard_map/all_to_all | solution.py:580
  (30 other events, 177.5 us)

commit v3 on v2

--- a/solution.py
+++ b/solution.py
@@ -41,8 +41,8 @@
     return pl.CostEstimate(flops=int(us * 10**6), bytes_accessed=int(us * (1 << 20)), transcendentals=0)
 
 
-def params():
-    return pltpu.CompilerParams(vmem_limit_bytes=VMEM_LIMIT)
+def params(limit=VMEM_LIMIT):
+    return pltpu.CompilerParams(vmem_limit_bytes=limit)
 
 
 def dot_nt(a, b):
@@ -393,7 +393,7 @@
             scratch_shapes=[pltpu.VMEM((WCOLS, 8 * TOK), BF16)],
         ),
         out_shape=jax.ShapeDtypeStruct((8, 8, 2, 16, WCOLS), BF16),
-        compiler_params=params(),
+        compiler_params=params(24 * 1024 * 1024),
         cost_estimate=cost(0.1),
         name="weight_grad",
     )(sel, *tokens, *direct, *via, *jq, *jkv)

time: 214 us -> 216 us (level)
  starting transfers between devices: 48.4 us -> 57.9 us
  Pallas kernels: 73.1 us -> 63.9 us
  waiting for transfers between devices: 60.5 us -> 64 us
    all_to_all x1, starting transfers between devices: 3.75 us -> 14.6 us  [body(): dkv = lax.all_to_all(dkv, 'y', 0, 0, tiled=True)]
    pallas_call x1, Pallas kernels: 24 us -> 16.3 us  [attention_call(): pl.pallas_call(attention_kernel, in_specs=[pl.BlockSpec(memory_space=pltp...]
    ppermute x1, waiting for transfers between devices: 0.01 us -> 2.22 us  [body(): n3 = lax.ppermute(sent, PAIR, VISITOR_ACROSS)]
    unnamed x52 -> x48, local copies, waits for them, and re-layouts: 4.87 us -> 5.25 us
  transfers between devices with their start and end apart: 28 -> 28, of which waited for: 14 -> 16; matrix products, arithmetic and copies ran while one was open for 9% -> 8% of each run, Pallas kernels for 29% -> 24%
where the time goes in v3:
time: 216 us; the launch traced here: 215 us
  waiting for transfers between devices  64 us (30%)
  Pallas kernels  63.9 us (30%)
  starting transfers between devices  57.9 us (27%)
  other arithmetic  13.5 us (6%)
  local copies, waits for them, and re-layouts  12.5 us (6%)
  between operations  3.48 us (2%)
    ppermute x9, waiting for transfers between devices, shift(): return lax.ppermute(value, axis, [(i, (i + by) % 4) for i in range(4)])  25.8 us
    all_to_all x1, waiting for transfers between devices, body(): lax.all_to_all(after(parts, d2).reshape(64, 2, 16, WCOLS), ('x', 'zh', 'y...  16.9 us
    pallas_call x1, Pallas kernels, attention_call(): pl.pallas_call(attention_kernel, in_specs=[pl.BlockSpec(memory_space=pltp...  16.3 us
    all_to_all x1, starting transfers between devices, body(): dkv = lax.all_to_all(dkv, 'y', 0, 0, tiled=True)  14.6 us
    pallas_call x2, Pallas kernels, q_call(): pl.pallas_call(q_kernel, grid_spec=pltpu.PrefetchScalarGridSpec(num_scala...  10.2 us
    all_to_all x1, starting transfers between devices, body(): lax.all_to_all(after(parts, d2).reshape(64, 2, 16, WCOLS), ('x', 'zh', 'y...  8.17 us
    pallas_call x1, Pallas kernels, weight_call(): pl.pallas_call(weight_kernel, grid_spec=pltpu.PrefetchScalarGridSpec(num_...  7.66 us
    ppermute x9, starting transfers between devices, shift(): return lax.ppermute(value, axis, [(i, (i + by) % 4) for i in range(4)])  7 us
  transfers between devices with their start and end apart: 28, of which 16 were waited for; matrix products, arithmetic and copies ran while one was open for 8% of the time, Pallas kernels for 24%

profile of v3, /device:TPU:1, one launch (start us, length us, event | category | flops | bytes accessed | tf_op | source)
XLA Modules:
  0.0 215.1 jit_solution(7201572112747729575)
XLA Ops:
  2.5 6.0 %kv_home.1 = (bf16[256,2048]{1,0:T(8,128)(2,1)}, bf16[256,512]{1,0:T(8,128)(2,1)}, bf16[256,512]{1,0:T(8,128)(2,1)}) custom-call(s32[3]{0:T(128)} %add_add_fusion.1.sel_ref, bf16[256,2048]{1,0:T(8,128)(2,1)} %bitcast.45, f32[1,2048]{1,0:T(1,128)} %bitcast.50, bf16[2048,3072]{1,0:T(8,128)(2,1)} %wv_ref.3, bf16[2048,3072]{1,0:T(8,128)(2,1)} %wv_ref.3, ...), custom_call_target="tpu_custom_call" | custom-call | flops 10000 | bytes 10485 | tf_op jit(solution)/shard_map/kv_home/pallas_call | solution.py:94
  9.8 4.9 %collective-permute-start.5 = (bf16[256,512]{1,0:T(8,128)(2,1)}, bf16[256,512]{1,0:T(8,128)(2,1)}, u32[]{:S(2)}, u32[]{:S(2)}) collective-permute-start(bf16[256,512]{1,0:T(8,128)(2,1)} %get-tuple-element.50), channel_id=1, source_target_pairs={{1,8},{8,1},{3,10},{10,3},{5,12},{12,5},{7,14},{14,7},{17,24},{24,... | collective-permute-start | bytes 786440 | tf_op jit(solution)/shard_map/ppermute | solution.py:509
  26.9 3.2 %collective-permute-start.6 = (bf16[256,2048]{1,0:T(8,128)(2,1)S(1)}, bf16[256,2048]{1,0:T(8,128)(2,1)}, u32[]{:S(2)}, u32[]{:S(2)}) collective-permute-start(bf16[256,2048]{1,0:T(8,128)(2,1)S(1)} %copy-done.11), channel_id=1, source_target_pairs={{1,0},{8,9},{3,2},{10,11},{5,4},{12,13},{7,6},{14,15},{17,16},{24,... | collective-permute-start | bytes 3145736 | tf_op jit(solution)/shard_map/ppermute | solution.py:517
  33.5 4.5 %all-to-all-start = ((bf16[4,2,256,512]{3,2,1,0:T(8,128)(2,1)}), bf16[4,2,256,512]{3,2,1,0:T(8,128)(2,1)}, u32[]{:S(2)}, u32[]{:S(2)}) async-start(bf16[4,2,256,512]{3,2,1,0:T(8,128)(2,1)} %broadcast_in_dim.35), calls=%async_computation | async-start | bytes 4194304 | tf_op jit(solution)/shard_map/all_to_all | solution.py:515
  39.7 5.0 %q_proj.2.qs_ref = bf16[256,1024]{1,0:T(8,128)(2,1)} custom-call(s32[3]{0:T(128)} %add_add_fusion.sel_ref, bf16[256,2048]{1,0:T(8,128)(2,1)} %broadcast_select_fusion.2.n_ref.ns, bf16[2048,3072]{1,0:T(8,128)(2,1)} %wv_ref.3, f32[2048,256]{1,0:T(8,128)} %constant.64.clone.ta_ref.tb_ref, f32[2048,256]{1,0:T(8,128)} %constant.64.clone.ta_ref.tb_ref), custom_call_target="tpu_custom_call" | custom-call | flops 100000 | bytes 104857 | tf_op jit(solution)/shard_map/q_proj/pallas_call | solution.py:129
  44.7 2.9 %collective-permute-start.3 = (bf16[256,1024]{1,0:T(8,128)(2,1)S(1)}, bf16[256,1024]{1,0:T(8,128)(2,1)S(1)}, u32[]{:S(2)}, u32[]{:S(2)}) collective-permute-start(bf16[256,1024]{1,0:T(8,128)(2,1)S(1)} %get-tuple-element.49), channel_id=1, source_target_pairs={{1,8},{8,1},{3,10},{10,3},{5,12},{12,5},{7,14},{14,7},{17,24},{24,... | collective-permute-start | bytes 1572872 | tf_op jit(solution)/shard_map/ppermute | solution.py:523
  52.5 5.2 %q_proj.3.qm_ref = bf16[256,1024]{1,0:T(8,128)(2,1)} custom-call(s32[3]{0:T(128)} %pad_add_fusion.sel_ref, bf16[256,2048]{1,0:T(8,128)(2,1)} %get-tuple-element.109.n_ref.nm, bf16[2048,3072]{1,0:T(8,128)(2,1)} %wv_ref.3, f32[2048,256]{1,0:T(8,128)} %constant.64.clone.ta_ref.tb_ref, f32[2048,256]{1,0:T(8,128)} %constant.64.clone.ta_ref.tb_ref), custom_call_target="tpu_custom_call" | custom-call | flops 100000 | bytes 104857 | tf_op jit(solution)/shard_map/q_proj/pallas_call | solution.py:129
  57.7 5.5 %collective-permute-done.3 = bf16[256,1024]{1,0:T(8,128)(2,1)S(1)} collective-permute-done((bf16[256,1024]{1,0:T(8,128)(2,1)S(1)}, bf16[256,1024]{1,0:T(8,128)(2,1)S(1)}, u32[]{:S(2)}, u32[]{:S(2)}) %collective-permute-start.3) | collective-permute-done | bytes 524320 | tf_op jit(solution)/shard_map/ppermute | solution.py:523
  67.9 16.3 %attention.1 = (bf16[256,1024]{1,0:T(8,128)(2,1)}, bf16[256,1024]{1,0:T(8,128)(2,1)}, bf16[512,1024]{1,0:T(8,128)(2,1)}, bf16[512,256]{1,0:T(8,128)(2,1)}, bf16[...) custom-call(s32[24]{0:T(128)} %stack.135.where_ref, ...), custom_call_target="tpu_custom_call" | custom-call | flops 100000 | bytes 104857 | tf_op jit(solution)/shard_map/attention/pallas_call | solution.py:258
  84.2 3.1 %collective-permute-start.8 = (bf16[256,1024]{1,0:T(8,128)(2,1)}, bf16[256,1024]{1,0:T(8,128)(2,1)}, u32[]{:S(2)}, u32[]{:S(2)}) collective-permute-start(bf16[256,1024]{1,0:T(8,128)(2,1)} %get-tuple-element.59), channel_id=1, source_target_pairs={{1,8},{8,1},{3,10},{10,3},{5,12},{12,5},{7,14},{14,7},{17,24},{24,... | collective-permute-start | bytes 1572872 | tf_op jit(solution)/shard_map/ppermute | solution.py:564
  87.3 14.6 %all-to-all-start.1 = ((bf16[4,512,512]{2,1,0:T(8,128)(2,1)}), bf16[4,512,512]{2,1,0:T(8,128)(2,1)}, u32[]{:S(2)}, u32[]{:S(2)}) async-start(bf16[4,512,512]{2,1,0:T(8,128)(2,1)} %get-tuple-element.62), calls=%async_computation.1 | async-start | bytes 4194304 | tf_op jit(solution)/shard_map/all_to_all | solution.py:559
  101.9 7.9 %collective-permute-done.10.d1 = bf16[256,2048]{1,0:T(8,128)(2,1)S(1)} collective-permute-done((bf16[256,2048]{1,0:T(8,128)(2,1)}, bf16[256,2048]{1,0:T(8,128)(2,1)S(1)}, u32[]{:S(2)}, u32[]{:S(2)}) %collective-permute-start.10) | collective-permute-done | bytes 1048608 | tf_op jit(solution)/shard_map/ppermute | solution.py:479
  109.8 3.9 %collective-permute-done.12.d3 = bf16[256,2048]{1,0:T(8,128)(2,1)S(1)} collective-permute-done((bf16[256,2048]{1,0:T(8,128)(2,1)}, bf16[256,2048]{1,0:T(8,128)(2,1)S(1)}, u32[]{:S(2)}, u32[]{:S(2)}) %collective-permute-start.12) | collective-permute-done | bytes 1048608 | tf_op jit(solution)/shard_map/ppermute | solution.py:479
  116.8 6.8 %d_normed_q.1.part_ref = bf16[512,2048]{1,0:T(8,128)(2,1)} custom-call(s32[2]{0:T(128)} %pad_add_fusion.1.sel_ref, bf16[512,1024]{1,0:T(8,128)(2,1)} %get-tuple-element.61.j_ref, bf16[2048,3072]{1,0:T(8,128)(2,1)} %wv_ref.3), custom_call_target="tpu_custom_call" | custom-call | flops 10000 | bytes 10485 | tf_op jit(solution)/shard_map/d_normed_q/pallas_call | solution.py:308
  124.6 5.0 %collective-permute-done.15.q3 = bf16[512,256]{1,0:T(8,128)(2,1)S(1)} collective-permute-done((bf16[512,256]{1,0:T(8,128)(2,1)}, bf16[512,256]{1,0:T(8,128)(2,1)S(1)}, u32[]{:S(2)}, u32[]{:S(2)}) %collective-permute-start.15) | collective-permute-done | bytes 262176 | tf_op jit(solution)/shard_map/ppermute | solution.py:479
  136.2 3.0 %joined_kv.1 = (bf16[512,512]{1,0:T(8,128)(2,1)}, bf16[512,128]{1,0:T(8,128)(2,1)}, bf16[512,128]{1,0:T(8,128)(2,1)}, bf16[512,128]{1,0:T(8,128)(2,1)}, bf16[512,128]{1,0:T(8,128)(2,1)}) custom-call(s32[1]{0:T(128)} %bitcast.7.x_ref, bf16[4,512,512]{2,1,0:T(8,128)(2,1)} %all-to-all-done.1.parts_ref, f32[512,256]{1,0:T(8,128)} %pad_maximum_fusion.2.table_ref), custom_call_target="tpu_custom_call" | custom-call | flops 100000 | bytes 104857 | tf_op jit(solution)/shard_map/joined_kv/pallas_call | solution.py:290
  139.3 5.3 %d_normed.1 = (bf16[256,2048]{1,0:T(8,128)(2,1)}, bf16[256,2048]{1,0:T(8,128)(2,1)}) custom-call(s32[2]{0:T(128)} %pad_add_fusion.1.sel_ref, bf16[512,2048]{1,0:T(8,128)(2,1)} %d_normed_q.1.part_ref, bf16[512,512]{1,0:T(8,128)(2,1)} %get-tuple-element.74.jkv_ref, bf16[2048,3072]{1,0:T(8,128)(2,1)} %wv_ref.3, bf16[2048,3072]{1,0:T(8,128)(2,1)} %wv_ref.3), custom_call_target="tpu_custom_call" | custom-call | flops 10000 | bytes 10485 | tf_op jit(solution)/shard_map/d_normed/pallas_call | solution.py:338
  147.0 3.0 %collective-permute-done.20.k1 = bf16[512,128]{1,0:T(8,128)(2,1)S(1)} collective-permute-done((bf16[512,128]{1,0:T(8,128)(2,1)S(1)}, bf16[512,128]{1,0:T(8,128)(2,1)S(1)}, u32[]{:S(2)}, u32[]{:S(2)}) %collective-permute-start.20) | collective-permute-done | bytes 131104 | tf_op jit(solution)/shard_map/ppermute | solution.py:479
  152.5 3.1 %collective-permute-done.22.k3 = bf16[512,128]{1,0:T(8,128)(2,1)S(1)} collective-permute-done((bf16[512,128]{1,0:T(8,128)(2,1)S(1)}, bf16[512,128]{1,0:T(8,128)(2,1)S(1)}, u32[]{:S(2)}, u32[]{:S(2)}) %collective-permute-start.22) | collective-permute-done | bytes 131104 | tf_op jit(solution)/shard_map/ppermute | solution.py:479
  160.2 7.7 %weight_grad.1 = bf16[8,8,2,16,384]{4,3,2,1,0:T(8,128)(2,1)} custom-call(s32[2]{0:T(128)S(1)} %copy-done.8, bf16[256,2048]{1,0:T(8,128)(2,1)S(1)} %copy-done, bf16[256,2048]{1,0:T(8,128)(2,1)S(1)} %copy-done.1, bf16[256,2048]{1,0:T(8,128)(2,1)S(1)} %collective-permute-done.10.d1, bf16[256,2048]{1,0:T(8,128)(2,1)S(1)} %collective-permute-done.11.d2, ...), custom_call_target="tpu_custom_call" | custom-call | flops 100000 | bytes 104857 | tf_op jit(solution)/shard_map/weight_grad/pallas_call | solution.py:384
  167.9 6.5 %collective-permute-done.23.far_ref = bf16[256,2048]{1,0:T(8,128)(2,1)S(1)} collective-permute-done((bf16[256,2048]{1,0:T(8,128)(2,1)S(1)}, bf16[256,2048]{1,0:T(8,128)(2,1)S(1)}, u32[]{:S(2)}, u32[]{:S(2)}) %collective-permute-start.23) | collective-permute-done | bytes 1048608 | tf_op jit(solution)/shard_map/ppermute | solution.py:578
  175.4 8.2 %all-to-all-start.2 = ((bf16[64,2,16,384]{3,2,1,0:T(8,128)(2,1)}), bf16[64,2,16,384]{3,2,1,0:T(8,128)(2,1)S(1)}, u32[]{:S(2)}, u32[]{:S(2)}) async-start(bf16[64,2,16,384]{3,2,1,0:T(8,128)(2,1)} %bitcast.35), calls=%async_computation.2 | async-start | bytes 3145728 | tf_op jit(solution)/shard_map/all_to_all | solution.py:580
  186.4 4.5 %inputs_grad.1 = bf16[256,2048]{1,0:T(8,128)(2,1)} custom-call(s32[2]{0:T(128)} %pad_add_fusion.1.sel_ref, bf16[256,2048]{1,0:T(8,128)(2,1)} %bitcast.46, f32[1,2048]{1,0:T(1,128)} %bitcast.51, bf16[256,2048]{1,0:T(8,128)(2,1)} %get-tuple-element.75.keep_ref, bf16[256,2048]{1,0:T(8,128)(2,1)} %copy-done.10, bf16[256,2048]{1,0:T(8,128)(2,1)} %copy-done.15), custom_call_target="tpu_custom_call" | custom-call | flops 100000 | bytes 104857 | tf_op jit(solution)/shard_map/inputs_grad/pallas_call | solution.py:463
  190.9 16.9 %all-to-all-done.2.parts_ref = bf16[64,2,16,384]{3,2,1,0:T(8,128)(2,1)S(1)} async-done(((bf16[64,2,16,384]{3,2,1,0:T(8,128)(2,1)}), bf16[64,2,16,384]{3,2,1,0:T(8,128)(2,1)S(1)}, u32[]{:S(2)}, u32[]{:S(2)}) %all-to-all-start.2) | async-done | bytes 1572896 | tf_op jit(solution)/shard_map/all_to_all | solution.py:580
  (118 shorter events, 58.6 us)
Async XLA Ops:
  0.6 17.8 %collective-permute-start = (s32[16]{0:T(128)}, s32[16]{0:T(128)S(1)}, u32[]{:S(2)}, u32[]{:S(2)}) collective-permute-start(s32[16]{0:T(128)} %bitcast.54), channel_id=1, source_target_pairs={{0,8},{9,1},{2,10},{11,3},{4,12},{13,5},{6,14},{15,7},{16,24},{25,... | collective-permute-start | bytes 200 | tf_op jit(solution)/shard_map/ppermute | solution.py:504
  8.5 14.5 %collective-permute-start.1 = (bf16[256,2048]{1,0:T(8,128)(2,1)}, bf16[256,2048]{1,0:T(8,128)(2,1)S(1)}, u32[]{:S(2)}, u32[]{:S(2)}) collective-permute-start(bf16[256,2048]{1,0:T(8,128)(2,1)} %get-tuple-element.53), channel_id=1, source_target_pairs={{0,8},{9,1},{2,10},{11,3},{4,12},{13,5},{6,14},{15,7},{16,24},{25,... | collective-permute-start | bytes 3145736 | tf_op jit(solution)/shard_map/ppermute | solution.py:513
  9.8 9.3 %collective-permute-start.5 = (bf16[256,512]{1,0:T(8,128)(2,1)}, bf16[256,512]{1,0:T(8,128)(2,1)}, u32[]{:S(2)}, u32[]{:S(2)}) collective-permute-start(bf16[256,512]{1,0:T(8,128)(2,1)} %get-tuple-element.50), channel_id=1, source_target_pairs={{1,8},{8,1},{3,10},{10,3},{5,12},{12,5},{7,14},{14,7},{17,24},{24,... | collective-permute-start | bytes 786440 | tf_op jit(solution)/shard_map/ppermute | solution.py:509
  24.6 25.2 %collective-permute-start.7 = (bf16[256,2048]{1,0:T(8,128)(2,1)S(1)}, bf16[256,2048]{1,0:T(8,128)(2,1)}, u32[]{:S(2)}, u32[]{:S(2)}) collective-permute-start(bf16[256,2048]{1,0:T(8,128)(2,1)S(1)} %copy-done.11), channel_id=1, source_target_pairs={{1,8},{8,1},{3,10},{10,3},{5,12},{12,5},{7,14},{14,7},{17,24},{24,... | collective-permute-start | bytes 3145736 | tf_op jit(solution)/shard_map/ppermute | solution.py:516
  26.9 23.0 %collective-permute-start.6 = (bf16[256,2048]{1,0:T(8,128)(2,1)S(1)}, bf16[256,2048]{1,0:T(8,128)(2,1)}, u32[]{:S(2)}, u32[]{:S(2)}) collective-permute-start(bf16[256,2048]{1,0:T(8,128)(2,1)S(1)} %copy-done.11), channel_id=1, source_target_pairs={{1,0},{8,9},{3,2},{10,11},{5,4},{12,13},{7,6},{14,15},{17,16},{24,... | collective-permute-start | bytes 3145736 | tf_op jit(solution)/shard_map/ppermute | solution.py:517
  33.5 34.4 %all-to-all-start = ((bf16[4,2,256,512]{3,2,1,0:T(8,128)(2,1)}), bf16[4,2,256,512]{3,2,1,0:T(8,128)(2,1)}, u32[]{:S(2)}, u32[]{:S(2)}) async-start(bf16[4,2,256,512]{3,2,1,0:T(8,128)(2,1)} %broadcast_in_dim.35), calls=%async_computation | async-start | bytes 4194304 | tf_op jit(solution)/shard_map/all_to_all | solution.py:515
  44.7 13.0 %collective-permute-start.2 = (bf16[256,1024]{1,0:T(8,128)(2,1)S(1)}, bf16[256,1024]{1,0:T(8,128)(2,1)S(1)}, u32[]{:S(2)}, u32[]{:S(2)}) collective-permute-start(bf16[256,1024]{1,0:T(8,128)(2,1)S(1)} %get-tuple-element.48), channel_id=1, source_target_pairs={{0,8},{9,1},{1,0},{8,9},{2,10},{11,3},{3,2},{10,11},{4,12},{13,5},... | collective-permute-start | bytes 1572872 | tf_op jit(solution)/shard_map/ppermute | solution.py:522
  44.7 18.5 %collective-permute-start.3 = (bf16[256,1024]{1,0:T(8,128)(2,1)S(1)}, bf16[256,1024]{1,0:T(8,128)(2,1)S(1)}, u32[]{:S(2)}, u32[]{:S(2)}) collective-permute-start(bf16[256,1024]{1,0:T(8,128)(2,1)S(1)} %get-tuple-element.49), channel_id=1, source_target_pairs={{1,8},{8,1},{3,10},{10,3},{5,12},{12,5},{7,14},{14,7},{17,24},{24,... | collective-permute-start | bytes 1572872 | tf_op jit(solution)/shard_map/ppermute | solution.py:523
  63.2 46.6 %collective-permute-start.10 = (bf16[256,2048]{1,0:T(8,128)(2,1)}, bf16[256,2048]{1,0:T(8,128)(2,1)S(1)}, u32[]{:S(2)}, u32[]{:S(2)}) collective-permute-start(bf16[256,2048]{1,0:T(8,128)(2,1)} %get-tuple-element.63), channel_id=1, source_target_pairs={{0,96},{32,0},{64,32},{96,64},{1,97},{33,1},{65,33},{97,65},{2,98}... | collective-permute-start | bytes 3145736 | tf_op jit(solution)/shard_map/ppermute | solution.py:479
  65.7 44.1 %collective-permute-start.11 = (bf16[256,2048]{1,0:T(8,128)(2,1)}, bf16[256,2048]{1,0:T(8,128)(2,1)S(1)}, u32[]{:S(2)}, u32[]{:S(2)}) collective-permute-start(bf16[256,2048]{1,0:T(8,128)(2,1)} %get-tuple-element.63), channel_id=1, source_target_pairs={{0,64},{32,96},{64,0},{96,32},{1,65},{33,97},{65,1},{97,33},{2,66}... | collective-permute-start | bytes 3145736 | tf_op jit(solution)/shard_map/ppermute | solution.py:479
  66.2 47.5 %collective-permute-start.12 = (bf16[256,2048]{1,0:T(8,128)(2,1)}, bf16[256,2048]{1,0:T(8,128)(2,1)S(1)}, u32[]{:S(2)}, u32[]{:S(2)}) collective-permute-start(bf16[256,2048]{1,0:T(8,128)(2,1)} %get-tuple-element.63), channel_id=1, source_target_pairs={{0,32},{32,64},{64,96},{96,0},{1,33},{33,65},{65,97},{97,1},{2,34}... | collective-permute-start | bytes 3145736 | tf_op jit(solution)/shard_map/ppermute | solution.py:479
  84.2 39.4 %collective-permute-start.8 = (bf16[256,1024]{1,0:T(8,128)(2,1)}, bf16[256,1024]{1,0:T(8,128)(2,1)}, u32[]{:S(2)}, u32[]{:S(2)}) collective-permute-start(bf16[256,1024]{1,0:T(8,128)(2,1)} %get-tuple-element.59), channel_id=1, source_target_pairs={{1,8},{8,1},{3,10},{10,3},{5,12},{12,5},{7,14},{14,7},{17,24},{24,... | collective-permute-start | bytes 1572872 | tf_op jit(solution)/shard_map/ppermute | solution.py:564
  87.3 46.3 %all-to-all-start.1 = ((bf16[4,512,512]{2,1,0:T(8,128)(2,1)}), bf16[4,512,512]{2,1,0:T(8,128)(2,1)}, u32[]{:S(2)}, u32[]{:S(2)}) async-start(bf16[4,512,512]{2,1,0:T(8,128)(2,1)} %get-tuple-element.62), calls=%async_computation.1 | async-start | bytes 4194304 | tf_op jit(solution)/shard_map/all_to_all | solution.py:559
  113.7 9.9 %collective-permute-start.13 = (bf16[512,256]{1,0:T(8,128)(2,1)}, bf16[512,256]{1,0:T(8,128)(2,1)S(1)}, u32[]{:S(2)}, u32[]{:S(2)}) collective-permute-start(bf16[512,256]{1,0:T(8,128)(2,1)} %get-tuple-element.65), channel_id=1, source_target_pairs={{0,96},{32,0},{64,32},{96,64},{1,97},{33,1},{65,33},{97,65},{2,98}... | collective-permute-start | bytes 786440 | tf_op jit(solution)/shard_map/ppermute | solution.py:479
  114.1 9.9 %collective-permute-start.14 = (bf16[512,256]{1,0:T(8,128)(2,1)}, bf16[512,256]{1,0:T(8,128)(2,1)S(1)}, u32[]{:S(2)}, u32[]{:S(2)}) collective-permute-start(bf16[512,256]{1,0:T(8,128)(2,1)} %get-tuple-element.67), channel_id=1, source_target_pairs={{0,64},{32,96},{64,0},{96,32},{1,65},{33,97},{65,1},{97,33},{2,66}... | collective-permute-start | bytes 786440 | tf_op jit(solution)/shard_map/ppermute | solution.py:479
  114.6 15.1 %collective-permute-start.15 = (bf16[512,256]{1,0:T(8,128)(2,1)}, bf16[512,256]{1,0:T(8,128)(2,1)S(1)}, u32[]{:S(2)}, u32[]{:S(2)}) collective-permute-start(bf16[512,256]{1,0:T(8,128)(2,1)} %get-tuple-element.69), channel_id=1, source_target_pairs={{0,32},{32,64},{64,96},{96,0},{1,33},{33,65},{65,97},{97,1},{2,34}... | collective-permute-start | bytes 786440 | tf_op jit(solution)/shard_map/ppermute | solution.py:479
  115.2 16.1 %collective-permute-start.9 = (bf16[256,1024]{1,0:T(8,128)(2,1)}, bf16[256,1024]{1,0:T(8,128)(2,1)}, u32[]{:S(2)}, u32[]{:S(2)}) collective-permute-start(bf16[256,1024]{1,0:T(8,128)(2,1)} %get-tuple-element.60), channel_id=1, source_target_pairs={{8,0},{1,9},{0,1},{9,8},{10,2},{3,11},{2,3},{11,10},{12,4},{5,13},... | collective-permute-start | bytes 1572872 | tf_op jit(solution)/shard_map/ppermute | solution.py:563
  130.8 5.4 %collective-permute-start.18 = (bf16[256,2048]{1,0:T(8,128)(2,1)S(1)}, bf16[256,2048]{1,0:T(8,128)(2,1)}, u32[]{:S(2)}, u32[]{:S(2)}) collective-permute-start(bf16[256,2048]{1,0:T(8,128)(2,1)S(1)} %collective-permute-done.12.d3), channel_id=1, source_target_pairs={{0,8},{8,0},{1,9},{9,1},{2,10},{10,2},{3,11},{11,3},{4,12},{12,4},... | collective-permute-start | bytes 3145736 | tf_op jit(solution)/shard_map/ppermute | solution.py:483
  144.6 11.0 %collective-permute-start.19 = (bf16[256,2048]{1,0:T(8,128)(2,1)}, bf16[256,2048]{1,0:T(8,128)(2,1)S(1)}, u32[]{:S(2)}, u32[]{:S(2)}) collective-permute-start(bf16[256,2048]{1,0:T(8,128)(2,1)} %get-tuple-element.76), channel_id=1, source_target_pairs={{0,8},{8,0},{1,9},{9,1},{2,10},{10,2},{3,11},{11,3},{4,12},{12,4},... | collective-permute-start | bytes 3145736 | tf_op jit(solution)/shard_map/ppermute | solution.py:483
  145.1 5.0 %collective-permute-start.20 = (bf16[512,128]{1,0:T(8,128)(2,1)S(1)}, bf16[512,128]{1,0:T(8,128)(2,1)S(1)}, u32[]{:S(2)}, u32[]{:S(2)}) collective-permute-start(bf16[512,128]{1,0:T(8,128)(2,1)S(1)} %copy-done.23), channel_id=1, source_target_pairs={{0,96},{32,0},{64,32},{96,64},{1,97},{33,1},{65,33},{97,65},{2,98}... | collective-permute-start | bytes 393224 | tf_op jit(solution)/shard_map/ppermute | solution.py:479
  146.3 6.2 %collective-permute-start.21 = (bf16[512,128]{1,0:T(8,128)(2,1)S(1)}, bf16[512,128]{1,0:T(8,128)(2,1)S(1)}, u32[]{:S(2)}, u32[]{:S(2)}) collective-permute-start(bf16[512,128]{1,0:T(8,128)(2,1)S(1)} %copy-done.22), channel_id=1, source_target_pairs={{0,64},{32,96},{64,0},{96,32},{1,65},{33,97},{65,1},{97,33},{2,66}... | collective-permute-start | bytes 393224 | tf_op jit(solution)/shard_map/ppermute | solution.py:479
  146.3 9.3 %collective-permute-start.22 = (bf16[512,128]{1,0:T(8,128)(2,1)S(1)}, bf16[512,128]{1,0:T(8,128)(2,1)S(1)}, u32[]{:S(2)}, u32[]{:S(2)}) collective-permute-start(bf16[512,128]{1,0:T(8,128)(2,1)S(1)} %copy-done.21), channel_id=1, source_target_pairs={{0,32},{32,64},{64,96},{96,0},{1,33},{33,65},{65,97},{97,1},{2,34}... | collective-permute-start | bytes 393224 | tf_op jit(solution)/shard_map/ppermute | solution.py:479
  158.2 16.1 %collective-permute-start.23 = (bf16[256,2048]{1,0:T(8,128)(2,1)S(1)}, bf16[256,2048]{1,0:T(8,128)(2,1)S(1)}, u32[]{:S(2)}, u32[]{:S(2)}) collective-permute-start(bf16[256,2048]{1,0:T(8,128)(2,1)S(1)} %add_convert_fusion), channel_id=1, source_target_pairs={{1,8},{8,1},{3,10},{10,3},{5,12},{12,5},{7,14},{14,7},{17,24},{24,... | collective-permute-start | bytes 3145736 | tf_op jit(solution)/shard_map/ppermute | solution.py:578
  175.4 32.5 %all-to-all-start.2 = ((bf16[64,2,16,384]{3,2,1,0:T(8,128)(2,1)}), bf16[64,2,16,384]{3,2,1,0:T(8,128)(2,1)S(1)}, u32[]{:S(2)}, u32[]{:S(2)}) async-start(bf16[64,2,16,384]{3,2,1,0:T(8,128)(2,1)} %bitcast.35), calls=%async_computation.2 | async-start | bytes 3145728 | tf_op jit(solution)/shard_map/all_to_all | solution.py:580
  (28 other events, 220.5 us)

commit v4 on v2

--- a/solution.py
+++ b/solution.py
@@ -572,19 +572,19 @@
     jkv = {(4 - by) % 4: shift(jkv_to[by], "x", by) for by in (2, 1, 3)}
     jkv = [jkv_to[0], jkv[1], jkv[2], jkv[3]]
 
-    dn_keep, dn_give = dnorm_call(sel, dn_q, joined_kv, w)
+    parts = weight_call(sel, (n_s, n_m), direct, via, jq, jkv)
+    dn_keep, dn_give = dnorm_call(sel, after(dn_q, parts), joined_kv, w)
     d1 = swap_cores(dn_give)
-    summed = (dn_keep.astype(F32) + after(d1, *jkv).astype(F32)).astype(BF16)
+    summed = (dn_keep.astype(F32) + d1.astype(F32)).astype(BF16)
     d2 = lax.ppermute(summed, PAIR, SPREAD2)
-    parts = weight_call(after(sel, summed), (n_s, n_m), direct, via, jq, jkv)
-    parts = lax.all_to_all(after(parts, d2).reshape(64, 2, 16, WCOLS), ("x", "zh", "y", "zl"), 0, 0, tiled=True)
+    parts = lax.all_to_all(parts.reshape(64, 2, 16, WCOLS), ("x", "zh", "y", "zl"), 0, 0, tiled=True)
 
     inputs_grad = inputs_call(sel, x, gain2, dn_keep, d1, d2)
 
     at = ((((x_at * 2 + zh) * 2 + c) * 4 + y) * 2 + zl) * 16
     w_rows = lax.dynamic_slice_in_dim(w, at, 16, 0)
     gain_rows = lax.dynamic_slice_in_dim(gain2, at, 16, 1)
-    keep, give = sum_call(sel, after(parts, inputs_grad, w_rows, gain_rows))
+    keep, give = sum_call(sel, after(parts, w_rows, gain_rows))
     got = swap_cores(give)
     qkv_grad, gain_grad = finish_call(sel, keep, got, w_rows, gain_rows)
     return (

time: 214 us -> 214 us (level)
  starting transfers between devices: 48.4 us -> 66.4 us
  waiting for transfers between devices: 60.5 us -> 47.9 us
  Pallas kernels: 73.1 us -> 65.1 us
    ppermute x1, starting transfers between devices: 3.32 us -> 11.9 us  [body(): h2 = lax.ppermute(o_keep, PAIR, SPREAD2)]
    pallas_call x1, Pallas kernels: 24 us -> 16.2 us  [attention_call(): pl.pallas_call(attention_kernel, in_specs=[pl.BlockSpec(memory_space=pltp...]
    ppermute x1, waiting for transfers between devices: 4.88 us -> 0.01 us  [body(): d2 = lax.ppermute(summed, PAIR, SPREAD2)]
    ppermute x9, waiting for transfers between devices: 26.4 us -> 21.9 us  [shift(): return lax.ppermute(value, axis, [(i, (i + by) % 4) for i in range(4)])]
    ppermute x9, starting transfers between devices: 6.91 us -> 10.4 us  [shift(): return lax.ppermute(value, axis, [(i, (i + by) % 4) for i in range(4)])]
    all_to_all x1, waiting for transfers between devices: 16.8 us -> 14.7 us  [body(): lax.all_to_all(parts.reshape(64, 2, 16, WCOLS), ('x', 'zh', 'y', 'zl'), 0...]
    unnamed x52 -> x46, local copies, waits for them, and re-layouts: 4.87 us -> 6.52 us
  transfers between devices with their start and end apart: 28 -> 28, of which waited for: 14 -> 13; matrix products, arithmetic and copies ran while one was open for 9% -> 10% of each run, Pallas kernels for 29% -> 20%
where the time goes in v4:
time: 214 us; the launch traced here: 213 us
  starting transfers between devices  66.4 us (31%)
  Pallas kernels  65.1 us (30%)
  waiting for transfers between devices  47.9 us (22%)
  other arithmetic  14.9 us (7%)
  local copies, waits for them, and re-layouts  14.6 us (7%)
  between operations  3.54 us (2%)
    ppermute x9, waiting for transfers between devices, shift(): return lax.ppermute(value, axis, [(i, (i + by) % 4) for i in range(4)])  21.9 us
    pallas_call x1, Pallas kernels, attention_call(): pl.pallas_call(attention_kernel, in_specs=[pl.BlockSpec(memory_space=pltp...  16.2 us
    all_to_all x1, waiting for transfers between devices, body(): lax.all_to_all(parts.reshape(64, 2, 16, WCOLS), ('x', 'zh', 'y', 'zl'), 0...  14.7 us
    ppermute x1, starting transfers between devices, body(): h2 = lax.ppermute(o_keep, PAIR, SPREAD2)  11.9 us
    ppermute x9, starting transfers between devices, shift(): return lax.ppermute(value, axis, [(i, (i + by) % 4) for i in range(4)])  10.4 us
    pallas_call x2, Pallas kernels, q_call(): pl.pallas_call(q_kernel, grid_spec=pltpu.PrefetchScalarGridSpec(num_scala...  10.2 us
    pallas_call x1, Pallas kernels, weight_call(): pl.pallas_call(weight_kernel, grid_spec=pltpu.PrefetchScalarGridSpec(num_...  9.25 us
    all_to_all x1, starting transfers between devices, body(): lax.all_to_all(parts.reshape(64, 2, 16, WCOLS), ('x', 'zh', 'y', 'zl'), 0...  8.87 us
  transfers between devices with their start and end apart: 28, of which 13 were waited for; matrix products, arithmetic and copies ran while one was open for 10% of the time, Pallas kernels for 20%

profile of v4, /device:TPU:1, one launch (start us, length us, event | category | flops | bytes accessed | tf_op | source)
XLA Modules:
  0.0 212.6 jit_solution(16529148488823990965)
XLA Ops:
  2.5 6.0 %kv_home.1 = (bf16[256,2048]{1,0:T(8,128)(2,1)}, bf16[256,512]{1,0:T(8,128)(2,1)}, bf16[256,512]{1,0:T(8,128)(2,1)}) custom-call(s32[3]{0:T(128)} %add_add_fusion.1.sel_ref, bf16[256,2048]{1,0:T(8,128)(2,1)} %bitcast.45, f32[1,2048]{1,0:T(1,128)} %bitcast.50, bf16[2048,3072]{1,0:T(8,128)(2,1)} %wv_ref.3, bf16[2048,3072]{1,0:T(8,128)(2,1)} %wv_ref.3, ...), custom_call_target="tpu_custom_call" | custom-call | flops 10000 | bytes 10485 | tf_op jit(solution)/shard_map/kv_home/pallas_call | solution.py:94
  8.5 4.9 %collective-permute-start.5 = (bf16[256,512]{1,0:T(8,128)(2,1)}, bf16[256,512]{1,0:T(8,128)(2,1)S(1)}, u32[]{:S(2)}, u32[]{:S(2)}) collective-permute-start(bf16[256,512]{1,0:T(8,128)(2,1)} %get-tuple-element.48), channel_id=1, source_target_pairs={{1,8},{8,1},{3,10},{10,3},{5,12},{12,5},{7,14},{14,7},{17,24},{24,... | collective-permute-start | bytes 786440 | tf_op jit(solution)/shard_map/ppermute | solution.py:509
  20.2 3.2 %collective-permute-done.4 = bf16[256,512]{1,0:T(8,128)(2,1)S(1)} collective-permute-done((bf16[256,512]{1,0:T(8,128)(2,1)S(1)}, bf16[256,512]{1,0:T(8,128)(2,1)S(1)}, u32[]{:S(2)}, u32[]{:S(2)}) %collective-permute-start.4) | collective-permute-done | bytes 262176 | tf_op jit(solution)/shard_map/ppermute | solution.py:508
  25.2 4.5 %collective-permute-start.7 = (bf16[256,2048]{1,0:T(8,128)(2,1)S(1)}, bf16[256,2048]{1,0:T(8,128)(2,1)}, u32[]{:S(2)}, u32[]{:S(2)}) collective-permute-start(bf16[256,2048]{1,0:T(8,128)(2,1)S(1)} %copy-done.4), channel_id=1, source_target_pairs={{1,8},{8,1},{3,10},{10,3},{5,12},{12,5},{7,14},{14,7},{17,24},{24,... | collective-permute-start | bytes 3145736 | tf_op jit(solution)/shard_map/ppermute | solution.py:516
  35.5 4.2 %all-to-all-start = ((bf16[4,2,256,512]{3,2,1,0:T(8,128)(2,1)}), bf16[4,2,256,512]{3,2,1,0:T(8,128)(2,1)S(1)}, u32[]{:S(2)}, u32[]{:S(2)}) async-start(bf16[4,2,256,512]{3,2,1,0:T(8,128)(2,1)} %broadcast_in_dim.35), calls=%async_computation | async-start | bytes 4194304 | tf_op jit(solution)/shard_map/all_to_all | solution.py:515
  42.7 5.2 %q_proj.2.qs_ref = bf16[256,1024]{1,0:T(8,128)(2,1)} custom-call(s32[3]{0:T(128)} %add_add_fusion.sel_ref, bf16[256,2048]{1,0:T(8,128)(2,1)} %broadcast_select_fusion.2.n_ref.ns, bf16[2048,3072]{1,0:T(8,128)(2,1)} %wv_ref.3, f32[2048,256]{1,0:T(8,128)} %constant.64.clone.ta_ref.tb_ref, f32[2048,256]{1,0:T(8,128)} %constant.64.clone.ta_ref.tb_ref), custom_call_target="tpu_custom_call" | custom-call | flops 100000 | bytes 104857 | tf_op jit(solution)/shard_map/q_proj/pallas_call | solution.py:129
  47.9 5.0 %collective-permute-start.3 = (bf16[256,1024]{1,0:T(8,128)(2,1)S(1)}, bf16[256,1024]{1,0:T(8,128)(2,1)S(1)}, u32[]{:S(2)}, u32[]{:S(2)}) collective-permute-start(bf16[256,1024]{1,0:T(8,128)(2,1)S(1)} %copy-done.5), channel_id=1, source_target_pairs={{1,8},{8,1},{3,10},{10,3},{5,12},{12,5},{7,14},{14,7},{17,24},{24,... | collective-permute-start | bytes 1572872 | tf_op jit(solution)/shard_map/ppermute | solution.py:523
  55.7 5.0 %q_proj.3.qm_ref = bf16[256,1024]{1,0:T(8,128)(2,1)} custom-call(s32[3]{0:T(128)} %pad_add_fusion.sel_ref, bf16[256,2048]{1,0:T(8,128)(2,1)} %get-tuple-element.105.n_ref.nm, bf16[2048,3072]{1,0:T(8,128)(2,1)} %wv_ref.3, f32[2048,256]{1,0:T(8,128)} %constant.64.clone.ta_ref.tb_ref, f32[2048,256]{1,0:T(8,128)} %constant.64.clone.ta_ref.tb_ref), custom_call_target="tpu_custom_call" | custom-call | flops 100000 | bytes 104857 | tf_op jit(solution)/shard_map/q_proj/pallas_call | solution.py:129
  60.8 4.2 %collective-permute-done.3 = bf16[256,1024]{1,0:T(8,128)(2,1)S(1)} collective-permute-done((bf16[256,1024]{1,0:T(8,128)(2,1)S(1)}, bf16[256,1024]{1,0:T(8,128)(2,1)S(1)}, u32[]{:S(2)}, u32[]{:S(2)}) %collective-permute-start.3) | collective-permute-done | bytes 524320 | tf_op jit(solution)/shard_map/ppermute | solution.py:523
  72.2 16.2 %attention.1 = (bf16[256,1024]{1,0:T(8,128)(2,1)}, bf16[256,1024]{1,0:T(8,128)(2,1)}, bf16[512,1024]{1,0:T(8,128)(2,1)}, bf16[512,256]{1,0:T(8,128)(2,1)}, bf16[...) custom-call(s32[24]{0:T(128)} %stack.135.where_ref, ...), custom_call_target="tpu_custom_call" | custom-call | flops 100000 | bytes 104857 | tf_op jit(solution)/shard_map/attention/pallas_call | solution.py:258
  88.5 11.9 %collective-permute-start.8 = (bf16[256,1024]{1,0:T(8,128)(2,1)}, bf16[256,1024]{1,0:T(8,128)(2,1)S(1)}, u32[]{:S(2)}, u32[]{:S(2)}) collective-permute-start(bf16[256,1024]{1,0:T(8,128)(2,1)} %get-tuple-element.57), channel_id=1, source_target_pairs={{1,8},{8,1},{3,10},{10,3},{5,12},{12,5},{7,14},{14,7},{17,24},{24,... | collective-permute-start | bytes 1572872 | tf_op jit(solution)/shard_map/ppermute | solution.py:564
  100.4 3.8 %all-to-all-start.1 = ((bf16[4,512,512]{2,1,0:T(8,128)(2,1)}), bf16[4,512,512]{2,1,0:T(8,128)(2,1)S(1)}, u32[]{:S(2)}, u32[]{:S(2)}) async-start(bf16[4,512,512]{2,1,0:T(8,128)(2,1)} %get-tuple-element.71), calls=%async_computation.1 | async-start | bytes 4194304 | tf_op jit(solution)/shard_map/all_to_all | solution.py:559
  104.2 8.6 %collective-permute-done.11.d2 = bf16[256,2048]{1,0:T(8,128)(2,1)} collective-permute-done((bf16[256,2048]{1,0:T(8,128)(2,1)}, bf16[256,2048]{1,0:T(8,128)(2,1)}, u32[]{:S(2)}, u32[]{:S(2)}) %collective-permute-start.11) | collective-permute-done | bytes 1048608 | tf_op jit(solution)/shard_map/ppermute | solution.py:479
  117.6 6.8 %d_normed_q.1.part_ref = bf16[512,2048]{1,0:T(8,128)(2,1)} custom-call(s32[2]{0:T(128)} %pad_add_fusion.1.sel_ref, bf16[512,1024]{1,0:T(8,128)(2,1)} %get-tuple-element.59.j_ref, bf16[2048,3072]{1,0:T(8,128)(2,1)} %wv_ref.3), custom_call_target="tpu_custom_call" | custom-call | flops 10000 | bytes 10485 | tf_op jit(solution)/shard_map/d_normed_q/pallas_call | solution.py:308
  125.9 5.0 %collective-permute-done.15.q3 = bf16[512,256]{1,0:T(8,128)(2,1)} collective-permute-done((bf16[512,256]{1,0:T(8,128)(2,1)S(1)}, bf16[512,256]{1,0:T(8,128)(2,1)}, u32[]{:S(2)}, u32[]{:S(2)}) %collective-permute-start.15) | collective-permute-done | bytes 262176 | tf_op jit(solution)/shard_map/ppermute | solution.py:479
  137.1 3.1 %joined_kv.1 = (bf16[512,512]{1,0:T(8,128)(2,1)}, bf16[512,128]{1,0:T(8,128)(2,1)}, bf16[512,128]{1,0:T(8,128)(2,1)}, bf16[512,128]{1,0:T(8,128)(2,1)}, bf16[512,128]{1,0:T(8,128)(2,1)}) custom-call(s32[1]{0:T(128)} %bitcast.7.x_ref, bf16[4,512,512]{2,1,0:T(8,128)(2,1)} %copy-done, f32[512,256]{1,0:T(8,128)} %pad_maximum_fusion.2.table_ref), custom_call_target="tpu_custom_call" | custom-call | flops 100000 | bytes 104857 | tf_op jit(solution)/shard_map/joined_kv/pallas_call | solution.py:290
  142.1 2.9 %collective-permute-done.19.k1 = bf16[512,128]{1,0:T(8,128)(2,1)S(1)} collective-permute-done((bf16[512,128]{1,0:T(8,128)(2,1)}, bf16[512,128]{1,0:T(8,128)(2,1)S(1)}, u32[]{:S(2)}, u32[]{:S(2)}) %collective-permute-start.19) | collective-permute-done | bytes 131104 | tf_op jit(solution)/shard_map/ppermute | solution.py:479
  146.6 3.7 %collective-permute-done.21.k3 = bf16[512,128]{1,0:T(8,128)(2,1)S(1)} collective-permute-done((bf16[512,128]{1,0:T(8,128)(2,1)}, bf16[512,128]{1,0:T(8,128)(2,1)S(1)}, u32[]{:S(2)}, u32[]{:S(2)}) %collective-permute-start.21) | collective-permute-done | bytes 131104 | tf_op jit(solution)/shard_map/ppermute | solution.py:479
  150.9 9.3 %weight_grad.1 = bf16[8,8,2,16,384]{4,3,2,1,0:T(8,128)(2,1)} custom-call(s32[2]{0:T(128)} %pad_add_fusion.1.sel_ref, bf16[256,2048]{1,0:T(8,128)(2,1)} %broadcast_select_fusion.2.n_ref.ns, bf16[256,2048]{1,0:T(8,128)(2,1)} %get-tuple-element.105.n_ref.nm, bf16[256,2048]{1,0:T(8,128)(2,1)} %collective-permute-done.10.d1, ...), custom_call_target="tpu_custom_call" | custom-call | flops 100000 | bytes 104857 | tf_op jit(solution)/shard_map/weight_grad/pallas_call | solution.py:384
  160.2 5.1 %d_normed.1 = (bf16[256,2048]{1,0:T(8,128)(2,1)}, bf16[256,2048]{1,0:T(8,128)(2,1)}) custom-call(s32[2]{0:T(128)} %pad_add_fusion.1.sel_ref, bf16[512,2048]{1,0:T(8,128)(2,1)} %d_normed_q.1.part_ref, bf16[512,512]{1,0:T(8,128)(2,1)} %get-tuple-element.78.jkv_ref, bf16[2048,3072]{1,0:T(8,128)(2,1)} %wv_ref.3, bf16[2048,3072]{1,0:T(8,128)(2,1)} %wv_ref.3), custom_call_target="tpu_custom_call" | custom-call | flops 10000 | bytes 10485 | tf_op jit(solution)/shard_map/d_normed/pallas_call | solution.py:338
  165.9 8.9 %all-to-all-start.2 = ((bf16[64,2,16,384]{3,2,1,0:T(8,128)(2,1)}), bf16[64,2,16,384]{3,2,1,0:T(8,128)(2,1)S(1)}, u32[]{:S(2)}, u32[]{:S(2)}) async-start(bf16[64,2,16,384]{3,2,1,0:T(8,128)(2,1)} %bitcast.35), calls=%async_computation.2 | async-start | bytes 3145728 | tf_op jit(solution)/shard_map/all_to_all | solution.py:580
  177.4 3.5 %collective-permute-start.23 = (bf16[256,2048]{1,0:T(8,128)(2,1)}, bf16[256,2048]{1,0:T(8,128)(2,1)S(1)}, u32[]{:S(2)}, u32[]{:S(2)}) collective-permute-start(bf16[256,2048]{1,0:T(8,128)(2,1)} %add_convert_fusion), channel_id=1, source_target_pairs={{1,8},{8,1},{3,10},{10,3},{5,12},{12,5},{7,14},{14,7},{17,24},{24,... | collective-permute-start | bytes 3145736 | tf_op jit(solution)/shard_map/ppermute | solution.py:579
  183.9 14.7 %all-to-all-done.2.parts_ref = bf16[64,2,16,384]{3,2,1,0:T(8,128)(2,1)S(1)} async-done(((bf16[64,2,16,384]{3,2,1,0:T(8,128)(2,1)}), bf16[64,2,16,384]{3,2,1,0:T(8,128)(2,1)S(1)}, u32[]{:S(2)}, u32[]{:S(2)}) %all-to-all-start.2) | async-done | bytes 1572896 | tf_op jit(solution)/shard_map/all_to_all | solution.py:580
  208.1 4.5 %inputs_grad.1 = bf16[256,2048]{1,0:T(8,128)(2,1)} custom-call(s32[2]{0:T(128)} %pad_add_fusion.1.sel_ref, bf16[256,2048]{1,0:T(8,128)(2,1)} %bitcast.46, f32[1,2048]{1,0:T(1,128)} %bitcast.51, bf16[256,2048]{1,0:T(8,128)(2,1)} %get-tuple-element.79.keep_ref, bf16[256,2048]{1,0:T(8,128)(2,1)} %collective-permute-done.22.near_ref, bf16[256,2048]{1,0:T(8,128)(2,1)} %copy-done.9), custom_call_target="tpu_custom_call" | custom-call | flops 100000 | bytes 104857 | tf_op jit(solution)/shard_map/inputs_grad/pallas_call | solution.py:463
  (116 shorter events, 58.8 us)
Async XLA Ops:
  0.6 18.6 %collective-permute-start = (s32[16]{0:T(128)}, s32[16]{0:T(128)S(1)}, u32[]{:S(2)}, u32[]{:S(2)}) collective-permute-start(s32[16]{0:T(128)} %bitcast.54), channel_id=1, source_target_pairs={{0,8},{9,1},{2,10},{11,3},{4,12},{13,5},{6,14},{15,7},{16,24},{25,... | collective-permute-start | bytes 200 | tf_op jit(solution)/shard_map/ppermute | solution.py:504
  8.5 11.7 %collective-permute-start.5 = (bf16[256,512]{1,0:T(8,128)(2,1)}, bf16[256,512]{1,0:T(8,128)(2,1)S(1)}, u32[]{:S(2)}, u32[]{:S(2)}) collective-permute-start(bf16[256,512]{1,0:T(8,128)(2,1)} %get-tuple-element.48), channel_id=1, source_target_pairs={{1,8},{8,1},{3,10},{10,3},{5,12},{12,5},{7,14},{14,7},{17,24},{24,... | collective-permute-start | bytes 786440 | tf_op jit(solution)/shard_map/ppermute | solution.py:509
  13.4 10.1 %collective-permute-start.1 = (bf16[256,2048]{1,0:T(8,128)(2,1)}, bf16[256,2048]{1,0:T(8,128)(2,1)S(1)}, u32[]{:S(2)}, u32[]{:S(2)}) collective-permute-start(bf16[256,2048]{1,0:T(8,128)(2,1)} %get-tuple-element.51), channel_id=1, source_target_pairs={{0,8},{9,1},{2,10},{11,3},{4,12},{13,5},{6,14},{15,7},{16,24},{25,... | collective-permute-start | bytes 3145736 | tf_op jit(solution)/shard_map/ppermute | solution.py:513
  25.2 27.7 %collective-permute-start.7 = (bf16[256,2048]{1,0:T(8,128)(2,1)S(1)}, bf16[256,2048]{1,0:T(8,128)(2,1)}, u32[]{:S(2)}, u32[]{:S(2)}) collective-permute-start(bf16[256,2048]{1,0:T(8,128)(2,1)S(1)} %copy-done.4), channel_id=1, source_target_pairs={{1,8},{8,1},{3,10},{10,3},{5,12},{12,5},{7,14},{14,7},{17,24},{24,... | collective-permute-start | bytes 3145736 | tf_op jit(solution)/shard_map/ppermute | solution.py:516
  29.7 23.2 %collective-permute-start.6 = (bf16[256,2048]{1,0:T(8,128)(2,1)S(1)}, bf16[256,2048]{1,0:T(8,128)(2,1)}, u32[]{:S(2)}, u32[]{:S(2)}) collective-permute-start(bf16[256,2048]{1,0:T(8,128)(2,1)S(1)} %copy-done.4), channel_id=1, source_target_pairs={{1,0},{8,9},{3,2},{10,11},{5,4},{12,13},{7,6},{14,15},{17,16},{24,... | collective-permute-start | bytes 3145736 | tf_op jit(solution)/shard_map/ppermute | solution.py:517
  35.5 35.4 %all-to-all-start = ((bf16[4,2,256,512]{3,2,1,0:T(8,128)(2,1)}), bf16[4,2,256,512]{3,2,1,0:T(8,128)(2,1)S(1)}, u32[]{:S(2)}, u32[]{:S(2)}) async-start(bf16[4,2,256,512]{3,2,1,0:T(8,128)(2,1)} %broadcast_in_dim.35), calls=%async_computation | async-start | bytes 4194304 | tf_op jit(solution)/shard_map/all_to_all | solution.py:515
  47.9 12.9 %collective-permute-start.2 = (bf16[256,1024]{1,0:T(8,128)(2,1)S(1)}, bf16[256,1024]{1,0:T(8,128)(2,1)S(1)}, u32[]{:S(2)}, u32[]{:S(2)}) collective-permute-start(bf16[256,1024]{1,0:T(8,128)(2,1)S(1)} %copy-done.11), channel_id=1, source_target_pairs={{0,8},{9,1},{1,0},{8,9},{2,10},{11,3},{3,2},{10,11},{4,12},{13,5},... | collective-permute-start | bytes 1572872 | tf_op jit(solution)/shard_map/ppermute | solution.py:522
  47.9 17.1 %collective-permute-start.3 = (bf16[256,1024]{1,0:T(8,128)(2,1)S(1)}, bf16[256,1024]{1,0:T(8,128)(2,1)S(1)}, u32[]{:S(2)}, u32[]{:S(2)}) collective-permute-start(bf16[256,1024]{1,0:T(8,128)(2,1)S(1)} %copy-done.5), channel_id=1, source_target_pairs={{1,8},{8,1},{3,10},{10,3},{5,12},{12,5},{7,14},{14,7},{17,24},{24,... | collective-permute-start | bytes 1572872 | tf_op jit(solution)/shard_map/ppermute | solution.py:523
  65.0 39.2 %collective-permute-start.12 = (bf16[256,2048]{1,0:T(8,128)(2,1)}, bf16[256,2048]{1,0:T(8,128)(2,1)}, u32[]{:S(2)}, u32[]{:S(2)}) collective-permute-start(bf16[256,2048]{1,0:T(8,128)(2,1)} %get-tuple-element.60), channel_id=1, source_target_pairs={{0,32},{32,64},{64,96},{96,0},{1,33},{33,65},{65,97},{97,1},{2,34}... | collective-permute-start | bytes 3145736 | tf_op jit(solution)/shard_map/ppermute | solution.py:479
  66.2 46.6 %collective-permute-start.11 = (bf16[256,2048]{1,0:T(8,128)(2,1)}, bf16[256,2048]{1,0:T(8,128)(2,1)}, u32[]{:S(2)}, u32[]{:S(2)}) collective-permute-start(bf16[256,2048]{1,0:T(8,128)(2,1)} %get-tuple-element.60), channel_id=1, source_target_pairs={{0,64},{32,96},{64,0},{96,32},{1,65},{33,97},{65,1},{97,33},{2,66}... | collective-permute-start | bytes 3145736 | tf_op jit(solution)/shard_map/ppermute | solution.py:479
  68.6 44.3 %collective-permute-start.10 = (bf16[256,2048]{1,0:T(8,128)(2,1)}, bf16[256,2048]{1,0:T(8,128)(2,1)}, u32[]{:S(2)}, u32[]{:S(2)}) collective-permute-start(bf16[256,2048]{1,0:T(8,128)(2,1)} %get-tuple-element.60), channel_id=1, source_target_pairs={{0,96},{32,0},{64,32},{96,64},{1,97},{33,1},{65,33},{97,65},{2,98}... | collective-permute-start | bytes 3145736 | tf_op jit(solution)/shard_map/ppermute | solution.py:479
  88.5 36.0 %collective-permute-start.8 = (bf16[256,1024]{1,0:T(8,128)(2,1)}, bf16[256,1024]{1,0:T(8,128)(2,1)S(1)}, u32[]{:S(2)}, u32[]{:S(2)}) collective-permute-start(bf16[256,1024]{1,0:T(8,128)(2,1)} %get-tuple-element.57), channel_id=1, source_target_pairs={{1,8},{8,1},{3,10},{10,3},{5,12},{12,5},{7,14},{14,7},{17,24},{24,... | collective-permute-start | bytes 1572872 | tf_op jit(solution)/shard_map/ppermute | solution.py:564
  100.4 33.9 %all-to-all-start.1 = ((bf16[4,512,512]{2,1,0:T(8,128)(2,1)}), bf16[4,512,512]{2,1,0:T(8,128)(2,1)S(1)}, u32[]{:S(2)}, u32[]{:S(2)}) async-start(bf16[4,512,512]{2,1,0:T(8,128)(2,1)} %get-tuple-element.71), calls=%async_computation.1 | async-start | bytes 4194304 | tf_op jit(solution)/shard_map/all_to_all | solution.py:559
  112.9 11.5 %collective-permute-start.13 = (bf16[512,256]{1,0:T(8,128)(2,1)}, bf16[512,256]{1,0:T(8,128)(2,1)S(1)}, u32[]{:S(2)}, u32[]{:S(2)}) collective-permute-start(bf16[512,256]{1,0:T(8,128)(2,1)} %get-tuple-element.62), channel_id=1, source_target_pairs={{0,96},{32,0},{64,32},{96,64},{1,97},{33,1},{65,33},{97,65},{2,98}... | collective-permute-start | bytes 786440 | tf_op jit(solution)/shard_map/ppermute | solution.py:479
  115.3 9.2 %collective-permute-start.14 = (bf16[512,256]{1,0:T(8,128)(2,1)}, bf16[512,256]{1,0:T(8,128)(2,1)S(1)}, u32[]{:S(2)}, u32[]{:S(2)}) collective-permute-start(bf16[512,256]{1,0:T(8,128)(2,1)} %get-tuple-element.64), channel_id=1, source_target_pairs={{0,64},{32,96},{64,0},{96,32},{1,65},{33,97},{65,1},{97,33},{2,66}... | collective-permute-start | bytes 786440 | tf_op jit(solution)/shard_map/ppermute | solution.py:479
  116.4 14.5 %collective-permute-start.15 = (bf16[512,256]{1,0:T(8,128)(2,1)S(1)}, bf16[512,256]{1,0:T(8,128)(2,1)}, u32[]{:S(2)}, u32[]{:S(2)}) collective-permute-start(bf16[512,256]{1,0:T(8,128)(2,1)S(1)} %copy-done.22), channel_id=1, source_target_pairs={{0,32},{32,64},{64,96},{96,0},{1,33},{33,65},{65,97},{97,1},{2,34}... | collective-permute-start | bytes 786440 | tf_op jit(solution)/shard_map/ppermute | solution.py:479
  116.5 15.4 %collective-permute-start.9 = (bf16[256,1024]{1,0:T(8,128)(2,1)}, bf16[256,1024]{1,0:T(8,128)(2,1)}, u32[]{:S(2)}, u32[]{:S(2)}) collective-permute-start(bf16[256,1024]{1,0:T(8,128)(2,1)} %get-tuple-element.58), channel_id=1, source_target_pairs={{8,0},{1,9},{0,1},{9,8},{10,2},{3,11},{2,3},{11,10},{12,4},{5,13},... | collective-permute-start | bytes 1572872 | tf_op jit(solution)/shard_map/ppermute | solution.py:563
  131.5 5.6 %collective-permute-start.18 = (bf16[256,2048]{1,0:T(8,128)(2,1)}, bf16[256,2048]{1,0:T(8,128)(2,1)}, u32[]{:S(2)}, u32[]{:S(2)}) collective-permute-start(bf16[256,2048]{1,0:T(8,128)(2,1)} %collective-permute-done.12.d3), channel_id=1, source_target_pairs={{0,8},{8,0},{1,9},{9,1},{2,10},{10,2},{3,11},{11,3},{4,12},{12,4},... | collective-permute-start | bytes 3145736 | tf_op jit(solution)/shard_map/ppermute | solution.py:483
  140.1 4.9 %collective-permute-start.19 = (bf16[512,128]{1,0:T(8,128)(2,1)}, bf16[512,128]{1,0:T(8,128)(2,1)S(1)}, u32[]{:S(2)}, u32[]{:S(2)}) collective-permute-start(bf16[512,128]{1,0:T(8,128)(2,1)} %get-tuple-element.74), channel_id=1, source_target_pairs={{0,96},{32,0},{64,32},{96,64},{1,97},{33,1},{65,33},{97,65},{2,98}... | collective-permute-start | bytes 393224 | tf_op jit(solution)/shard_map/ppermute | solution.py:479
  140.5 6.1 %collective-permute-start.20 = (bf16[512,128]{1,0:T(8,128)(2,1)}, bf16[512,128]{1,0:T(8,128)(2,1)S(1)}, u32[]{:S(2)}, u32[]{:S(2)}) collective-permute-start(bf16[512,128]{1,0:T(8,128)(2,1)} %get-tuple-element.75), channel_id=1, source_target_pairs={{0,64},{32,96},{64,0},{96,32},{1,65},{33,97},{65,1},{97,33},{2,66}... | collective-permute-start | bytes 393224 | tf_op jit(solution)/shard_map/ppermute | solution.py:479
  141.6 8.7 %collective-permute-start.21 = (bf16[512,128]{1,0:T(8,128)(2,1)}, bf16[512,128]{1,0:T(8,128)(2,1)S(1)}, u32[]{:S(2)}, u32[]{:S(2)}) collective-permute-start(bf16[512,128]{1,0:T(8,128)(2,1)} %get-tuple-element.76), channel_id=1, source_target_pairs={{0,32},{32,64},{64,96},{96,0},{1,33},{33,65},{65,97},{97,1},{2,34}... | collective-permute-start | bytes 393224 | tf_op jit(solution)/shard_map/ppermute | solution.py:479
  165.3 9.5 %collective-permute-start.22 = (bf16[256,2048]{1,0:T(8,128)(2,1)}, bf16[256,2048]{1,0:T(8,128)(2,1)}, u32[]{:S(2)}, u32[]{:S(2)}) collective-permute-start(bf16[256,2048]{1,0:T(8,128)(2,1)} %get-tuple-element.80), channel_id=1, source_target_pairs={{0,8},{8,0},{1,9},{9,1},{2,10},{10,2},{3,11},{11,3},{4,12},{12,4},... | collective-permute-start | bytes 3145736 | tf_op jit(solution)/shard_map/ppermute | solution.py:483
  165.9 32.6 %all-to-all-start.2 = ((bf16[64,2,16,384]{3,2,1,0:T(8,128)(2,1)}), bf16[64,2,16,384]{3,2,1,0:T(8,128)(2,1)S(1)}, u32[]{:S(2)}, u32[]{:S(2)}) async-start(bf16[64,2,16,384]{3,2,1,0:T(8,128)(2,1)} %bitcast.35), calls=%async_computation.2 | async-start | bytes 3145728 | tf_op jit(solution)/shard_map/all_to_all | solution.py:580
  177.4 29.6 %collective-permute-start.23 = (bf16[256,2048]{1,0:T(8,128)(2,1)}, bf16[256,2048]{1,0:T(8,128)(2,1)S(1)}, u32[]{:S(2)}, u32[]{:S(2)}) collective-permute-start(bf16[256,2048]{1,0:T(8,128)(2,1)} %add_convert_fusion), channel_id=1, source_target_pairs={{1,8},{8,1},{3,10},{10,3},{5,12},{12,5},{7,14},{14,7},{17,24},{24,... | collective-permute-start | bytes 3145736 | tf_op jit(solution)/shard_map/ppermute | solution.py:579
  (27 other events, 139.4 us)
